TPU v7x, 256 devices: a whole 4x4x8 slice. The times are simulated.
256 devices in a mesh: ctx: 64 (over z, y, x_lo), head: 4 (over x_hi, core).
Axes of the slice: x: 4 (x_hi: 2, x_lo: 2; x = x_hi * 2 + x_lo), y: 4, z: 8, core: 2. Of those that a mesh axis runs over, the one named last changes fastest.
Arguments:
- queries: bfloat16 [8192, 2048], P('ctx', 'head'), may hold values from -4.5 to 4.5
- key_vectors: bfloat16 [8192, 2048], P('ctx', 'head'), may hold values from -4.5 to 4.5
- value_vectors: bfloat16 [8192, 2048], P('ctx', 'head'), may hold values from -6 to 6
- out_weight: bfloat16 [2048, 4096], P('head'), may hold values from -0.125 to 0.125
Outputs:
- layer_out: float32 [8192, 4096], P(('ctx', 'head'))
All inputs are finite; a program needn't handle non-finite values.
Results may differ from a plain program's by a relative error of at most 0.009.
Values may be sent and summed in bfloat16 or wider, within the bound.
No kernel may reach another device: no remote copies, remote signals or barrier semaphores. Data moves between devices by JAX's collectives and lax.ppermute only.
A program may use at most 128 MiB of HBM per device.

v0:
```python
import jax
import jax.numpy as jnp
from jax import lax
from jax.sharding import PartitionSpec as P

DH = 128


def for_sending(x):
    return jax.tree.map(lambda a: a.astype(jnp.bfloat16) if a.dtype == jnp.float32 else a, x)


def shifted(x, axis, by):
    peers = lax.axis_size(axis)
    return lax.ppermute(x, axis, [(i, (i + by) % peers) for i in range(peers)])


def block_state(query_block, key_block, value_block):
    score_scale = query_block.shape[2] ** (-0.5)
    scores = (
        jnp.einsum("qhd,khd->hqk", query_block, key_block, preferred_element_type=jnp.float32)
        * score_scale
    )
    row_peak = jnp.max(scores, axis=2)
    exponent = jnp.exp(scores - row_peak[:, :, None])
    row_sum = jnp.sum(exponent, axis=2)
    summed = jnp.einsum(
        "hqk,khd->qhd",
        exponent.astype(jnp.bfloat16),
        value_block,
        preferred_element_type=jnp.float32,
    )
    return (summed, row_peak, row_sum)


def merge_state(former, latter):
    joint_peak = jnp.maximum(former[1], latter[1])
    former_weight = jnp.exp(former[1] - joint_peak)
    latter_weight = jnp.exp(latter[1] - joint_peak)
    summed = former[0] * former_weight.T[:, :, None] + latter[0] * latter_weight.T[:, :, None]
    return (summed, joint_peak, former[2] * former_weight + latter[2] * latter_weight)


def travel(visitor):
    return jax.tree.map(
        lambda part, own: part.astype(own.dtype), shifted(for_sending(visitor), "ctx", 1), visitor
    )


def body(queries, key_vectors, value_vectors, out_weight):
    tok_rows = queries.shape[0]
    local_width = queries.shape[1]
    local_heads = local_width // DH
    home_queries = queries.reshape(tok_rows, local_heads, DH)
    home_keys = key_vectors.reshape(tok_rows, local_heads, DH)
    home_values = value_vectors.reshape(tok_rows, local_heads, DH)
    half_loop = lax.axis_size("ctx") // 2
    state_home = block_state(home_queries, home_keys, home_values)
    visitor = travel((home_queries, home_keys, home_values))
    state_home = merge_state(state_home, block_state(home_queries, visitor[1], visitor[2]))
    state_away = block_state(visitor[0], home_keys, home_values)

    def hop_once(hop_index, loop_state):
        visitor, state_home, state_away = loop_state
        visitor = travel(visitor)
        state_away = shifted((state_away[0], state_away[1], state_away[2]), "ctx", 1)
        state_home = merge_state(state_home, block_state(home_queries, visitor[1], visitor[2]))
        state_away = merge_state(state_away, block_state(visitor[0], home_keys, home_values))
        return (visitor, state_home, state_away)

    visitor, state_home, state_away = lax.fori_loop(
        0, half_loop - 2, hop_once, (visitor, state_home, state_away)
    )
    returned = shifted((state_away[0], state_away[1], state_away[2]), "ctx", -(half_loop - 1))
    far_pair = shifted((visitor[1], visitor[2]), "ctx", 1)
    state_home = merge_state(state_home, block_state(home_queries, far_pair[0], far_pair[1]))
    state_home = merge_state(state_home, returned)
    attended = (
        (state_home[0] / state_home[2].T[:, :, None])
        .astype(jnp.bfloat16)
        .reshape(tok_rows, local_width)
    )
    return lax.psum_scatter(
        jnp.dot(attended, out_weight, preferred_element_type=jnp.float32),
        "head",
        scatter_dimension=0,
        tiled=True,
    )


def solution(mesh):
    placed = (P("ctx", "head"), P("ctx", "head"), P("ctx", "head"), P("head", None))
    return jax.shard_map(
        body, mesh=mesh, in_specs=placed, out_specs=P(("ctx", "head"), None), check_vma=False
    )
```

profile of v0, /device:TPU:1, one launch (start us, length us, event | category | flops | bytes accessed | tf_op | source)
XLA Modules:
  0.0 710.8 jit_solution(919364510414035872)
XLA Ops:
  15.1 8.5 %collective-permute-done.7 = bf16[128,4,128]{2,0,1:T(8,128)(2,1)S(1)} collective-permute-done((bf16[128,4,128]{2,0,1:T(8,128)(2,1)S(1)}, bf16[128,4,128]{2,0,1:T(8,128)(2,1)S(1)}, u32[]{:S(2)}, u32[]{:S(2)}) %collective-permute-start.7) | collective-permute-done | bytes 131104 | tf_op jit(solution)/shard_map/ppermute | solution.py:15
  27.3 601.8 %while.26 = (s32[]{:T(128)}, bf16[128,4,128]{2,0,1:T(8,128)(2,1)S(1)}, bf16[128,4,128]{2,0,1:T(8,128)(2,1)S(1)}, bf16[128,4,128]{2,0,1:T(8,128)(2,1)S(1)}, f32[1...) while((s32[]{:T(128)}, ...), condition=%wide.region_11.0_spmd, body=%wide.region_6.0_spmd.sunk | while | flops 68294656 | bytes 6906229 | solution.py:71
  96.6 8.1 %collective-permute-done.3 = f32[128,4,128]{2,0,1:T(8,128)S(1)} collective-permute-done((f32[128,4,128]{2,0,1:T(8,128)S(1)}, f32[128,4,128]{2,0,1:T(8,128)S(1)}, u32[]{:S(2)}, u32[]{:S(2)}) %collective-permute-start.3) | collective-permute-done | bytes 262176 | tf_op jit(solution)/shard_map/while/body/eval_jaxpr/ppermute | solution.py:15
  116.7 8.1 %collective-permute-done.3 = f32[128,4,128]{2,0,1:T(8,128)S(1)} collective-permute-done((f32[128,4,128]{2,0,1:T(8,128)S(1)}, f32[128,4,128]{2,0,1:T(8,128)S(1)}, u32[]{:S(2)}, u32[]{:S(2)}) %collective-permute-start.3) | collective-permute-done | bytes 262176 | tf_op jit(solution)/shard_map/while/body/eval_jaxpr/ppermute | solution.py:15
  136.9 8.1 %collective-permute-done.3 = f32[128,4,128]{2,0,1:T(8,128)S(1)} collective-permute-done((f32[128,4,128]{2,0,1:T(8,128)S(1)}, f32[128,4,128]{2,0,1:T(8,128)S(1)}, u32[]{:S(2)}, u32[]{:S(2)}) %collective-permute-start.3) | collective-permute-done | bytes 262176 | tf_op jit(solution)/shard_map/while/body/eval_jaxpr/ppermute | solution.py:15
  157.0 8.1 %collective-permute-done.3 = f32[128,4,128]{2,0,1:T(8,128)S(1)} collective-permute-done((f32[128,4,128]{2,0,1:T(8,128)S(1)}, f32[128,4,128]{2,0,1:T(8,128)S(1)}, u32[]{:S(2)}, u32[]{:S(2)}) %collective-permute-start.3) | collective-permute-done | bytes 262176 | tf_op jit(solution)/shard_map/while/body/eval_jaxpr/ppermute | solution.py:15
  177.2 8.1 %collective-permute-done.3 = f32[128,4,128]{2,0,1:T(8,128)S(1)} collective-permute-done((f32[128,4,128]{2,0,1:T(8,128)S(1)}, f32[128,4,128]{2,0,1:T(8,128)S(1)}, u32[]{:S(2)}, u32[]{:S(2)}) %collective-permute-start.3) | collective-permute-done | bytes 262176 | tf_op jit(solution)/shard_map/while/body/eval_jaxpr/ppermute | solution.py:15
  197.4 8.1 %collective-permute-done.3 = f32[128,4,128]{2,0,1:T(8,128)S(1)} collective-permute-done((f32[128,4,128]{2,0,1:T(8,128)S(1)}, f32[128,4,128]{2,0,1:T(8,128)S(1)}, u32[]{:S(2)}, u32[]{:S(2)}) %collective-permute-start.3) | collective-permute-done | bytes 262176 | tf_op jit(solution)/shard_map/while/body/eval_jaxpr/ppermute | solution.py:15
  217.5 8.1 %collective-permute-done.3 = f32[128,4,128]{2,0,1:T(8,128)S(1)} collective-permute-done((f32[128,4,128]{2,0,1:T(8,128)S(1)}, f32[128,4,128]{2,0,1:T(8,128)S(1)}, u32[]{:S(2)}, u32[]{:S(2)}) %collective-permute-start.3) | collective-permute-done | bytes 262176 | tf_op jit(solution)/shard_map/while/body/eval_jaxpr/ppermute | solution.py:15
  278.0 8.1 %collective-permute-done.3 = f32[128,4,128]{2,0,1:T(8,128)S(1)} collective-permute-done((f32[128,4,128]{2,0,1:T(8,128)S(1)}, f32[128,4,128]{2,0,1:T(8,128)S(1)}, u32[]{:S(2)}, u32[]{:S(2)}) %collective-permute-start.3) | collective-permute-done | bytes 262176 | tf_op jit(solution)/shard_map/while/body/eval_jaxpr/ppermute | solution.py:15
  298.2 8.1 %collective-permute-done.3 = f32[128,4,128]{2,0,1:T(8,128)S(1)} collective-permute-done((f32[128,4,128]{2,0,1:T(8,128)S(1)}, f32[128,4,128]{2,0,1:T(8,128)S(1)}, u32[]{:S(2)}, u32[]{:S(2)}) %collective-permute-start.3) | collective-permute-done | bytes 262176 | tf_op jit(solution)/shard_map/while/body/eval_jaxpr/ppermute | solution.py:15
  318.3 8.1 %collective-permute-done.3 = f32[128,4,128]{2,0,1:T(8,128)S(1)} collective-permute-done((f32[128,4,128]{2,0,1:T(8,128)S(1)}, f32[128,4,128]{2,0,1:T(8,128)S(1)}, u32[]{:S(2)}, u32[]{:S(2)}) %collective-permute-start.3) | collective-permute-done | bytes 262176 | tf_op jit(solution)/shard_map/while/body/eval_jaxpr/ppermute | solution.py:15
  338.5 8.1 %collective-permute-done.3 = f32[128,4,128]{2,0,1:T(8,128)S(1)} collective-permute-done((f32[128,4,128]{2,0,1:T(8,128)S(1)}, f32[128,4,128]{2,0,1:T(8,128)S(1)}, u32[]{:S(2)}, u32[]{:S(2)}) %collective-permute-start.3) | collective-permute-done | bytes 262176 | tf_op jit(solution)/shard_map/while/body/eval_jaxpr/ppermute | solution.py:15
  358.6 8.1 %collective-permute-done.3 = f32[128,4,128]{2,0,1:T(8,128)S(1)} collective-permute-done((f32[128,4,128]{2,0,1:T(8,128)S(1)}, f32[128,4,128]{2,0,1:T(8,128)S(1)}, u32[]{:S(2)}, u32[]{:S(2)}) %collective-permute-start.3) | collective-permute-done | bytes 262176 | tf_op jit(solution)/shard_map/while/body/eval_jaxpr/ppermute | solution.py:15
  378.8 8.1 %collective-permute-done.3 = f32[128,4,128]{2,0,1:T(8,128)S(1)} collective-permute-done((f32[128,4,128]{2,0,1:T(8,128)S(1)}, f32[128,4,128]{2,0,1:T(8,128)S(1)}, u32[]{:S(2)}, u32[]{:S(2)}) %collective-permute-start.3) | collective-permute-done | bytes 262176 | tf_op jit(solution)/shard_map/while/body/eval_jaxpr/ppermute | solution.py:15
  399.0 8.1 %collective-permute-done.3 = f32[128,4,128]{2,0,1:T(8,128)S(1)} collective-permute-done((f32[128,4,128]{2,0,1:T(8,128)S(1)}, f32[128,4,128]{2,0,1:T(8,128)S(1)}, u32[]{:S(2)}, u32[]{:S(2)}) %collective-permute-start.3) | collective-permute-done | bytes 262176 | tf_op jit(solution)/shard_map/while/body/eval_jaxpr/ppermute | solution.py:15
  419.1 8.1 %collective-permute-done.3 = f32[128,4,128]{2,0,1:T(8,128)S(1)} collective-permute-done((f32[128,4,128]{2,0,1:T(8,128)S(1)}, f32[128,4,128]{2,0,1:T(8,128)S(1)}, u32[]{:S(2)}, u32[]{:S(2)}) %collective-permute-start.3) | collective-permute-done | bytes 262176 | tf_op jit(solution)/shard_map/while/body/eval_jaxpr/ppermute | solution.py:15
  479.6 8.1 %collective-permute-done.3 = f32[128,4,128]{2,0,1:T(8,128)S(1)} collective-permute-done((f32[128,4,128]{2,0,1:T(8,128)S(1)}, f32[128,4,128]{2,0,1:T(8,128)S(1)}, u32[]{:S(2)}, u32[]{:S(2)}) %collective-permute-start.3) | collective-permute-done | bytes 262176 | tf_op jit(solution)/shard_map/while/body/eval_jaxpr/ppermute | solution.py:15
  499.7 8.1 %collective-permute-done.3 = f32[128,4,128]{2,0,1:T(8,128)S(1)} collective-permute-done((f32[128,4,128]{2,0,1:T(8,128)S(1)}, f32[128,4,128]{2,0,1:T(8,128)S(1)}, u32[]{:S(2)}, u32[]{:S(2)}) %collective-permute-start.3) | collective-permute-done | bytes 262176 | tf_op jit(solution)/shard_map/while/body/eval_jaxpr/ppermute | solution.py:15
  519.9 8.1 %collective-permute-done.3 = f32[128,4,128]{2,0,1:T(8,128)S(1)} collective-permute-done((f32[128,4,128]{2,0,1:T(8,128)S(1)}, f32[128,4,128]{2,0,1:T(8,128)S(1)}, u32[]{:S(2)}, u32[]{:S(2)}) %collective-permute-start.3) | collective-permute-done | bytes 262176 | tf_op jit(solution)/shard_map/while/body/eval_jaxpr/ppermute | solution.py:15
  540.1 8.1 %collective-permute-done.3 = f32[128,4,128]{2,0,1:T(8,128)S(1)} collective-permute-done((f32[128,4,128]{2,0,1:T(8,128)S(1)}, f32[128,4,128]{2,0,1:T(8,128)S(1)}, u32[]{:S(2)}, u32[]{:S(2)}) %collective-permute-start.3) | collective-permute-done | bytes 262176 | tf_op jit(solution)/shard_map/while/body/eval_jaxpr/ppermute | solution.py:15
  560.2 8.1 %collective-permute-done.3 = f32[128,4,128]{2,0,1:T(8,128)S(1)} collective-permute-done((f32[128,4,128]{2,0,1:T(8,128)S(1)}, f32[128,4,128]{2,0,1:T(8,128)S(1)}, u32[]{:S(2)}, u32[]{:S(2)}) %collective-permute-start.3) | collective-permute-done | bytes 262176 | tf_op jit(solution)/shard_map/while/body/eval_jaxpr/ppermute | solution.py:15
  580.4 8.1 %collective-permute-done.3 = f32[128,4,128]{2,0,1:T(8,128)S(1)} collective-permute-done((f32[128,4,128]{2,0,1:T(8,128)S(1)}, f32[128,4,128]{2,0,1:T(8,128)S(1)}, u32[]{:S(2)}, u32[]{:S(2)}) %collective-permute-start.3) | collective-permute-done | bytes 262176 | tf_op jit(solution)/shard_map/while/body/eval_jaxpr/ppermute | solution.py:15
  649.1 54.8 %reduce-scatter.2.cloned.1.call-done = f32[32,4096]{1,0:T(8,128)} async-done(((f32[128,4096]{1,0:T(8,128)}), f32[32,4096]{1,0:T(8,128)}) %reduce-scatter.2.cloned.1.call-update) | async-done | bytes 524304 | tf_op jit(solution)/shard_map/reduce_scatter | solution.py:83
  (802 shorter events, 458.9 us)
Async XLA Ops:
  6.5 697.4 %reduce-scatter.2.cloned.1.call-start = ((), (), s32[]{:S(2)}) async-start(), calls=%async_computation.1 | async-start | bytes 2621440 | tf_op jit(solution)/shard_map/reduce_scatter | solution.py:83
  7.7 19.3 %collective-permute-start.8 = (bf16[128,4,128]{2,0,1:T(8,128)(2,1)S(1)}, bf16[128,4,128]{2,0,1:T(8,128)(2,1)S(1)}, u32[]{:S(2)}, u32[]{:S(2)}) collective-permute-start(bf16[128,4,128]{2,0,1:T(8,128)(2,1)S(1)} %copy.21), channel_id=1, source_target_pairs={{0,4},{4,8},{8,12},{12,16},{16,20},{20,24},{24,28},{28,32},{32,36}... | collective-permute-start | bytes 393224 | tf_op jit(solution)/shard_map/ppermute | solution.py:15
  11.0 12.6 %collective-permute-start.7 = (bf16[128,4,128]{2,0,1:T(8,128)(2,1)S(1)}, bf16[128,4,128]{2,0,1:T(8,128)(2,1)S(1)}, u32[]{:S(2)}, u32[]{:S(2)}) collective-permute-start(bf16[128,4,128]{2,0,1:T(8,128)(2,1)S(1)} %copy.19), channel_id=1, source_target_pairs={{0,4},{4,8},{8,12},{12,16},{16,20},{20,24},{24,28},{28,32},{32,36}... | collective-permute-start | bytes 393224 | tf_op jit(solution)/shard_map/ppermute | solution.py:15
  13.5 12.9 %collective-permute-start.6 = (bf16[128,4,128]{2,0,1:T(8,128)(2,1)S(1)}, bf16[128,4,128]{2,0,1:T(8,128)(2,1)S(1)}, u32[]{:S(2)}, u32[]{:S(2)}) collective-permute-start(bf16[128,4,128]{2,0,1:T(8,128)(2,1)S(1)} %copy.17), channel_id=1, source_target_pairs={{0,4},{4,8},{8,12},{12,16},{16,20},{20,24},{24,28},{28,32},{32,36}... | collective-permute-start | bytes 393224 | tf_op jit(solution)/shard_map/ppermute | solution.py:15
  27.4 14.0 %collective-permute-start.5 = (f32[4,128]{1,0:T(4,128)S(1)}, f32[4,128]{1,0:T(4,128)S(1)}, u32[]{:S(2)}, u32[]{:S(2)}) collective-permute-start(f32[4,128]{1,0:T(4,128)S(1)} %get-tuple-element.281), channel_id=1, source_target_pairs={{0,4},{4,8},{8,12},{12,16},{16,20},{20,24},{24,28},{28,32},{32,36}... | collective-permute-start | bytes 6152 | tf_op jit(solution)/shard_map/while/body/eval_jaxpr/ppermute | solution.py:15
  27.5 13.9 %collective-permute-start.4 = (f32[4,128]{1,0:T(4,128)S(1)}, f32[4,128]{1,0:T(4,128)S(1)}, u32[]{:S(2)}, u32[]{:S(2)}) collective-permute-start(f32[4,128]{1,0:T(4,128)S(1)} %get-tuple-element.280), channel_id=1, source_target_pairs={{0,4},{4,8},{8,12},{12,16},{16,20},{20,24},{24,28},{28,32},{32,36}... | collective-permute-start | bytes 6152 | tf_op jit(solution)/shard_map/while/body/eval_jaxpr/ppermute | solution.py:15
  27.6 13.9 %collective-permute-start.2 = (bf16[128,4,128]{2,0,1:T(8,128)(2,1)S(1)}, bf16[128,4,128]{2,0,1:T(8,128)(2,1)S(1)}, u32[]{:S(2)}, u32[]{:S(2)}) collective-permute-start(bf16[128,4,128]{2,0,1:T(8,128)(2,1)S(1)} %get-tuple-element.275), channel_id=1, source_target_pairs={{0,4},{4,8},{8,12},{12,16},{16,20},{20,24},{24,28},{28,32},{32,36}... | collective-permute-start | bytes 393224 | tf_op jit(solution)/shard_map/while/body/eval_jaxpr/ppermute | solution.py:15
  27.6 13.4 %collective-permute-start = (bf16[128,4,128]{2,0,1:T(8,128)(2,1)S(1)}, bf16[128,4,128]{2,0,1:T(8,128)(2,1)S(1)}, u32[]{:S(2)}, u32[]{:S(2)}) collective-permute-start(bf16[128,4,128]{2,0,1:T(8,128)(2,1)S(1)} %get-tuple-element.273), channel_id=1, source_target_pairs={{0,4},{4,8},{8,12},{12,16},{16,20},{20,24},{24,28},{28,32},{32,36}... | collective-permute-start | bytes 393224 | tf_op jit(solution)/shard_map/while/body/eval_jaxpr/ppermute | solution.py:15
  113.1 11.7 %collective-permute-start.3 = (f32[128,4,128]{2,0,1:T(8,128)S(1)}, f32[128,4,128]{2,0,1:T(8,128)S(1)}, u32[]{:S(2)}, u32[]{:S(2)}) collective-permute-start(f32[128,4,128]{2,0,1:T(8,128)S(1)} %get-tuple-element.279), channel_id=1, source_target_pairs={{0,4},{4,8},{8,12},{12,16},{16,20},{20,24},{24,28},{28,32},{32,36}... | collective-permute-start | bytes 786440 | tf_op jit(solution)/shard_map/while/body/eval_jaxpr/ppermute | solution.py:15
  133.3 11.7 %collective-permute-start.3 = (f32[128,4,128]{2,0,1:T(8,128)S(1)}, f32[128,4,128]{2,0,1:T(8,128)S(1)}, u32[]{:S(2)}, u32[]{:S(2)}) collective-permute-start(f32[128,4,128]{2,0,1:T(8,128)S(1)} %get-tuple-element.279), channel_id=1, source_target_pairs={{0,4},{4,8},{8,12},{12,16},{16,20},{20,24},{24,28},{28,32},{32,36}... | collective-permute-start | bytes 786440 | tf_op jit(solution)/shard_map/while/body/eval_jaxpr/ppermute | solution.py:15
  153.4 11.7 %collective-permute-start.3 = (f32[128,4,128]{2,0,1:T(8,128)S(1)}, f32[128,4,128]{2,0,1:T(8,128)S(1)}, u32[]{:S(2)}, u32[]{:S(2)}) collective-permute-start(f32[128,4,128]{2,0,1:T(8,128)S(1)} %get-tuple-element.279), channel_id=1, source_target_pairs={{0,4},{4,8},{8,12},{12,16},{16,20},{20,24},{24,28},{28,32},{32,36}... | collective-permute-start | bytes 786440 | tf_op jit(solution)/shard_map/while/body/eval_jaxpr/ppermute | solution.py:15
  173.6 11.7 %collective-permute-start.3 = (f32[128,4,128]{2,0,1:T(8,128)S(1)}, f32[128,4,128]{2,0,1:T(8,128)S(1)}, u32[]{:S(2)}, u32[]{:S(2)}) collective-permute-start(f32[128,4,128]{2,0,1:T(8,128)S(1)} %get-tuple-element.279), channel_id=1, source_target_pairs={{0,4},{4,8},{8,12},{12,16},{16,20},{20,24},{24,28},{28,32},{32,36}... | collective-permute-start | bytes 786440 | tf_op jit(solution)/shard_map/while/body/eval_jaxpr/ppermute | solution.py:15
  193.7 11.7 %collective-permute-start.3 = (f32[128,4,128]{2,0,1:T(8,128)S(1)}, f32[128,4,128]{2,0,1:T(8,128)S(1)}, u32[]{:S(2)}, u32[]{:S(2)}) collective-permute-start(f32[128,4,128]{2,0,1:T(8,128)S(1)} %get-tuple-element.279), channel_id=1, source_target_pairs={{0,4},{4,8},{8,12},{12,16},{16,20},{20,24},{24,28},{28,32},{32,36}... | collective-permute-start | bytes 786440 | tf_op jit(solution)/shard_map/while/body/eval_jaxpr/ppermute | solution.py:15
  314.7 11.7 %collective-permute-start.3 = (f32[128,4,128]{2,0,1:T(8,128)S(1)}, f32[128,4,128]{2,0,1:T(8,128)S(1)}, u32[]{:S(2)}, u32[]{:S(2)}) collective-permute-start(f32[128,4,128]{2,0,1:T(8,128)S(1)} %get-tuple-element.279), channel_id=1, source_target_pairs={{0,4},{4,8},{8,12},{12,16},{16,20},{20,24},{24,28},{28,32},{32,36}... | collective-permute-start | bytes 786440 | tf_op jit(solution)/shard_map/while/body/eval_jaxpr/ppermute | solution.py:15
  334.9 11.7 %collective-permute-start.3 = (f32[128,4,128]{2,0,1:T(8,128)S(1)}, f32[128,4,128]{2,0,1:T(8,128)S(1)}, u32[]{:S(2)}, u32[]{:S(2)}) collective-permute-start(f32[128,4,128]{2,0,1:T(8,128)S(1)} %get-tuple-element.279), channel_id=1, source_target_pairs={{0,4},{4,8},{8,12},{12,16},{16,20},{20,24},{24,28},{28,32},{32,36}... | collective-permute-start | bytes 786440 | tf_op jit(solution)/shard_map/while/body/eval_jaxpr/ppermute | solution.py:15
  355.0 11.7 %collective-permute-start.3 = (f32[128,4,128]{2,0,1:T(8,128)S(1)}, f32[128,4,128]{2,0,1:T(8,128)S(1)}, u32[]{:S(2)}, u32[]{:S(2)}) collective-permute-start(f32[128,4,128]{2,0,1:T(8,128)S(1)} %get-tuple-element.279), channel_id=1, source_target_pairs={{0,4},{4,8},{8,12},{12,16},{16,20},{20,24},{24,28},{28,32},{32,36}... | collective-permute-start | bytes 786440 | tf_op jit(solution)/shard_map/while/body/eval_jaxpr/ppermute | solution.py:15
  375.2 11.7 %collective-permute-start.3 = (f32[128,4,128]{2,0,1:T(8,128)S(1)}, f32[128,4,128]{2,0,1:T(8,128)S(1)}, u32[]{:S(2)}, u32[]{:S(2)}) collective-permute-start(f32[128,4,128]{2,0,1:T(8,128)S(1)} %get-tuple-element.279), channel_id=1, source_target_pairs={{0,4},{4,8},{8,12},{12,16},{16,20},{20,24},{24,28},{28,32},{32,36}... | collective-permute-start | bytes 786440 | tf_op jit(solution)/shard_map/while/body/eval_jaxpr/ppermute | solution.py:15
  395.3 11.7 %collective-permute-start.3 = (f32[128,4,128]{2,0,1:T(8,128)S(1)}, f32[128,4,128]{2,0,1:T(8,128)S(1)}, u32[]{:S(2)}, u32[]{:S(2)}) collective-permute-start(f32[128,4,128]{2,0,1:T(8,128)S(1)} %get-tuple-element.279), channel_id=1, source_target_pairs={{0,4},{4,8},{8,12},{12,16},{16,20},{20,24},{24,28},{28,32},{32,36}... | collective-permute-start | bytes 786440 | tf_op jit(solution)/shard_map/while/body/eval_jaxpr/ppermute | solution.py:15
  516.3 11.7 %collective-permute-start.3 = (f32[128,4,128]{2,0,1:T(8,128)S(1)}, f32[128,4,128]{2,0,1:T(8,128)S(1)}, u32[]{:S(2)}, u32[]{:S(2)}) collective-permute-start(f32[128,4,128]{2,0,1:T(8,128)S(1)} %get-tuple-element.279), channel_id=1, source_target_pairs={{0,4},{4,8},{8,12},{12,16},{16,20},{20,24},{24,28},{28,32},{32,36}... | collective-permute-start | bytes 786440 | tf_op jit(solution)/shard_map/while/body/eval_jaxpr/ppermute | solution.py:15
  536.4 11.7 %collective-permute-start.3 = (f32[128,4,128]{2,0,1:T(8,128)S(1)}, f32[128,4,128]{2,0,1:T(8,128)S(1)}, u32[]{:S(2)}, u32[]{:S(2)}) collective-permute-start(f32[128,4,128]{2,0,1:T(8,128)S(1)} %get-tuple-element.279), channel_id=1, source_target_pairs={{0,4},{4,8},{8,12},{12,16},{16,20},{20,24},{24,28},{28,32},{32,36}... | collective-permute-start | bytes 786440 | tf_op jit(solution)/shard_map/while/body/eval_jaxpr/ppermute | solution.py:15
  556.6 11.7 %collective-permute-start.3 = (f32[128,4,128]{2,0,1:T(8,128)S(1)}, f32[128,4,128]{2,0,1:T(8,128)S(1)}, u32[]{:S(2)}, u32[]{:S(2)}) collective-permute-start(f32[128,4,128]{2,0,1:T(8,128)S(1)} %get-tuple-element.279), channel_id=1, source_target_pairs={{0,4},{4,8},{8,12},{12,16},{16,20},{20,24},{24,28},{28,32},{32,36}... | collective-permute-start | bytes 786440 | tf_op jit(solution)/shard_map/while/body/eval_jaxpr/ppermute | solution.py:15
  576.8 11.7 %collective-permute-start.3 = (f32[128,4,128]{2,0,1:T(8,128)S(1)}, f32[128,4,128]{2,0,1:T(8,128)S(1)}, u32[]{:S(2)}, u32[]{:S(2)}) collective-permute-start(f32[128,4,128]{2,0,1:T(8,128)S(1)} %get-tuple-element.279), channel_id=1, source_target_pairs={{0,4},{4,8},{8,12},{12,16},{16,20},{20,24},{24,28},{28,32},{32,36}... | collective-permute-start | bytes 786440 | tf_op jit(solution)/shard_map/while/body/eval_jaxpr/ppermute | solution.py:15
  596.9 11.7 %collective-permute-start.3 = (f32[128,4,128]{2,0,1:T(8,128)S(1)}, f32[128,4,128]{2,0,1:T(8,128)S(1)}, u32[]{:S(2)}, u32[]{:S(2)}) collective-permute-start(f32[128,4,128]{2,0,1:T(8,128)S(1)} %get-tuple-element.279), channel_id=1, source_target_pairs={{0,4},{4,8},{8,12},{12,16},{16,20},{20,24},{24,28},{28,32},{32,36}... | collective-permute-start | bytes 786440 | tf_op jit(solution)/shard_map/while/body/eval_jaxpr/ppermute | solution.py:15
  630.1 14.6 %collective-permute-start.12 = (f32[128,4,128]{0,2,1:T(8,128)S(1)}, f32[128,4,128]{0,2,1:T(8,128)S(1)}, u32[]{:S(2)}, u32[]{:S(2)}) collective-permute-start(f32[128,4,128]{0,2,1:T(8,128)S(1)} %copy.38), channel_id=1, source_target_pairs={{0,132},{4,136},{8,140},{12,144},{16,148},{20,152},{24,156},{28,16... | collective-permute-start | bytes 786440 | tf_op jit(solution)/shard_map/ppermute | solution.py:15
  (165 other events, 1727.0 us)
Sparse Core Ops, SparseCore 0:
  649.2 54.6 reduce-scatter.1
where the time goes:
time: 711 us
  waiting for transfers between devices  626 us (88%)
  matrix products  38.3 us (5%)
  starting transfers between devices  17.9 us (3%)
  between operations  13.6 us (2%)
    ppermute x188, waiting for transfers between devices, shifted(): return lax.ppermute(x, axis, [(i, (i + by) % peers) for i in range(peers)])  571 us
    reduce_scatter x1, waiting for transfers between devices, body(): lax.psum_scatter(jnp.dot(attended, out_weight, preferred_element_type=jnp...  54.8 us
    dot_general x64, matrix products, block_state(): jnp.einsum('hqk,khd->qhd', exponent.astype(jnp.bfloat16), value_block, pr...  19.7 us
    ppermute x188, starting transfers between devices, shifted(): return lax.ppermute(x, axis, [(i, (i + by) % peers) for i in range(peers)])  17.9 us
    dot_general x64, matrix products, block_state(): jnp.einsum('qhd,khd->hqk', query_block, key_block, preferred_element_type...  14.3 us
  transfers between devices with their start and end apart: 189, of which 96 were waited for; matrix products, arithmetic and copies ran while one was open for 5% of the time, Pallas kernels for 0%

commit v1 on v0

v1 whole, which is shorter than its diff:
```python
import functools

import jax
import jax.numpy as jnp
from jax import lax
from jax.experimental import pallas as pl
from jax.experimental.pallas import tpu as pltpu
from jax.sharding import Mesh, PartitionSpec as P

DH = 128
AXES = {"z": 8, "y": 4, "xl": 2, "xh": 2, "c": 2}
PLANE = ("y", "xl")
SLOTS = [(dy, f) for dy in range(4) for f in range(2)]
LOG2E = 1.4426950408889634
TOK = 128
HEADS_LOCAL = 4
STAT_ROWS = 16
VMEM = 48 * 1024 * 1024


def ring(x, by):
    return lax.ppermute(x, "z", [(i, (i + by) % AXES["z"]) for i in range(AXES["z"])])


def plane_perm(dy, f, back):
    pairs = []
    for y in range(4):
        for xl in range(2):
            src, dst = y * 2 + xl, ((y + dy) % 4) * 2 + (xl ^ f)
            pairs.append((dst, src) if back else (src, dst))
    return pairs


def flip(x, axis):
    return lax.ppermute(x, axis, [(0, 1), (1, 0)])


def dot(a, b, dims):
    return lax.dot_general(a, b, (dims, ((), ())), preferred_element_type=jnp.float32)


def attend_kernel(n_blocks, first, last, *refs):
    refs = list(refs)
    take = lambda n: [refs.pop(0) for _ in range(n)]
    q_refs, k_refs, v_refs = take(8), take(n_blocks), take(n_blocks)
    if not first:
        o_in, ml_in = take(2)
    if last:
        out_refs = take(8)
        (stat,) = take(1)
    else:
        o_out, ml_out = take(2)
    head = pl.program_id(0)
    scale = LOG2E * DH**-0.5
    keys = jnp.concatenate([r[...] for r in k_refs], axis=0)
    values = jnp.concatenate([r[...] for r in v_refs], axis=0)
    for j in range(4):
        cols = pl.ds(j * 256, 256)
        queries = jnp.concatenate([q_refs[2 * j][...], q_refs[2 * j + 1][...]], axis=0)
        s = dot(keys, queries, ((1,), (1,)))
        peak = jnp.max(s, axis=0, keepdims=True)
        if not first:
            old_peak = ml_in[0, 0:1, cols]
            peak = jnp.maximum(peak, old_peak)
        p = jnp.exp2((s - peak) * scale)
        total = jnp.sum(p, axis=0, keepdims=True)
        summed = dot(values, p.astype(jnp.bfloat16), ((0,), (0,)))
        if not first:
            decay = jnp.exp2((old_peak - peak) * scale)
            total = total + ml_in[0, 1:2, cols] * decay
            summed = summed + o_in[:, cols] * decay
        if last:
            summed = (summed / total).astype(jnp.bfloat16)
            for i in range(2):
                rows = pl.ds(pl.multiple_of(head * DH, DH), DH)
                out_refs[2 * j + i][rows, :] = summed[:, i * 128 : (i + 1) * 128]
            stat[head, :, cols] = peak * scale + jnp.log2(total)
        else:
            o_out[:, cols] = summed
            ml_out[0, 0:1, cols] = peak
            ml_out[0, 1:2, cols] = total
    if last:

        @pl.when(head == HEADS_LOCAL - 1)
        def _():
            lse = jnp.concatenate([stat[h] for h in range(HEADS_LOCAL)], axis=0)
            hi = lse.astype(jnp.bfloat16).astype(jnp.float32)
            mid = (lse - hi).astype(jnp.bfloat16).astype(jnp.float32)
            low = lse - hi - mid
            rows = jnp.concatenate([hi, mid, low, jnp.zeros_like(hi)], axis=0).astype(jnp.bfloat16)
            for r in range(8):
                out_refs[r][pl.ds(HEADS_LOCAL * DH, STAT_ROWS), :] = rows[:, r * 128 : (r + 1) * 128]


def attend(q_slots, keys, values, state, last):
    n = len(keys)
    first = state is None
    block = pl.BlockSpec((TOK, DH), lambda h: (0, h))
    o_spec = pl.BlockSpec((DH, 8 * TOK), lambda h: (h, 0))
    ml_spec = pl.BlockSpec((1, 2, 8 * TOK), lambda h: (h, 0, 0))
    in_specs = [block] * (8 + 2 * n) + ([] if first else [o_spec, ml_spec])
    if last:
        rows = HEADS_LOCAL * DH + STAT_ROWS
        out_shape = [jax.ShapeDtypeStruct((rows, TOK), jnp.bfloat16)] * 8
        out_specs = [pl.BlockSpec((rows, TOK), lambda h: (0, 0))] * 8
        scratch = [pltpu.VMEM((HEADS_LOCAL, 1, 8 * TOK), jnp.float32)]
    else:
        out_shape = [
            jax.ShapeDtypeStruct((HEADS_LOCAL * DH, 8 * TOK), jnp.float32),
            jax.ShapeDtypeStruct((HEADS_LOCAL, 2, 8 * TOK), jnp.float32),
        ]
        out_specs = [o_spec, ml_spec]
        scratch = []
    elements = HEADS_LOCAL * 8 * TOK * n * TOK
    return pl.pallas_call(
        functools.partial(attend_kernel, n, first, last),
        grid=(HEADS_LOCAL,),
        in_specs=in_specs,
        out_specs=out_specs,
        out_shape=out_shape,
        scratch_shapes=scratch,
        compiler_params=pltpu.CompilerParams(vmem_limit_bytes=VMEM),
        cost_estimate=pl.CostEstimate(
            flops=elements * DH * 4, transcendentals=elements, bytes_accessed=4 << 20
        ),
        name="attend",
    )(*q_slots, *keys, *values, *(() if first else state))


def project_kernel(place, *refs):
    parts, w_ref, send, keep, att = refs[:8], refs[8], refs[9], refs[10], refs[11]

    @pl.when(pl.program_id(0) == 0)
    def _():
        lse = []
        for r in range(8):
            s = parts[r][pl.ds(HEADS_LOCAL * DH, STAT_ROWS), :].astype(jnp.float32)
            lse.append(s[0:4] + s[4:8] + s[8:12])
        top = functools.reduce(jnp.maximum, lse)
        weights = [jnp.exp2(x - top) for x in lse]
        inverse = 1.0 / sum(weights)
        weights = [w * inverse for w in weights]
        c, xh = place[0], place[1]
        for h in range(HEADS_LOCAL):
            rows = pl.ds(h * DH, DH)
            merged = sum(parts[r][rows, :].astype(jnp.float32) * weights[r][h : h + 1, :] for r in range(8))
            tokens = merged.T.astype(jnp.bfloat16)
            for to_xh in range(2):
                for to_c in range(2):
                    here = (to_c ^ 1) * 2 + to_xh
                    there = jnp.where(c == to_c, 2, 0) + jnp.where(xh == to_xh, 1, 0)
                    piece = tokens[(to_xh * 2 + to_c) * 32 : (to_xh * 2 + to_c) * 32 + 32]
                    del here
                    att[pl.ds(pl.multiple_of(there * 32, 32), 32), pl.ds(h * DH, DH)] = piece

    product = dot(att[...], w_ref[...], ((1,), (0,)))
    send[...] = product[:64].astype(jnp.bfloat16)
    keep[...] = product[64:]


def project(place, parts, weight):
    rows = HEADS_LOCAL * DH + STAT_ROWS
    width = weight.shape[1]
    tile = 1024
    return pl.pallas_call(
        project_kernel,
        grid_spec=pltpu.PrefetchScalarGridSpec(
            num_scalar_prefetch=1,
            grid=(width // tile,),
            in_specs=[pl.BlockSpec((rows, TOK), lambda i, p: (0, 0))] * 8
            + [pl.BlockSpec((HEADS_LOCAL * DH, tile), lambda i, p: (0, i))],
            out_specs=[pl.BlockSpec((64, tile), lambda i, p: (0, i))] * 2,
            scratch_shapes=[pltpu.VMEM((TOK, HEADS_LOCAL * DH), jnp.bfloat16)],
        ),
        out_shape=[
            jax.ShapeDtypeStruct((64, width), jnp.bfloat16),
            jax.ShapeDtypeStruct((64, width), jnp.float32),
        ],
        compiler_params=pltpu.CompilerParams(vmem_limit_bytes=VMEM),
        cost_estimate=pl.CostEstimate(
            flops=2 * TOK * HEADS_LOCAL * DH * width, transcendentals=4096, bytes_accessed=6 << 20
        ),
        name="merge_project",
    )(place, *parts, weight)


def body(queries, key_vectors, value_vectors, out_weight):
    up = (key_vectors, value_vectors)
    down = up
    up_blocks, down_blocks = [], []
    for step in range(3):
        up = tuple(ring(x, 1) for x in up)
        down = tuple(ring(x, -1) for x in down)
        up_blocks.append(up)
        down_blocks.append(down)
        if step == 0:
            q_slots = [
                queries if slot == (0, 0) else lax.ppermute(queries, PLANE, plane_perm(*slot, False))
                for slot in SLOTS
            ]
    far = (ring(up[0], 1), ring(down[1], -1))
    near = [(key_vectors, value_vectors)] + up_blocks[:2] + down_blocks[:2]
    state = attend(q_slots, [b[0] for b in near], [b[1] for b in near], None, False)
    third = [up_blocks[2], down_blocks[2]]
    state = attend(q_slots, [b[0] for b in third], [b[1] for b in third], state, False)
    parts = attend(q_slots, [far[0]], [far[1]], state, True)
    parts = [
        part if slot == (0, 0) else lax.ppermute(part, PLANE, plane_perm(*slot, True))
        for slot, part in zip(SLOTS, parts)
    ]
    place = jnp.stack([lax.axis_index("c"), lax.axis_index("xh")]).astype(jnp.int32)
    send, keep = project(place, parts, out_weight)
    both = keep + flip(send, "c").astype(jnp.float32)
    return both[32:] + flip(both[:32].astype(jnp.bfloat16), "xh").astype(jnp.float32)


def solution(mesh):
    fine = Mesh(mesh.devices.reshape(tuple(AXES.values())), tuple(AXES))
    ctx, head = ("z", "y", "xl"), ("xh", "c")
    placed = (P(ctx, head), P(ctx, head), P(ctx, head), P(head, None))
    return jax.shard_map(
        body, mesh=fine, in_specs=placed, out_specs=P(ctx + head, None), check_vma=False
    )
```

time: 711 us -> 97.6 us (0.14)
  waiting for transfers between devices: 626 us -> 25 us
  matrix products: 38.3 us -> 0 us
  starting transfers between devices: 17.9 us -> 46.1 us
  Pallas kernels: 0 us -> 22.5 us
  between operations: 13.6 us -> 0.15 us
    ppermute x188 -> x30, waiting for transfers between devices: 571 us -> 25 us  [the longest x7 8.97 us: body(): lax.ppermute(part, PLANE, plane_perm(*slot, True))]
    reduce_scatter x1 -> x0, waiting for transfers between devices: 54.8 us -> none  [body(): lax.psum_scatter(jnp.dot(attended, out_weight, preferred_element_type=jnp...]
    dot_general x129 -> x0, matrix products: 38.3 us -> none  [the longest x64 19.7 us: block_state(): jnp.einsum('hqk,khd->qhd', exponent.astype(jnp.bfloat16), value_block, pr...]
    ppermute x188 -> x30, starting transfers between devices: 17.9 us -> 46.1 us  [the longest x14 21.6 us: ring(): lax.ppermute(x, 'z', [(i, (i + by) % AXES['z']) for i in range(AXES['z'])])]
    pallas_call x0 -> x4, Pallas kernels: none -> 22.5 us  [the longest x3 18 us: attend(): pl.pallas_call(functools.partial(attend_kernel, n, first, last), grid=(HE...]
  transfers between devices with their start and end apart: 189 -> 30, of which waited for: 96 -> 7; matrix products, arithmetic and copies ran while one was open for 5% -> 0% of each run, Pallas kernels for 0% -> 15%
where the time goes in v1:
time: 97.6 us; the launch traced here: 97.4 us
  starting transfers between devices  46.1 us (47%)
  waiting for transfers between devices  25 us (26%)
  Pallas kernels  22.5 us (23%)
  local copies, waits for them, and re-layouts  2.74 us (3%)
  other arithmetic  1.01 us (1%)
    ppermute x14, starting transfers between devices, ring(): lax.ppermute(x, 'z', [(i, (i + by) % AXES['z']) for i in range(AXES['z'])])  21.6 us
    pallas_call x3, Pallas kernels, attend(): pl.pallas_call(functools.partial(attend_kernel, n, first, last), grid=(HE...  18 us
    ppermute x7, starting transfers between devices, body(): lax.ppermute(queries, PLANE, plane_perm(*slot, False))  10.5 us
    ppermute x7, waiting for transfers between devices, body(): lax.ppermute(part, PLANE, plane_perm(*slot, True))  8.97 us
    ppermute x2, waiting for transfers between devices, flip(): return lax.ppermute(x, axis, [(0, 1), (1, 0)])  8.08 us
    ppermute x7, starting transfers between devices, body(): lax.ppermute(part, PLANE, plane_perm(*slot, True))  8.05 us
    ppermute x2, starting transfers between devices, flip(): return lax.ppermute(x, axis, [(0, 1), (1, 0)])  5.93 us
    pallas_call x1, Pallas kernels, project(): pl.pallas_call(project_kernel, grid_spec=pltpu.PrefetchScalarGridSpec(num...  4.47 us
  transfers between devices with their start and end apart: 30, of which 7 were waited for; matrix products, arithmetic and copies ran while one was open for 0% of the time, Pallas kernels for 15%

profile of v1, /device:TPU:1, one launch (start us, length us, event | category | flops | bytes accessed | tf_op | source)
XLA Modules:
  0.0 97.4 jit_solution(15893199628767968363)
XLA Ops:
  0.0 6.4 %collective-permute-start.11 = (bf16[128,512]{1,0:T(8,128)(2,1)}, bf16[128,512]{1,0:T(8,128)(2,1)S(1)}, u32[]{:S(2)}, u32[]{:S(2)}) collective-permute-start(bf16[128,512]{1,0:T(8,128)(2,1)} %refs_13_.1), channel_id=1, source_target_pairs={{0,224},{32,0},{64,32},{96,64},{128,96},{160,128},{192,160},{224,1... | collective-permute-start | bytes 393224 | tf_op jit(solution)/shard_map/ppermute | solution.py:22
  11.7 2.2 %collective-permute-start.2 = (bf16[128,512]{1,0:T(8,128)(2,1)}, bf16[128,512]{1,0:T(8,128)(2,1)S(1)}, u32[]{:S(2)}, u32[]{:S(2)}) collective-permute-start(bf16[128,512]{1,0:T(8,128)(2,1)} %refs_0_.5), channel_id=1, source_target_pairs={{0,12},{4,8},{8,20},{12,16},{16,28},{20,24},{24,4},{28,0},{1,13},{... | collective-permute-start | bytes 393224 | tf_op jit(solution)/shard_map/ppermute | solution.py:198
  13.9 2.6 %collective-permute-start.3 = (bf16[128,512]{1,0:T(8,128)(2,1)}, bf16[128,512]{1,0:T(8,128)(2,1)S(1)}, u32[]{:S(2)}, u32[]{:S(2)}) collective-permute-start(bf16[128,512]{1,0:T(8,128)(2,1)} %refs_0_.5), channel_id=1, source_target_pairs={{0,16},{4,20},{8,24},{12,28},{16,0},{20,4},{24,8},{28,12},{1,17},{... | collective-permute-start | bytes 393224 | tf_op jit(solution)/shard_map/ppermute | solution.py:198
  16.5 2.4 %collective-permute-start.4 = (bf16[128,512]{1,0:T(8,128)(2,1)}, bf16[128,512]{1,0:T(8,128)(2,1)S(1)}, u32[]{:S(2)}, u32[]{:S(2)}) collective-permute-start(bf16[128,512]{1,0:T(8,128)(2,1)} %refs_0_.5), channel_id=1, source_target_pairs={{0,20},{4,16},{8,28},{12,24},{16,4},{20,0},{24,12},{28,8},{1,21},{... | collective-permute-start | bytes 393224 | tf_op jit(solution)/shard_map/ppermute | solution.py:198
  19.0 2.7 %collective-permute-start.12 = (bf16[128,512]{1,0:T(8,128)(2,1)S(1)}, bf16[128,512]{1,0:T(8,128)(2,1)S(1)}, u32[]{:S(2)}, u32[]{:S(2)}) collective-permute-start(bf16[128,512]{1,0:T(8,128)(2,1)S(1)} %collective-permute-done.11.refs_16_), channel_id=1, source_target_pairs={{0,224},{32,0},{64,32},{96,64},{128,96},{160,128},{192,160},{224,1... | collective-permute-start | bytes 393224 | tf_op jit(solution)/shard_map/ppermute | solution.py:22
  22.4 4.1 %collective-permute-done.3.refs_4_ = bf16[128,512]{1,0:T(8,128)(2,1)S(1)} collective-permute-done((bf16[128,512]{1,0:T(8,128)(2,1)}, bf16[128,512]{1,0:T(8,128)(2,1)S(1)}, u32[]{:S(2)}, u32[]{:S(2)}) %collective-permute-start.3) | collective-permute-done | bytes 131104 | tf_op jit(solution)/shard_map/ppermute | solution.py:198
  26.5 3.3 %collective-permute-start.16 = (bf16[128,512]{1,0:T(8,128)(2,1)S(1)}, bf16[128,512]{1,0:T(8,128)(2,1)S(1)}, u32[]{:S(2)}, u32[]{:S(2)}) collective-permute-start(bf16[128,512]{1,0:T(8,128)(2,1)S(1)} %collective-permute-done.15.refs_11_), channel_id=1, source_target_pairs={{0,224},{32,0},{64,32},{96,64},{128,96},{160,128},{192,160},{224,1... | collective-permute-start | bytes 393224 | tf_op jit(solution)/shard_map/ppermute | solution.py:22
  29.9 2.7 %collective-permute-start.13 = (bf16[128,512]{1,0:T(8,128)(2,1)S(1)}, bf16[128,512]{1,0:T(8,128)(2,1)S(1)}, u32[]{:S(2)}, u32[]{:S(2)}) collective-permute-start(bf16[128,512]{1,0:T(8,128)(2,1)S(1)} %collective-permute-done.12.refs_17_), channel_id=1, source_target_pairs={{0,224},{32,0},{64,32},{96,64},{128,96},{160,128},{192,160},{224,1... | collective-permute-start | bytes 393224 | tf_op jit(solution)/shard_map/ppermute | solution.py:22
  32.6 2.2 %collective-permute-start.17 = (bf16[128,512]{1,0:T(8,128)(2,1)S(1)}, bf16[128,512]{1,0:T(8,128)(2,1)S(1)}, u32[]{:S(2)}, u32[]{:S(2)}) collective-permute-start(bf16[128,512]{1,0:T(8,128)(2,1)S(1)} %collective-permute-done.16.refs_12_), channel_id=1, source_target_pairs={{0,224},{32,0},{64,32},{96,64},{128,96},{160,128},{192,160},{224,1... | collective-permute-start | bytes 393224 | tf_op jit(solution)/shard_map/ppermute | solution.py:22
  34.8 2.5 %collective-permute-done.9.refs_8_ = bf16[128,512]{1,0:T(8,128)(2,1)S(1)} collective-permute-done((bf16[128,512]{1,0:T(8,128)(2,1)S(1)}, bf16[128,512]{1,0:T(8,128)(2,1)S(1)}, u32[]{:S(2)}, u32[]{:S(2)}) %collective-permute-start.9) | collective-permute-done | bytes 131104 | tf_op jit(solution)/shard_map/ppermute | solution.py:22
  37.4 2.7 %collective-permute-start.14 = (bf16[128,512]{1,0:T(8,128)(2,1)S(1)}, bf16[128,512]{1,0:T(8,128)(2,1)S(1)}, u32[]{:S(2)}, u32[]{:S(2)}) collective-permute-start(bf16[128,512]{1,0:T(8,128)(2,1)S(1)} %collective-permute-done.13.refs_11_), channel_id=1, source_target_pairs={{0,224},{32,0},{64,32},{96,64},{128,96},{160,128},{192,160},{224,1... | collective-permute-start | bytes 393224 | tf_op jit(solution)/shard_map/ppermute | solution.py:22
  42.8 9.2 %attend.3 = (f32[512,1024]{1,0:T(8,128)S(1)}, f32[4,2,1024]{2,1,0:T(2,128)S(1)}) custom-call(bf16[128,512]{1,0:T(8,128)(2,1)S(1)} %copy-done, bf16[128,512]{1,0:T(8,128)(2,1)S(1)} %collective-permute-done.refs_1_, bf16[128,512]{1,0:T(8,128)(2,1)S(1)} %collective-permute-done.1.refs_2_, bf16[128,512]{1,0:T(8,128)(2,1)S(1)} %collective-permute-done.2.refs_3_, ...), custom_call_target="tpu_custom_call" | custom-call | flops 1342177280 | bytes 4194304 | tf_op jit(solution)/shard_map/attend/pallas_call | solution.py:115
  51.9 5.7 %attend.4 = (f32[512,1024]{1,0:T(8,128)S(1)}, f32[4,2,1024]{2,1,0:T(2,128)S(1)}) custom-call(bf16[128,512]{1,0:T(8,128)(2,1)S(1)} %copy-done, bf16[128,512]{1,0:T(8,128)(2,1)S(1)} %collective-permute-done.refs_1_, bf16[128,512]{1,0:T(8,128)(2,1)S(1)} %collective-permute-done.1.refs_2_, bf16[128,512]{1,0:T(8,128)(2,1)S(1)} %collective-permute-done.2.refs_3_, ...), custom_call_target="tpu_custom_call" | custom-call | flops 536870912 | bytes 4194304 | tf_op jit(solution)/shard_map/attend/pallas_call | solution.py:115
  57.7 3.2 %attend.5 = (bf16[528,128]{1,0:T(8,128)(2,1)S(1)}, bf16[528,128]{1,0:T(8,128)(2,1)S(1)}, bf16[528,128]{1,0:T(8,128)(2,1)S(1)}, bf16[528,128]{1,0:T(8,128)(2,1)S(...) custom-call(bf16[128,512]{1,0:T(8,128)(2,1)S(1)} %copy-done, ...), custom_call_target="tpu_custom_call" | custom-call | flops 268435456 | bytes 4194304 | tf_op jit(solution)/shard_map/attend/pallas_call | solution.py:115
  61.0 2.4 %collective-permute-start.23 = (bf16[528,128]{1,0:T(8,128)(2,1)S(1)}, bf16[528,128]{1,0:T(8,128)(2,1)S(1)}, u32[]{:S(2)}, u32[]{:S(2)}) collective-permute-start(bf16[528,128]{1,0:T(8,128)(2,1)S(1)} %get-tuple-element.26), channel_id=1, source_target_pairs={{12,0},{8,4},{20,8},{16,12},{28,16},{24,20},{4,24},{0,28},{13,1},{... | collective-permute-start | bytes 405512 | tf_op jit(solution)/shard_map/ppermute | solution.py:208
  63.5 1.9 %collective-permute-start.24 = (bf16[528,128]{1,0:T(8,128)(2,1)S(1)}, bf16[528,128]{1,0:T(8,128)(2,1)S(1)}, u32[]{:S(2)}, u32[]{:S(2)}) collective-permute-start(bf16[528,128]{1,0:T(8,128)(2,1)S(1)} %get-tuple-element.27), channel_id=1, source_target_pairs={{16,0},{20,4},{24,8},{28,12},{0,16},{4,20},{8,24},{12,28},{17,1},{... | collective-permute-start | bytes 405512 | tf_op jit(solution)/shard_map/ppermute | solution.py:208
  66.9 2.0 %collective-permute-start.27 = (bf16[528,128]{1,0:T(8,128)(2,1)S(1)}, bf16[528,128]{1,0:T(8,128)(2,1)S(1)}, u32[]{:S(2)}, u32[]{:S(2)}) collective-permute-start(bf16[528,128]{1,0:T(8,128)(2,1)S(1)} %get-tuple-element.30), channel_id=1, source_target_pairs={{28,0},{24,4},{4,8},{0,12},{12,16},{8,20},{20,24},{16,28},{29,1},{... | collective-permute-start | bytes 405512 | tf_op jit(solution)/shard_map/ppermute | solution.py:208
  69.0 3.1 %collective-permute-done.25.refs_5_ = bf16[528,128]{1,0:T(8,128)(2,1)S(1)} collective-permute-done((bf16[528,128]{1,0:T(8,128)(2,1)S(1)}, bf16[528,128]{1,0:T(8,128)(2,1)S(1)}, u32[]{:S(2)}, u32[]{:S(2)}) %collective-permute-start.25) | collective-permute-done | bytes 135200 | tf_op jit(solution)/shard_map/ppermute | solution.py:208
  72.1 5.8 %collective-permute-done.26.refs_6_ = bf16[528,128]{1,0:T(8,128)(2,1)S(1)} collective-permute-done((bf16[528,128]{1,0:T(8,128)(2,1)S(1)}, bf16[528,128]{1,0:T(8,128)(2,1)S(1)}, u32[]{:S(2)}, u32[]{:S(2)}) %collective-permute-start.26) | collective-permute-done | bytes 135200 | tf_op jit(solution)/shard_map/ppermute | solution.py:208
  78.0 4.5 %merge_project.1 = (bf16[64,4096]{1,0:T(8,128)(2,1)S(1)}, f32[64,4096]{1,0:T(8,128)S(1)}) custom-call(s32[2]{0:T(128)S(1)} %pad_add_fusion.place, bf16[528,128]{1,0:T(8,128)(2,1)S(1)} %get-tuple-element.23.refs_0_, bf16[528,128]{1,0:T(8,128)(2,1)S(1)} %collective-permute-done.21.refs_1_, bf16[528,128]{1,0:T(8,128)(2,1)S(1)} %collective-permute-done.22.refs_2_, ...), custom_call_target="tpu_custom_call" | custom-call | flops 536870912 | bytes 6291456 | tf_op jit(solution)/shard_map/merge_project/pallas_call | solution.py:165
  82.4 3.4 %collective-permute-start.28 = (bf16[64,4096]{1,0:T(8,128)(2,1)S(1)}, bf16[64,4096]{1,0:T(8,128)(2,1)S(1)}, u32[]{:S(2)}, u32[]{:S(2)}) collective-permute-start(bf16[64,4096]{1,0:T(8,128)(2,1)S(1)} %get-tuple-element.32), channel_id=1, source_target_pairs={{0,1},{1,0},{2,3},{3,2},{4,5},{5,4},{6,7},{7,6},{8,9},{9,8},{10,11... | collective-permute-start | bytes 1572872 | tf_op jit(solution)/shard_map/ppermute | solution.py:35
  85.8 1.5 %collective-permute-done.28 = bf16[64,4096]{1,0:T(8,128)(2,1)S(1)} collective-permute-done((bf16[64,4096]{1,0:T(8,128)(2,1)S(1)}, bf16[64,4096]{1,0:T(8,128)(2,1)S(1)}, u32[]{:S(2)}, u32[]{:S(2)}) %collective-permute-start.28) | collective-permute-done | bytes 524320 | tf_op jit(solution)/shard_map/ppermute | solution.py:35
  87.5 2.6 %collective-permute-start.29 = (bf16[32,4096]{1,0:T(8,128)(2,1)S(1)}, bf16[32,4096]{1,0:T(8,128)(2,1)S(1)}, u32[]{:S(2)}, u32[]{:S(2)}) collective-permute-start(bf16[32,4096]{1,0:T(8,128)(2,1)S(1)} %slice.13), channel_id=1, source_target_pairs={{0,2},{2,0},{1,3},{3,1},{4,6},{6,4},{5,7},{7,5},{8,10},{10,8},{9,1... | collective-permute-start | bytes 786440 | tf_op jit(solution)/shard_map/ppermute | solution.py:35
  90.0 6.5 %collective-permute-done.29 = bf16[32,4096]{1,0:T(8,128)(2,1)S(1)} collective-permute-done((bf16[32,4096]{1,0:T(8,128)(2,1)S(1)}, bf16[32,4096]{1,0:T(8,128)(2,1)S(1)}, u32[]{:S(2)}, u32[]{:S(2)}) %collective-permute-start.29) | collective-permute-done | bytes 262176 | tf_op jit(solution)/shard_map/ppermute | solution.py:35
  (50 shorter events, 11.7 us)
Async XLA Ops:
  0.0 9.1 %collective-permute-start.11 = (bf16[128,512]{1,0:T(8,128)(2,1)}, bf16[128,512]{1,0:T(8,128)(2,1)S(1)}, u32[]{:S(2)}, u32[]{:S(2)}) collective-permute-start(bf16[128,512]{1,0:T(8,128)(2,1)} %refs_13_.1), channel_id=1, source_target_pairs={{0,224},{32,0},{64,32},{96,64},{128,96},{160,128},{192,160},{224,1... | collective-permute-start | bytes 393224 | tf_op jit(solution)/shard_map/ppermute | solution.py:22
  7.1 6.8 %collective-permute-start.18 = (bf16[128,512]{1,0:T(8,128)(2,1)}, bf16[128,512]{1,0:T(8,128)(2,1)S(1)}, u32[]{:S(2)}, u32[]{:S(2)}) collective-permute-start(bf16[128,512]{1,0:T(8,128)(2,1)} %refs_13_.1), channel_id=1, source_target_pairs={{0,32},{32,64},{64,96},{96,128},{128,160},{160,192},{192,224},{224... | collective-permute-start | bytes 393224 | tf_op jit(solution)/shard_map/ppermute | solution.py:22
  7.9 8.7 %collective-permute-start.7 = (bf16[128,512]{1,0:T(8,128)(2,1)}, bf16[128,512]{1,0:T(8,128)(2,1)S(1)}, u32[]{:S(2)}, u32[]{:S(2)}) collective-permute-start(bf16[128,512]{1,0:T(8,128)(2,1)} %refs_8_.2), channel_id=1, source_target_pairs={{0,32},{32,64},{64,96},{96,128},{128,160},{160,192},{192,224},{224... | collective-permute-start | bytes 393224 | tf_op jit(solution)/shard_map/ppermute | solution.py:22
  7.9 11.1 %collective-permute-start = (bf16[128,512]{1,0:T(8,128)(2,1)}, bf16[128,512]{1,0:T(8,128)(2,1)S(1)}, u32[]{:S(2)}, u32[]{:S(2)}) collective-permute-start(bf16[128,512]{1,0:T(8,128)(2,1)} %refs_0_.5), channel_id=1, source_target_pairs={{0,4},{4,0},{8,12},{12,8},{16,20},{20,16},{24,28},{28,24},{1,5},{5... | collective-permute-start | bytes 393224 | tf_op jit(solution)/shard_map/ppermute | solution.py:198
  9.1 9.8 %collective-permute-start.1 = (bf16[128,512]{1,0:T(8,128)(2,1)}, bf16[128,512]{1,0:T(8,128)(2,1)S(1)}, u32[]{:S(2)}, u32[]{:S(2)}) collective-permute-start(bf16[128,512]{1,0:T(8,128)(2,1)} %refs_0_.5), channel_id=1, source_target_pairs={{0,8},{4,12},{8,16},{12,20},{16,24},{20,28},{24,0},{28,4},{1,9},{5... | collective-permute-start | bytes 393224 | tf_op jit(solution)/shard_map/ppermute | solution.py:198
  11.7 9.9 %collective-permute-start.2 = (bf16[128,512]{1,0:T(8,128)(2,1)}, bf16[128,512]{1,0:T(8,128)(2,1)S(1)}, u32[]{:S(2)}, u32[]{:S(2)}) collective-permute-start(bf16[128,512]{1,0:T(8,128)(2,1)} %refs_0_.5), channel_id=1, source_target_pairs={{0,12},{4,8},{8,20},{12,16},{16,28},{20,24},{24,4},{28,0},{1,13},{... | collective-permute-start | bytes 393224 | tf_op jit(solution)/shard_map/ppermute | solution.py:198
  13.9 12.6 %collective-permute-start.3 = (bf16[128,512]{1,0:T(8,128)(2,1)}, bf16[128,512]{1,0:T(8,128)(2,1)S(1)}, u32[]{:S(2)}, u32[]{:S(2)}) collective-permute-start(bf16[128,512]{1,0:T(8,128)(2,1)} %refs_0_.5), channel_id=1, source_target_pairs={{0,16},{4,20},{8,24},{12,28},{16,0},{20,4},{24,8},{28,12},{1,17},{... | collective-permute-start | bytes 393224 | tf_op jit(solution)/shard_map/ppermute | solution.py:198
  16.5 13.2 %collective-permute-start.4 = (bf16[128,512]{1,0:T(8,128)(2,1)}, bf16[128,512]{1,0:T(8,128)(2,1)S(1)}, u32[]{:S(2)}, u32[]{:S(2)}) collective-permute-start(bf16[128,512]{1,0:T(8,128)(2,1)} %refs_0_.5), channel_id=1, source_target_pairs={{0,20},{4,16},{8,28},{12,24},{16,4},{20,0},{24,12},{28,8},{1,21},{... | collective-permute-start | bytes 393224 | tf_op jit(solution)/shard_map/ppermute | solution.py:198
  19.0 10.8 %collective-permute-start.8 = (bf16[128,512]{1,0:T(8,128)(2,1)S(1)}, bf16[128,512]{1,0:T(8,128)(2,1)S(1)}, u32[]{:S(2)}, u32[]{:S(2)}) collective-permute-start(bf16[128,512]{1,0:T(8,128)(2,1)S(1)} %collective-permute-done.7.refs_9_), channel_id=1, source_target_pairs={{0,32},{32,64},{64,96},{96,128},{128,160},{160,192},{192,224},{224... | collective-permute-start | bytes 393224 | tf_op jit(solution)/shard_map/ppermute | solution.py:22
  19.0 10.9 %collective-permute-start.12 = (bf16[128,512]{1,0:T(8,128)(2,1)S(1)}, bf16[128,512]{1,0:T(8,128)(2,1)S(1)}, u32[]{:S(2)}, u32[]{:S(2)}) collective-permute-start(bf16[128,512]{1,0:T(8,128)(2,1)S(1)} %collective-permute-done.11.refs_16_), channel_id=1, source_target_pairs={{0,224},{32,0},{64,32},{96,64},{128,96},{160,128},{192,160},{224,1... | collective-permute-start | bytes 393224 | tf_op jit(solution)/shard_map/ppermute | solution.py:22
  21.6 10.9 %collective-permute-start.5 = (bf16[128,512]{1,0:T(8,128)(2,1)}, bf16[128,512]{1,0:T(8,128)(2,1)S(1)}, u32[]{:S(2)}, u32[]{:S(2)}) collective-permute-start(bf16[128,512]{1,0:T(8,128)(2,1)} %refs_0_.5), channel_id=1, source_target_pairs={{0,24},{4,28},{8,0},{12,4},{16,8},{20,12},{24,16},{28,20},{1,25},{... | collective-permute-start | bytes 393224 | tf_op jit(solution)/shard_map/ppermute | solution.py:198
  26.5 6.1 %collective-permute-start.16 = (bf16[128,512]{1,0:T(8,128)(2,1)S(1)}, bf16[128,512]{1,0:T(8,128)(2,1)S(1)}, u32[]{:S(2)}, u32[]{:S(2)}) collective-permute-start(bf16[128,512]{1,0:T(8,128)(2,1)S(1)} %collective-permute-done.15.refs_11_), channel_id=1, source_target_pairs={{0,224},{32,0},{64,32},{96,64},{128,96},{160,128},{192,160},{224,1... | collective-permute-start | bytes 393224 | tf_op jit(solution)/shard_map/ppermute | solution.py:22
  29.8 7.6 %collective-permute-start.9 = (bf16[128,512]{1,0:T(8,128)(2,1)S(1)}, bf16[128,512]{1,0:T(8,128)(2,1)S(1)}, u32[]{:S(2)}, u32[]{:S(2)}) collective-permute-start(bf16[128,512]{1,0:T(8,128)(2,1)S(1)} %collective-permute-done.8.refs_10_), channel_id=1, source_target_pairs={{0,32},{32,64},{64,96},{96,128},{128,160},{160,192},{192,224},{224... | collective-permute-start | bytes 393224 | tf_op jit(solution)/shard_map/ppermute | solution.py:22
  29.9 7.5 %collective-permute-start.13 = (bf16[128,512]{1,0:T(8,128)(2,1)S(1)}, bf16[128,512]{1,0:T(8,128)(2,1)S(1)}, u32[]{:S(2)}, u32[]{:S(2)}) collective-permute-start(bf16[128,512]{1,0:T(8,128)(2,1)S(1)} %collective-permute-done.12.refs_17_), channel_id=1, source_target_pairs={{0,224},{32,0},{64,32},{96,64},{128,96},{160,128},{192,160},{224,1... | collective-permute-start | bytes 393224 | tf_op jit(solution)/shard_map/ppermute | solution.py:22
  32.6 7.5 %collective-permute-start.6 = (bf16[128,512]{1,0:T(8,128)(2,1)}, bf16[128,512]{1,0:T(8,128)(2,1)S(1)}, u32[]{:S(2)}, u32[]{:S(2)}) collective-permute-start(bf16[128,512]{1,0:T(8,128)(2,1)} %refs_0_.5), channel_id=1, source_target_pairs={{0,28},{4,24},{8,4},{12,0},{16,12},{20,8},{24,20},{28,16},{1,29},{... | collective-permute-start | bytes 393224 | tf_op jit(solution)/shard_map/ppermute | solution.py:198
  32.6 19.4 %collective-permute-start.17 = (bf16[128,512]{1,0:T(8,128)(2,1)S(1)}, bf16[128,512]{1,0:T(8,128)(2,1)S(1)}, u32[]{:S(2)}, u32[]{:S(2)}) collective-permute-start(bf16[128,512]{1,0:T(8,128)(2,1)S(1)} %collective-permute-done.16.refs_12_), channel_id=1, source_target_pairs={{0,224},{32,0},{64,32},{96,64},{128,96},{160,128},{192,160},{224,1... | collective-permute-start | bytes 393224 | tf_op jit(solution)/shard_map/ppermute | solution.py:22
  34.8 17.1 %collective-permute-start.20 = (bf16[128,512]{1,0:T(8,128)(2,1)S(1)}, bf16[128,512]{1,0:T(8,128)(2,1)S(1)}, u32[]{:S(2)}, u32[]{:S(2)}) collective-permute-start(bf16[128,512]{1,0:T(8,128)(2,1)S(1)} %collective-permute-done.19.refs_15_), channel_id=1, source_target_pairs={{0,32},{32,64},{64,96},{96,128},{128,160},{160,192},{192,224},{224... | collective-permute-start | bytes 393224 | tf_op jit(solution)/shard_map/ppermute | solution.py:22
  37.4 20.3 %collective-permute-start.10 = (bf16[128,512]{1,0:T(8,128)(2,1)S(1)}, bf16[128,512]{1,0:T(8,128)(2,1)S(1)}, u32[]{:S(2)}, u32[]{:S(2)}) collective-permute-start(bf16[128,512]{1,0:T(8,128)(2,1)S(1)} %collective-permute-done.9.refs_8_), channel_id=1, source_target_pairs={{0,32},{32,64},{64,96},{96,128},{128,160},{160,192},{192,224},{224... | collective-permute-start | bytes 393224 | tf_op jit(solution)/shard_map/ppermute | solution.py:22
  37.4 20.3 %collective-permute-start.14 = (bf16[128,512]{1,0:T(8,128)(2,1)S(1)}, bf16[128,512]{1,0:T(8,128)(2,1)S(1)}, u32[]{:S(2)}, u32[]{:S(2)}) collective-permute-start(bf16[128,512]{1,0:T(8,128)(2,1)S(1)} %collective-permute-done.13.refs_11_), channel_id=1, source_target_pairs={{0,224},{32,0},{64,32},{96,64},{128,96},{160,128},{192,160},{224,1... | collective-permute-start | bytes 393224 | tf_op jit(solution)/shard_map/ppermute | solution.py:22
  61.0 8.0 %collective-permute-start.23 = (bf16[528,128]{1,0:T(8,128)(2,1)S(1)}, bf16[528,128]{1,0:T(8,128)(2,1)S(1)}, u32[]{:S(2)}, u32[]{:S(2)}) collective-permute-start(bf16[528,128]{1,0:T(8,128)(2,1)S(1)} %get-tuple-element.26), channel_id=1, source_target_pairs={{12,0},{8,4},{20,8},{16,12},{28,16},{24,20},{4,24},{0,28},{13,1},{... | collective-permute-start | bytes 405512 | tf_op jit(solution)/shard_map/ppermute | solution.py:208
  65.4 6.8 %collective-permute-start.25 = (bf16[528,128]{1,0:T(8,128)(2,1)S(1)}, bf16[528,128]{1,0:T(8,128)(2,1)S(1)}, u32[]{:S(2)}, u32[]{:S(2)}) collective-permute-start(bf16[528,128]{1,0:T(8,128)(2,1)S(1)} %get-tuple-element.28), channel_id=1, source_target_pairs={{20,0},{16,4},{28,8},{24,12},{4,16},{0,20},{12,24},{8,28},{21,1},{... | collective-permute-start | bytes 405512 | tf_op jit(solution)/shard_map/ppermute | solution.py:208
  66.9 11.1 %collective-permute-start.26 = (bf16[528,128]{1,0:T(8,128)(2,1)S(1)}, bf16[528,128]{1,0:T(8,128)(2,1)S(1)}, u32[]{:S(2)}, u32[]{:S(2)}) collective-permute-start(bf16[528,128]{1,0:T(8,128)(2,1)S(1)} %get-tuple-element.29), channel_id=1, source_target_pairs={{24,0},{28,4},{0,8},{4,12},{8,16},{12,20},{16,24},{20,28},{25,1},{... | collective-permute-start | bytes 405512 | tf_op jit(solution)/shard_map/ppermute | solution.py:208
  66.9 11.1 %collective-permute-start.27 = (bf16[528,128]{1,0:T(8,128)(2,1)S(1)}, bf16[528,128]{1,0:T(8,128)(2,1)S(1)}, u32[]{:S(2)}, u32[]{:S(2)}) collective-permute-start(bf16[528,128]{1,0:T(8,128)(2,1)S(1)} %get-tuple-element.30), channel_id=1, source_target_pairs={{28,0},{24,4},{4,8},{0,12},{12,16},{8,20},{20,24},{16,28},{29,1},{... | collective-permute-start | bytes 405512 | tf_op jit(solution)/shard_map/ppermute | solution.py:208
  87.5 9.1 %collective-permute-start.29 = (bf16[32,4096]{1,0:T(8,128)(2,1)S(1)}, bf16[32,4096]{1,0:T(8,128)(2,1)S(1)}, u32[]{:S(2)}, u32[]{:S(2)}) collective-permute-start(bf16[32,4096]{1,0:T(8,128)(2,1)S(1)} %slice.13), channel_id=1, source_target_pairs={{0,2},{2,0},{1,3},{3,1},{4,6},{6,4},{5,7},{7,5},{8,10},{10,8},{9,1... | collective-permute-start | bytes 786440 | tf_op jit(solution)/shard_map/ppermute | solution.py:35
  (9 other events, 35.4 us)

commit v2 on v0

v2 whole, which is shorter than its diff:
```python
import functools

import jax
import jax.numpy as jnp
from jax import lax
from jax.experimental import pallas as pl
from jax.experimental.pallas import tpu as pltpu
from jax.sharding import Mesh, PartitionSpec as P

DH = 128
AXES = {"z": 8, "y": 4, "xl": 2, "xh": 2, "c": 2}
PLANE = ("y", "xl")
SLOTS = ((0, 0), (0, 1), (2, 0), (2, 1), (-1, 0), (-1, 1), (1, 0), (1, 1))
FIRST_OUT = (2, 3, 5, 7, 4, 6, 1)
SPAN = 4
LOG2E = 1.4426950408889634
TOK = 128
HEADS_LOCAL = 4
STAT_ROWS = 16
VMEM = 24 * 1024 * 1024
CHUNK = 1024


def shift(x, axis, by):
    n = AXES[axis]
    return lax.ppermute(x, axis, [(i, (i + by) % n) for i in range(n)])


def to_slot(x, slot):
    dy, f = slot
    pairs = [(y * 2 + xl, (y + dy) % 4 * 2 + (xl ^ f)) for y in range(4) for xl in range(2)]
    return lax.ppermute(x, PLANE, pairs)


def flip(x, axis):
    return lax.ppermute(x, axis, [(0, 1), (1, 0)])


def dot(a, b, dims):
    return lax.dot_general(a, b, (dims, ((), ())), preferred_element_type=jnp.float32)


def pack_kernel(k, v, own):
    own[:TOK] = k[...]
    own[TOK:] = v[...]


def pack(keys, values):
    return pl.pallas_call(
        pack_kernel,
        grid=(1,),
        in_specs=[pl.BlockSpec(keys.shape, lambda i: (0, 0))] * 2,
        out_specs=pl.BlockSpec((2 * TOK, keys.shape[1]), lambda i: (0, 0)),
        out_shape=jax.ShapeDtypeStruct((2 * TOK, keys.shape[1]), jnp.bfloat16),
        name="pack",
    )(keys, values)


def attend_kernel(n_blocks, last, *refs):
    refs = list(refs)
    take = lambda n: [refs.pop(0) for _ in range(n)]
    q_refs, kv_refs = take(5), take(n_blocks)
    if last:
        far_k, far_v, o_in, ml_in = take(4)
        out_refs = take(8)
    else:
        o_out, ml_out = take(2)
    scale = LOG2E * DH**-0.5

    def operands(h):
        lanes = slice(h * DH, (h + 1) * DH)
        keys = [r[:TOK, lanes] for r in kv_refs]
        values = [r[TOK:, lanes] for r in kv_refs]
        if last:
            keys.append(far_k[:, lanes])
            values.append(far_v[:, lanes])
        return lanes, jnp.concatenate(keys, axis=0), jnp.concatenate(values, axis=0).T

    def scores(lanes, keys, j):
        pieces = q_refs[:3] if j == 0 else q_refs[3:]
        return dot(keys, jnp.concatenate([r[:, lanes] for r in pieces], axis=0), ((1,), (1,)))

    work = []
    for h in range(HEADS_LOCAL):
        lanes, keys, values = operands(h)
        for j in range(8 // SPAN):
            work.append((h, j, lanes, keys, values))
    lse = [[None] * (8 // SPAN) for _ in range(HEADS_LOCAL)]
    ahead = scores(*work[0][2:4], work[0][1])
    for i, (h, j, _, _, values) in enumerate(work):
        s = ahead
        if i + 1 < len(work):
            ahead = scores(*work[i + 1][2:4], work[i + 1][1])
        cols = slice(j * SPAN * TOK, (j + 1) * SPAN * TOK)
        rows = slice(h * DH, (h + 1) * DH)
        peak = jnp.max(s, axis=0, keepdims=True)
        if last:
            old_peak = ml_in[h, 0:1, cols]
            peak = jnp.maximum(peak, old_peak)
        p = jnp.exp2((s - peak) * scale)
        total = jnp.sum(p, axis=0, keepdims=True)
        summed = dot(values, p.astype(jnp.bfloat16), ((1,), (0,)))
        if last:
            decay = jnp.exp2((old_peak - peak) * scale)
            total = total + ml_in[h, 1:2, cols] * decay
            inverse = 1.0 / total
            summed = (summed * inverse + o_in[rows, cols] * (decay * inverse)).astype(jnp.bfloat16)
            for i in range(SPAN):
                out_refs[j * SPAN + i][rows, :] = summed[:, i * TOK : (i + 1) * TOK]
            lse[h][j] = peak * scale + jnp.log2(total)
        else:
            o_out[rows, cols] = summed
            ml_out[h, 0:1, cols] = peak
            ml_out[h, 1:2, cols] = total
    if last:
        whole = jnp.concatenate([jnp.concatenate(x, axis=1) for x in lse], axis=0)
        hi = whole.astype(jnp.bfloat16).astype(jnp.float32)
        mid = (whole - hi).astype(jnp.bfloat16).astype(jnp.float32)
        low = whole - hi - mid
        stats = jnp.concatenate([hi, mid, low, jnp.zeros_like(hi)], axis=0).astype(jnp.bfloat16)
        for r in range(8):
            out_refs[r][HEADS_LOCAL * DH :, :] = stats[:, r * TOK : (r + 1) * TOK]


def attend(queries, blocks, far, state):
    last = far is not None
    whole = lambda x: pl.BlockSpec(x.shape, lambda i: (0,) * len(x.shape))
    operands = [*queries, *blocks] + ([*far, *state] if last else [])
    if last:
        out_shape = [
            jax.ShapeDtypeStruct((HEADS_LOCAL * DH + STAT_ROWS, TOK), jnp.bfloat16)
        ] * 8
    else:
        out_shape = [
            jax.ShapeDtypeStruct((HEADS_LOCAL * DH, 8 * TOK), jnp.float32),
            jax.ShapeDtypeStruct((HEADS_LOCAL, 2, 8 * TOK), jnp.float32),
        ]
    elements = HEADS_LOCAL * 8 * TOK * (len(blocks) + last) * TOK
    return pl.pallas_call(
        functools.partial(attend_kernel, len(blocks), last),
        grid=(1,),
        in_specs=[whole(x) for x in operands],
        out_specs=[whole(x) for x in out_shape],
        out_shape=out_shape,
        compiler_params=pltpu.CompilerParams(vmem_limit_bytes=VMEM),
        cost_estimate=pl.CostEstimate(
            flops=elements * DH * 12, transcendentals=elements, bytes_accessed=4 << 20
        ),
        name="attend",
    )(*operands)


def merge_kernel(place, *refs):
    parts, w_ref, sends, keeps = refs[:8], refs[8], refs[9:11], refs[11:13]
    att = refs[13]
    lse = []
    for r in range(8):
        s = parts[r][HEADS_LOCAL * DH :, :].astype(jnp.float32)
        lse.append(s[0:4] + s[4:8] + s[8:12])
    top = functools.reduce(jnp.maximum, lse)
    weights = [jnp.exp2(x - top) for x in lse]
    inverse = 1.0 / sum(weights)
    weights = [w * inverse for w in weights]
    c, xh = place[0], place[1]
    for h in range(HEADS_LOCAL):
        rows = slice(h * DH, (h + 1) * DH)
        merged = sum(parts[r][rows, :].astype(jnp.float32) * weights[r][h : h + 1, :] for r in range(8))
        tokens = merged.T.astype(jnp.bfloat16)
        for to in range(4):
            there = jnp.where(xh == to // 2, 2, 0) + jnp.where(c == to % 2, 1, 0)
            att[pl.ds(pl.multiple_of(there * 32, 32), 32), rows] = tokens[to * 32 : to * 32 + 32]
    for at in range(0, w_ref.shape[1], CHUNK):
        cols = slice(at, at + CHUNK)
        product = dot(att[...], w_ref[:, cols], ((1,), (0,)))
        for side in range(2):
            sends[side][:, cols] = product[side * 64 : side * 64 + 32].astype(jnp.bfloat16)
            keeps[side][:, cols] = product[side * 64 + 32 : side * 64 + 64]


def project(place, parts, weight):
    depth, width = weight.shape
    whole = lambda x: pl.BlockSpec(x.shape, lambda i, p: (0,) * len(x.shape))
    out_shape = [
        jax.ShapeDtypeStruct((32, width), dtype)
        for dtype in (jnp.bfloat16, jnp.bfloat16, jnp.float32, jnp.float32)
    ]
    return pl.pallas_call(
        merge_kernel,
        grid_spec=pltpu.PrefetchScalarGridSpec(
            num_scalar_prefetch=1,
            grid=(1,),
            in_specs=[whole(x) for x in parts] + [pl.BlockSpec(memory_space=pltpu.VMEM)],
            out_specs=[whole(x) for x in out_shape],
            scratch_shapes=[pltpu.VMEM((TOK, depth), jnp.bfloat16)],
        ),
        out_shape=out_shape,
        compiler_params=pltpu.CompilerParams(vmem_limit_bytes=VMEM),
        cost_estimate=pl.CostEstimate(
            flops=2 * TOK * depth * width, transcendentals=4096, bytes_accessed=6 << 20
        ),
        name="merge_project",
    )(place, *parts, weight)


def body(queries, key_vectors, value_vectors, out_weight):
    own = pack(key_vectors, value_vectors)
    pair = pack(queries, flip(queries, "xl"))
    up, down = shift(own, "z", 1), shift(own, "z", -1)
    blocks = [own, up, down]
    up, down, pair = lax.optimization_barrier((up, down, pair))
    above, below = shift(pair, "y", 1), shift(pair, "y", -1)
    up, down = shift(up, "z", 1), shift(down, "z", -1)
    blocks += [up, down]
    up, down, above, below = lax.optimization_barrier((up, down, above, below))
    up, down = shift(up, "z", 1), shift(down, "z", -1)
    blocks += [up, down]
    far = (shift(up[:TOK], "z", 1), shift(down[TOK:], "z", -1))
    q_parts = [pair, shift(above[:TOK], "y", 1), shift(below[TOK:], "y", -1), above, below]
    state = attend(q_parts, blocks, None, None)
    parts = attend(q_parts, [], far, state)
    parts = list(parts)
    for r in FIRST_OUT:
        parts[r] = to_slot(parts[r], SLOTS[r])
    place = jnp.stack([lax.axis_index("c"), lax.axis_index("xh")]).astype(jnp.int32)
    send_other, send_own, keep_other, keep_own = project(place, parts, out_weight)
    other = keep_other + flip(send_other, "c").astype(jnp.float32)
    arrived = flip(other.astype(jnp.bfloat16), "xh").astype(jnp.float32)
    return keep_own + flip(send_own, "c").astype(jnp.float32) + arrived


def solution(mesh):
    fine = Mesh(mesh.devices.reshape(tuple(AXES.values())), tuple(AXES))
    ctx, head = ("z", "y", "xl"), ("xh", "c")
    placed = (P(ctx, head), P(ctx, head), P(ctx, head), P(head, None))
    return jax.shard_map(
        body, mesh=fine, in_specs=placed, out_specs=P(ctx + head, None), check_vma=False
    )
```

time: 711 us -> 79.6 us (0.11)
  waiting for transfers between devices: 626 us -> 23.8 us
  matrix products: 38.3 us -> 0 us
  starting transfers between devices: 17.9 us -> 38.1 us
  between operations: 13.6 us -> 0.12 us
  Pallas kernels: 0 us -> 11.6 us
    ppermute x188 -> x23, waiting for transfers between devices: 571 us -> 23.8 us  [the longest x4 10.8 us: flip(): return lax.ppermute(x, axis, [(0, 1), (1, 0)])]
    reduce_scatter x1 -> x0, waiting for transfers between devices: 54.8 us -> none  [body(): lax.psum_scatter(jnp.dot(attended, out_weight, preferred_element_type=jnp...]
    dot_general x129 -> x0, matrix products: 38.3 us -> none  [the longest x64 19.7 us: block_state(): jnp.einsum('hqk,khd->qhd', exponent.astype(jnp.bfloat16), value_block, pr...]
    ppermute x188 -> x23, starting transfers between devices: 17.9 us -> 38.1 us  [the longest x12 20.4 us: shift(): return lax.ppermute(x, axis, [(i, (i + by) % n) for i in range(n)])]
    pallas_call x0 -> x5, Pallas kernels: none -> 11.6 us  [the longest x2 6.7 us: attend(): pl.pallas_call(functools.partial(attend_kernel, len(blocks), last), grid=...]
  transfers between devices with their start and end apart: 189 -> 23, of which waited for: 96 -> 10; matrix products, arithmetic and copies ran while one was open for 5% -> 0% of each run, Pallas kernels for 0% -> 9%
where the time goes in v2:
time: 79.6 us; the launch traced here: 79.4 us
  starting transfers between devices  38.1 us (48%)
  waiting for transfers between devices  23.8 us (30%)
  Pallas kernels  11.6 us (15%)
  local copies, waits for them, and re-layouts  4.77 us (6%)
  other arithmetic  0.99 us (1%)
    ppermute x12, starting transfers between devices, shift(): return lax.ppermute(x, axis, [(i, (i + by) % n) for i in range(n)])  20.4 us
    ppermute x4, waiting for transfers between devices, flip(): return lax.ppermute(x, axis, [(0, 1), (1, 0)])  10.8 us
    ppermute x4, starting transfers between devices, flip(): return lax.ppermute(x, axis, [(0, 1), (1, 0)])  9.65 us
    ppermute x7, starting transfers between devices, to_slot(): return lax.ppermute(x, PLANE, pairs)  8.07 us
    ppermute x7, waiting for transfers between devices, to_slot(): return lax.ppermute(x, PLANE, pairs)  8.05 us
    pallas_call x2, Pallas kernels, attend(): pl.pallas_call(functools.partial(attend_kernel, len(blocks), last), grid=...  6.7 us
    ppermute x12, waiting for transfers between devices, shift(): return lax.ppermute(x, axis, [(i, (i + by) % n) for i in range(n)])  5.02 us
    unnamed x8, local copies, waits for them, and re-layouts  4.73 us
  transfers between devices with their start and end apart: 23, of which 10 were waited for; matrix products, arithmetic and copies ran while one was open for 0% of the time, Pallas kernels for 9%

profile of v2, /device:TPU:1, one launch (start us, length us, event | category | flops | bytes accessed | tf_op | source)
XLA Modules:
  0.0 79.4 jit_solution(14338287166515097527)
XLA Ops:
  0.0 1.7 %pack.2.refs_5_ = bf16[256,512]{1,0:T(8,128)(2,1)} custom-call(bf16[128,512]{1,0:T(8,128)(2,1)} %k.2, bf16[128,512]{1,0:T(8,128)(2,1)} %v.1), custom_call_target="tpu_custom_call" | custom-call | tf_op jit(solution)/shard_map/pack/pallas_call | solution.py:49
  1.7 2.5 %collective-permute-start = (bf16[256,512]{1,0:T(8,128)(2,1)}, bf16[256,512]{1,0:T(8,128)(2,1)S(1)}, u32[]{:S(2)}, u32[]{:S(2)}) collective-permute-start(bf16[256,512]{1,0:T(8,128)(2,1)} %pack.2.refs_5_), channel_id=1, source_target_pairs={{0,32},{32,64},{64,96},{96,128},{128,160},{160,192},{192,224},{224... | collective-permute-start | bytes 786440 | tf_op jit(solution)/shard_map/ppermute | solution.py:26
  4.2 3.9 %collective-permute-start.1 = (bf16[256,512]{1,0:T(8,128)(2,1)}, bf16[256,512]{1,0:T(8,128)(2,1)S(1)}, u32[]{:S(2)}, u32[]{:S(2)}) collective-permute-start(bf16[256,512]{1,0:T(8,128)(2,1)} %pack.2.refs_5_), channel_id=1, source_target_pairs={{0,224},{32,0},{64,32},{96,64},{128,96},{160,128},{192,160},{224,1... | collective-permute-start | bytes 786440 | tf_op jit(solution)/shard_map/ppermute | solution.py:26
  9.3 3.1 %collective-permute-done.2.v = bf16[128,512]{1,0:T(8,128)(2,1)S(1)} collective-permute-done((bf16[128,512]{1,0:T(8,128)(2,1)}, bf16[128,512]{1,0:T(8,128)(2,1)S(1)}, u32[]{:S(2)}, u32[]{:S(2)}) %collective-permute-start.2) | collective-permute-done | bytes 131104 | tf_op jit(solution)/shard_map/ppermute | solution.py:36
  13.1 1.7 %pack.3.refs_0_ = bf16[256,512]{1,0:T(8,128)(2,1)} custom-call(bf16[128,512]{1,0:T(8,128)(2,1)} %k.3, bf16[128,512]{1,0:T(8,128)(2,1)} %copy-done.3), custom_call_target="tpu_custom_call" | custom-call | tf_op jit(solution)/shard_map/pack/pallas_call | solution.py:49
  16.1 1.5 %collective-permute-start.6 = (bf16[256,512]{1,0:T(8,128)(2,1)}, bf16[256,512]{1,0:T(8,128)(2,1)S(1)}, u32[]{:S(2)}, u32[]{:S(2)}) collective-permute-start(bf16[256,512]{1,0:T(8,128)(2,1)} %pack.3.refs_0_), channel_id=1, source_target_pairs={{0,24},{8,0},{16,8},{24,16},{1,25},{9,1},{17,9},{25,17},{2,26},{10... | collective-permute-start | bytes 786440 | tf_op jit(solution)/shard_map/ppermute | solution.py:26
  17.6 2.7 %collective-permute-start.4 = (bf16[256,512]{1,0:T(8,128)(2,1)S(1)}, bf16[256,512]{1,0:T(8,128)(2,1)S(1)}, u32[]{:S(2)}, u32[]{:S(2)}) collective-permute-start(bf16[256,512]{1,0:T(8,128)(2,1)S(1)} %collective-permute-done.1.refs_7_), channel_id=1, source_target_pairs={{0,224},{32,0},{64,32},{96,64},{128,96},{160,128},{192,160},{224,1... | collective-permute-start | bytes 786440 | tf_op jit(solution)/shard_map/ppermute | solution.py:26
  20.3 2.0 %collective-permute-done.5.refs_3_ = bf16[256,512]{1,0:T(8,128)(2,1)S(1)} collective-permute-done((bf16[256,512]{1,0:T(8,128)(2,1)}, bf16[256,512]{1,0:T(8,128)(2,1)S(1)}, u32[]{:S(2)}, u32[]{:S(2)}) %collective-permute-start.5) | collective-permute-done | bytes 262176 | tf_op jit(solution)/shard_map/ppermute | solution.py:26
  22.3 2.1 %collective-permute-done.3.refs_8_ = bf16[256,512]{1,0:T(8,128)(2,1)S(1)} collective-permute-done((bf16[256,512]{1,0:T(8,128)(2,1)S(1)}, bf16[256,512]{1,0:T(8,128)(2,1)S(1)}, u32[]{:S(2)}, u32[]{:S(2)}) %collective-permute-start.3) | collective-permute-done | bytes 262176 | tf_op jit(solution)/shard_map/ppermute | solution.py:26
  25.3 1.7 %collective-permute-start.11 = (bf16[256,512]{1,0:T(8,128)(2,1)S(1)}, bf16[256,512]{1,0:T(8,128)(2,1)S(1)}, u32[]{:S(2)}, u32[]{:S(2)}) collective-permute-start(bf16[256,512]{1,0:T(8,128)(2,1)S(1)} %collective-permute-done.4.refs_9_), channel_id=1, source_target_pairs={{0,224},{32,0},{64,32},{96,64},{128,96},{160,128},{192,160},{224,1... | collective-permute-start | bytes 786440 | tf_op jit(solution)/shard_map/ppermute | solution.py:26
  27.2 2.7 %collective-permute-start.8 = (bf16[128,512]{1,0:T(8,128)(2,1)S(1)}, bf16[128,512]{1,0:T(8,128)(2,1)S(1)}, u32[]{:S(2)}, u32[]{:S(2)}) collective-permute-start(bf16[128,512]{1,0:T(8,128)(2,1)S(1)} %slice.13), channel_id=1, source_target_pairs={{0,24},{8,0},{16,8},{24,16},{1,25},{9,1},{17,9},{25,17},{2,26},{10... | collective-permute-start | bytes 393224 | tf_op jit(solution)/shard_map/ppermute | solution.py:26
  30.9 2.9 %collective-permute-start.12 = (bf16[128,512]{1,0:T(8,128)(2,1)S(1)}, bf16[128,512]{1,0:T(8,128)(2,1)S(1)}, u32[]{:S(2)}, u32[]{:S(2)}) collective-permute-start(bf16[128,512]{1,0:T(8,128)(2,1)S(1)} %slice.17), channel_id=1, source_target_pairs={{0,224},{32,0},{64,32},{96,64},{128,96},{160,128},{192,160},{224,1... | collective-permute-start | bytes 393224 | tf_op jit(solution)/shard_map/ppermute | solution.py:26
  35.7 5.3 %attend.2 = (f32[512,1024]{1,0:T(8,128)S(1)}, f32[4,2,1024]{2,1,0:T(2,128)S(1)}) custom-call(bf16[256,512]{1,0:T(8,128)(2,1)S(1)} %copy-done.1, bf16[128,512]{1,0:T(8,128)(2,1)S(1)} %collective-permute-done.7.refs_1_, bf16[128,512]{1,0:T(8,128)(2,1)S(1)} %collective-permute-done.8.refs_2_, bf16[256,512]{1,0:T(8,128)(2,1)S(1)} %collective-permute-done.5.refs_3_, ...), custom_call_target="tpu_custom_call" | custom-call | flops 5637144576 | bytes 4194304 | tf_op jit(solution)/shard_map/attend/pallas_call | solution.py:139
  41.1 1.4 %attend.3 = (bf16[528,128]{1,0:T(8,128)(2,1)S(1)}, bf16[528,128]{1,0:T(8,128)(2,1)S(1)}, bf16[528,128]{1,0:T(8,128)(2,1)S(1)}, bf16[528,128]{1,0:T(8,128)(2,1)S(...) custom-call(bf16[256,512]{1,0:T(8,128)(2,1)S(1)} %copy-done.1, ...), custom_call_target="tpu_custom_call" | custom-call | flops 805306368 | bytes 4194304 | tf_op jit(solution)/shard_map/attend/pallas_call | solution.py:139
  45.0 1.8 %collective-permute-start.15 = (bf16[528,128]{1,0:T(8,128)(2,1)S(1)}, bf16[528,128]{1,0:T(8,128)(2,1)S(1)}, u32[]{:S(2)}, u32[]{:S(2)}) collective-permute-start(bf16[528,128]{1,0:T(8,128)(2,1)S(1)} %get-tuple-element.38), channel_id=1, source_target_pairs={{0,20},{4,16},{8,28},{12,24},{16,4},{20,0},{24,12},{28,8},{1,21},{... | collective-permute-start | bytes 405512 | tf_op jit(solution)/shard_map/ppermute | solution.py:32
  46.7 1.3 %collective-permute-start.16 = (bf16[528,128]{1,0:T(8,128)(2,1)S(1)}, bf16[528,128]{1,0:T(8,128)(2,1)S(1)}, u32[]{:S(2)}, u32[]{:S(2)}) collective-permute-start(bf16[528,128]{1,0:T(8,128)(2,1)S(1)} %get-tuple-element.39), channel_id=1, source_target_pairs={{0,24},{4,28},{8,0},{12,4},{16,8},{20,12},{24,16},{28,20},{1,25},{... | collective-permute-start | bytes 405512 | tf_op jit(solution)/shard_map/ppermute | solution.py:32
  49.1 1.3 %collective-permute-start.18 = (bf16[528,128]{1,0:T(8,128)(2,1)S(1)}, bf16[528,128]{1,0:T(8,128)(2,1)S(1)}, u32[]{:S(2)}, u32[]{:S(2)}) collective-permute-start(bf16[528,128]{1,0:T(8,128)(2,1)S(1)} %get-tuple-element.41), channel_id=1, source_target_pairs={{0,8},{4,12},{8,16},{12,20},{16,24},{20,28},{24,0},{28,4},{1,9},{5... | collective-permute-start | bytes 405512 | tf_op jit(solution)/shard_map/ppermute | solution.py:32
  51.4 1.8 %collective-permute-done.17.refs_5_ = bf16[528,128]{1,0:T(8,128)(2,1)S(1)} collective-permute-done((bf16[528,128]{1,0:T(8,128)(2,1)S(1)}, bf16[528,128]{1,0:T(8,128)(2,1)S(1)}, u32[]{:S(2)}, u32[]{:S(2)}) %collective-permute-start.17) | collective-permute-done | bytes 135200 | tf_op jit(solution)/shard_map/ppermute | solution.py:32
  53.2 5.5 %collective-permute-done.18.refs_6_ = bf16[528,128]{1,0:T(8,128)(2,1)S(1)} collective-permute-done((bf16[528,128]{1,0:T(8,128)(2,1)S(1)}, bf16[528,128]{1,0:T(8,128)(2,1)S(1)}, u32[]{:S(2)}, u32[]{:S(2)}) %collective-permute-start.18) | collective-permute-done | bytes 135200 | tf_op jit(solution)/shard_map/ppermute | solution.py:32
  58.7 2.2 %copy-done = bf16[512,4096]{1,0:T(8,128)(2,1)S(1)} copy-done((bf16[512,4096]{1,0:T(8,128)(2,1)S(1)}, bf16[512,4096]{1,0:T(8,128)(2,1)}, u32[]{:S(2)}) %copy-start) | copy-done | bytes 4194328
  60.9 1.5 %merge_project.1 = (bf16[32,4096]{1,0:T(8,128)(2,1)S(1)}, bf16[32,4096]{1,0:T(8,128)(2,1)S(1)}, f32[32,4096]{1,0:T(8,128)S(1)}, f32[32,4096]{1,0:T(8,128)S(1)}) custom-call(s32[2]{0:T(128)S(1)} %pad_add_fusion.place, bf16[528,128]{1,0:T(8,128)(2,1)S(1)} %get-tuple-element.35.refs_0_, bf16[528,128]{1,0:T(8,128)(2,1)S(1)} %collective-permute-done.13.refs_1_, ...), custom_call_target="tpu_custom_call" | custom-call | flops 536870912 | bytes 6291456 | tf_op jit(solution)/shard_map/merge_project/pallas_call | solution.py:187
  62.4 5.8 %collective-permute-start.21 = (bf16[32,4096]{1,0:T(8,128)(2,1)S(1)}, bf16[32,4096]{1,0:T(8,128)(2,1)S(1)}, u32[]{:S(2)}, u32[]{:S(2)}) collective-permute-start(bf16[32,4096]{1,0:T(8,128)(2,1)S(1)} %get-tuple-element.46), channel_id=1, source_target_pairs={{0,1},{1,0},{2,3},{3,2},{4,5},{5,4},{6,7},{7,6},{8,9},{9,8},{10,11... | collective-permute-start | bytes 786440 | tf_op jit(solution)/shard_map/ppermute | solution.py:36
  69.4 2.5 %collective-permute-start.22 = (bf16[32,4096]{1,0:T(8,128)(2,1)S(1)}, bf16[32,4096]{1,0:T(8,128)(2,1)S(1)}, u32[]{:S(2)}, u32[]{:S(2)}) collective-permute-start(bf16[32,4096]{1,0:T(8,128)(2,1)S(1)} %add_convert_fusion), channel_id=1, source_target_pairs={{0,2},{2,0},{1,3},{3,1},{4,6},{6,4},{5,7},{7,5},{8,10},{10,8},{9,1... | collective-permute-start | bytes 786440 | tf_op jit(solution)/shard_map/ppermute | solution.py:36
  72.0 6.6 %collective-permute-done.22 = bf16[32,4096]{1,0:T(8,128)(2,1)S(1)} collective-permute-done((bf16[32,4096]{1,0:T(8,128)(2,1)S(1)}, bf16[32,4096]{1,0:T(8,128)(2,1)S(1)}, u32[]{:S(2)}, u32[]{:S(2)}) %collective-permute-start.22) | collective-permute-done | bytes 262176 | tf_op jit(solution)/shard_map/ppermute | solution.py:36
  (42 shorter events, 13.7 us)
Async XLA Ops:
  1.7 13.1 %collective-permute-start = (bf16[256,512]{1,0:T(8,128)(2,1)}, bf16[256,512]{1,0:T(8,128)(2,1)S(1)}, u32[]{:S(2)}, u32[]{:S(2)}) collective-permute-start(bf16[256,512]{1,0:T(8,128)(2,1)} %pack.2.refs_5_), channel_id=1, source_target_pairs={{0,32},{32,64},{64,96},{96,128},{128,160},{160,192},{192,224},{224... | collective-permute-start | bytes 786440 | tf_op jit(solution)/shard_map/ppermute | solution.py:26
  4.2 10.6 %collective-permute-start.1 = (bf16[256,512]{1,0:T(8,128)(2,1)}, bf16[256,512]{1,0:T(8,128)(2,1)S(1)}, u32[]{:S(2)}, u32[]{:S(2)}) collective-permute-start(bf16[256,512]{1,0:T(8,128)(2,1)} %pack.2.refs_5_), channel_id=1, source_target_pairs={{0,224},{32,0},{64,32},{96,64},{128,96},{160,128},{192,160},{224,1... | collective-permute-start | bytes 786440 | tf_op jit(solution)/shard_map/ppermute | solution.py:26
  8.1 4.3 %collective-permute-start.2 = (bf16[128,512]{1,0:T(8,128)(2,1)}, bf16[128,512]{1,0:T(8,128)(2,1)S(1)}, u32[]{:S(2)}, u32[]{:S(2)}) collective-permute-start(bf16[128,512]{1,0:T(8,128)(2,1)} %k.3), channel_id=1, source_target_pairs={{0,4},{4,0},{1,5},{5,1},{2,6},{6,2},{3,7},{7,3},{8,12},{12,8},{9,1... | collective-permute-start | bytes 393224 | tf_op jit(solution)/shard_map/ppermute | solution.py:36
  14.8 7.5 %collective-permute-start.5 = (bf16[256,512]{1,0:T(8,128)(2,1)}, bf16[256,512]{1,0:T(8,128)(2,1)S(1)}, u32[]{:S(2)}, u32[]{:S(2)}) collective-permute-start(bf16[256,512]{1,0:T(8,128)(2,1)} %pack.3.refs_0_), channel_id=1, source_target_pairs={{0,8},{8,16},{16,24},{24,0},{1,9},{9,17},{17,25},{25,1},{2,10},{10... | collective-permute-start | bytes 786440 | tf_op jit(solution)/shard_map/ppermute | solution.py:26
  16.1 6.2 %collective-permute-start.6 = (bf16[256,512]{1,0:T(8,128)(2,1)}, bf16[256,512]{1,0:T(8,128)(2,1)S(1)}, u32[]{:S(2)}, u32[]{:S(2)}) collective-permute-start(bf16[256,512]{1,0:T(8,128)(2,1)} %pack.3.refs_0_), channel_id=1, source_target_pairs={{0,24},{8,0},{16,8},{24,16},{1,25},{9,1},{17,9},{25,17},{2,26},{10... | collective-permute-start | bytes 786440 | tf_op jit(solution)/shard_map/ppermute | solution.py:26
  17.6 6.8 %collective-permute-start.3 = (bf16[256,512]{1,0:T(8,128)(2,1)S(1)}, bf16[256,512]{1,0:T(8,128)(2,1)S(1)}, u32[]{:S(2)}, u32[]{:S(2)}) collective-permute-start(bf16[256,512]{1,0:T(8,128)(2,1)S(1)} %collective-permute-done.refs_6_), channel_id=1, source_target_pairs={{0,32},{32,64},{64,96},{96,128},{128,160},{160,192},{192,224},{224... | collective-permute-start | bytes 786440 | tf_op jit(solution)/shard_map/ppermute | solution.py:26
  17.6 6.8 %collective-permute-start.4 = (bf16[256,512]{1,0:T(8,128)(2,1)S(1)}, bf16[256,512]{1,0:T(8,128)(2,1)S(1)}, u32[]{:S(2)}, u32[]{:S(2)}) collective-permute-start(bf16[256,512]{1,0:T(8,128)(2,1)S(1)} %collective-permute-done.1.refs_7_), channel_id=1, source_target_pairs={{0,224},{32,0},{64,32},{96,64},{128,96},{160,128},{192,160},{224,1... | collective-permute-start | bytes 786440 | tf_op jit(solution)/shard_map/ppermute | solution.py:26
  24.4 6.4 %collective-permute-start.9 = (bf16[256,512]{1,0:T(8,128)(2,1)S(1)}, bf16[256,512]{1,0:T(8,128)(2,1)S(1)}, u32[]{:S(2)}, u32[]{:S(2)}) collective-permute-start(bf16[256,512]{1,0:T(8,128)(2,1)S(1)} %collective-permute-done.3.refs_8_), channel_id=1, source_target_pairs={{0,32},{32,64},{64,96},{96,128},{128,160},{160,192},{192,224},{224... | collective-permute-start | bytes 786440 | tf_op jit(solution)/shard_map/ppermute | solution.py:26
  25.3 5.6 %collective-permute-start.11 = (bf16[256,512]{1,0:T(8,128)(2,1)S(1)}, bf16[256,512]{1,0:T(8,128)(2,1)S(1)}, u32[]{:S(2)}, u32[]{:S(2)}) collective-permute-start(bf16[256,512]{1,0:T(8,128)(2,1)S(1)} %collective-permute-done.4.refs_9_), channel_id=1, source_target_pairs={{0,224},{32,0},{64,32},{96,64},{128,96},{160,128},{192,160},{224,1... | collective-permute-start | bytes 786440 | tf_op jit(solution)/shard_map/ppermute | solution.py:26
  27.0 6.8 %collective-permute-start.7 = (bf16[128,512]{1,0:T(8,128)(2,1)S(1)}, bf16[128,512]{1,0:T(8,128)(2,1)S(1)}, u32[]{:S(2)}, u32[]{:S(2)}) collective-permute-start(bf16[128,512]{1,0:T(8,128)(2,1)S(1)} %slice.12), channel_id=1, source_target_pairs={{0,8},{8,16},{16,24},{24,0},{1,9},{9,17},{17,25},{25,1},{2,10},{10... | collective-permute-start | bytes 393224 | tf_op jit(solution)/shard_map/ppermute | solution.py:26
  27.2 6.7 %collective-permute-start.8 = (bf16[128,512]{1,0:T(8,128)(2,1)S(1)}, bf16[128,512]{1,0:T(8,128)(2,1)S(1)}, u32[]{:S(2)}, u32[]{:S(2)}) collective-permute-start(bf16[128,512]{1,0:T(8,128)(2,1)S(1)} %slice.13), channel_id=1, source_target_pairs={{0,24},{8,0},{16,8},{24,16},{1,25},{9,1},{17,9},{25,17},{2,26},{10... | collective-permute-start | bytes 393224 | tf_op jit(solution)/shard_map/ppermute | solution.py:26
  30.8 10.2 %collective-permute-start.10 = (bf16[128,512]{1,0:T(8,128)(2,1)S(1)}, bf16[128,512]{1,0:T(8,128)(2,1)S(1)}, u32[]{:S(2)}, u32[]{:S(2)}) collective-permute-start(bf16[128,512]{1,0:T(8,128)(2,1)S(1)} %slice.16), channel_id=1, source_target_pairs={{0,32},{32,64},{64,96},{96,128},{128,160},{160,192},{192,224},{224... | collective-permute-start | bytes 393224 | tf_op jit(solution)/shard_map/ppermute | solution.py:26
  30.9 10.1 %collective-permute-start.12 = (bf16[128,512]{1,0:T(8,128)(2,1)S(1)}, bf16[128,512]{1,0:T(8,128)(2,1)S(1)}, u32[]{:S(2)}, u32[]{:S(2)}) collective-permute-start(bf16[128,512]{1,0:T(8,128)(2,1)S(1)} %slice.17), channel_id=1, source_target_pairs={{0,224},{32,0},{64,32},{96,64},{128,96},{160,128},{192,160},{224,1... | collective-permute-start | bytes 393224 | tf_op jit(solution)/shard_map/ppermute | solution.py:26
  42.5 6.6 %collective-permute-start.13 = (bf16[528,128]{1,0:T(8,128)(2,1)S(1)}, bf16[528,128]{1,0:T(8,128)(2,1)S(1)}, u32[]{:S(2)}, u32[]{:S(2)}) collective-permute-start(bf16[528,128]{1,0:T(8,128)(2,1)S(1)} %get-tuple-element.36), channel_id=1, source_target_pairs={{0,4},{4,0},{8,12},{12,8},{16,20},{20,16},{24,28},{28,24},{1,5},{5... | collective-permute-start | bytes 405512 | tf_op jit(solution)/shard_map/ppermute | solution.py:32
  43.8 6.7 %collective-permute-start.14 = (bf16[528,128]{1,0:T(8,128)(2,1)S(1)}, bf16[528,128]{1,0:T(8,128)(2,1)S(1)}, u32[]{:S(2)}, u32[]{:S(2)}) collective-permute-start(bf16[528,128]{1,0:T(8,128)(2,1)S(1)} %get-tuple-element.37), channel_id=1, source_target_pairs={{0,16},{4,20},{8,24},{12,28},{16,0},{20,4},{24,8},{28,12},{1,17},{... | collective-permute-start | bytes 405512 | tf_op jit(solution)/shard_map/ppermute | solution.py:32
  45.0 6.3 %collective-permute-start.15 = (bf16[528,128]{1,0:T(8,128)(2,1)S(1)}, bf16[528,128]{1,0:T(8,128)(2,1)S(1)}, u32[]{:S(2)}, u32[]{:S(2)}) collective-permute-start(bf16[528,128]{1,0:T(8,128)(2,1)S(1)} %get-tuple-element.38), channel_id=1, source_target_pairs={{0,20},{4,16},{8,28},{12,24},{16,4},{20,0},{24,12},{28,8},{1,21},{... | collective-permute-start | bytes 405512 | tf_op jit(solution)/shard_map/ppermute | solution.py:32
  46.7 4.7 %collective-permute-start.16 = (bf16[528,128]{1,0:T(8,128)(2,1)S(1)}, bf16[528,128]{1,0:T(8,128)(2,1)S(1)}, u32[]{:S(2)}, u32[]{:S(2)}) collective-permute-start(bf16[528,128]{1,0:T(8,128)(2,1)S(1)} %get-tuple-element.39), channel_id=1, source_target_pairs={{0,24},{4,28},{8,0},{12,4},{16,8},{20,12},{24,16},{28,20},{1,25},{... | collective-permute-start | bytes 405512 | tf_op jit(solution)/shard_map/ppermute | solution.py:32
  48.1 5.1 %collective-permute-start.17 = (bf16[528,128]{1,0:T(8,128)(2,1)S(1)}, bf16[528,128]{1,0:T(8,128)(2,1)S(1)}, u32[]{:S(2)}, u32[]{:S(2)}) collective-permute-start(bf16[528,128]{1,0:T(8,128)(2,1)S(1)} %get-tuple-element.40), channel_id=1, source_target_pairs={{0,28},{4,24},{8,4},{12,0},{16,12},{20,8},{24,20},{28,16},{1,29},{... | collective-permute-start | bytes 405512 | tf_op jit(solution)/shard_map/ppermute | solution.py:32
  49.1 9.6 %collective-permute-start.18 = (bf16[528,128]{1,0:T(8,128)(2,1)S(1)}, bf16[528,128]{1,0:T(8,128)(2,1)S(1)}, u32[]{:S(2)}, u32[]{:S(2)}) collective-permute-start(bf16[528,128]{1,0:T(8,128)(2,1)S(1)} %get-tuple-element.41), channel_id=1, source_target_pairs={{0,8},{4,12},{8,16},{12,20},{16,24},{20,28},{24,0},{28,4},{1,9},{5... | collective-permute-start | bytes 405512 | tf_op jit(solution)/shard_map/ppermute | solution.py:32
  50.5 8.2 %collective-permute-start.19 = (bf16[528,128]{1,0:T(8,128)(2,1)S(1)}, bf16[528,128]{1,0:T(8,128)(2,1)S(1)}, u32[]{:S(2)}, u32[]{:S(2)}) collective-permute-start(bf16[528,128]{1,0:T(8,128)(2,1)S(1)} %get-tuple-element.42), channel_id=1, source_target_pairs={{0,12},{4,8},{8,20},{12,16},{16,28},{20,24},{24,4},{28,0},{1,13},{... | collective-permute-start | bytes 405512 | tf_op jit(solution)/shard_map/ppermute | solution.py:32
  58.7 2.2 %copy-start = (bf16[512,4096]{1,0:T(8,128)(2,1)S(1)}, bf16[512,4096]{1,0:T(8,128)(2,1)}, u32[]{:S(2)}) copy-start(bf16[512,4096]{1,0:T(8,128)(2,1)} %refs_8_.1) | copy-start | bytes 12582916
  62.4 7.0 %collective-permute-start.21 = (bf16[32,4096]{1,0:T(8,128)(2,1)S(1)}, bf16[32,4096]{1,0:T(8,128)(2,1)S(1)}, u32[]{:S(2)}, u32[]{:S(2)}) collective-permute-start(bf16[32,4096]{1,0:T(8,128)(2,1)S(1)} %get-tuple-element.46), channel_id=1, source_target_pairs={{0,1},{1,0},{2,3},{3,2},{4,5},{5,4},{6,7},{7,6},{8,9},{9,8},{10,11... | collective-permute-start | bytes 786440 | tf_op jit(solution)/shard_map/ppermute | solution.py:36
  68.2 3.7 %collective-permute-start.20 = (bf16[32,4096]{1,0:T(8,128)(2,1)S(1)}, bf16[32,4096]{1,0:T(8,128)(2,1)S(1)}, u32[]{:S(2)}, u32[]{:S(2)}) collective-permute-start(bf16[32,4096]{1,0:T(8,128)(2,1)S(1)} %get-tuple-element.44), channel_id=1, source_target_pairs={{0,1},{1,0},{2,3},{3,2},{4,5},{5,4},{6,7},{7,6},{8,9},{9,8},{10,11... | collective-permute-start | bytes 786440 | tf_op jit(solution)/shard_map/ppermute | solution.py:36
  69.4 9.1 %collective-permute-start.22 = (bf16[32,4096]{1,0:T(8,128)(2,1)S(1)}, bf16[32,4096]{1,0:T(8,128)(2,1)S(1)}, u32[]{:S(2)}, u32[]{:S(2)}) collective-permute-start(bf16[32,4096]{1,0:T(8,128)(2,1)S(1)} %add_convert_fusion), channel_id=1, source_target_pairs={{0,2},{2,0},{1,3},{3,1},{4,6},{6,4},{5,7},{7,5},{8,10},{10,8},{9,1... | collective-permute-start | bytes 786440 | tf_op jit(solution)/shard_map/ppermute | solution.py:36
  (3 other events, 2.5 us)

commit v3 on v2

--- a/solution.py
+++ b/solution.py
@@ -17,7 +17,7 @@
 TOK = 128
 HEADS_LOCAL = 4
 STAT_ROWS = 16
-VMEM = 24 * 1024 * 1024
+VMEM = 13 * 1024 * 1024
 CHUNK = 1024
 
 
@@ -52,6 +52,10 @@
         in_specs=[pl.BlockSpec(keys.shape, lambda i: (0, 0))] * 2,
         out_specs=pl.BlockSpec((2 * TOK, keys.shape[1]), lambda i: (0, 0)),
         out_shape=jax.ShapeDtypeStruct((2 * TOK, keys.shape[1]), jnp.bfloat16),
+        compiler_params=pltpu.CompilerParams(vmem_limit_bytes=4 << 20),
+        cost_estimate=pl.CostEstimate(
+            flops=8 * keys.size, transcendentals=0, bytes_accessed=8 * keys.size
+        ),
         name="pack",
     )(keys, values)
 
@@ -124,7 +128,9 @@
 
 def attend(queries, blocks, far, state):
     last = far is not None
-    whole = lambda x: pl.BlockSpec(x.shape, lambda i: (0,) * len(x.shape))
+    whole = lambda x: pl.BlockSpec(
+        x.shape, lambda i: (0,) * len(x.shape), pipeline_mode=pl.Buffered(1)
+    )
     operands = [*queries, *blocks] + ([*far, *state] if last else [])
     if last:
         out_shape = [
@@ -150,7 +156,7 @@
     )(*operands)
 
 
-def merge_kernel(place, *refs):
+def merge_kernel(*refs):
     parts, w_ref, sends, keeps = refs[:8], refs[8], refs[9:11], refs[11:13]
     att = refs[13]
     lse = []
@@ -161,7 +167,7 @@
     weights = [jnp.exp2(x - top) for x in lse]
     inverse = 1.0 / sum(weights)
     weights = [w * inverse for w in weights]
-    c, xh = place[0], place[1]
+    c, xh = lax.axis_index("c"), lax.axis_index("xh")
     for h in range(HEADS_LOCAL):
         rows = slice(h * DH, (h + 1) * DH)
         merged = sum(parts[r][rows, :].astype(jnp.float32) * weights[r][h : h + 1, :] for r in range(8))
@@ -177,29 +183,31 @@
             keeps[side][:, cols] = product[side * 64 + 32 : side * 64 + 64]
 
 
-def project(place, parts, weight):
+def project(parts, weight):
     depth, width = weight.shape
-    whole = lambda x: pl.BlockSpec(x.shape, lambda i, p: (0,) * len(x.shape))
+    whole = lambda x: pl.BlockSpec(x.shape, lambda i: (0,) * len(x.shape))
     out_shape = [
         jax.ShapeDtypeStruct((32, width), dtype)
         for dtype in (jnp.bfloat16, jnp.bfloat16, jnp.float32, jnp.float32)
     ]
     return pl.pallas_call(
         merge_kernel,
-        grid_spec=pltpu.PrefetchScalarGridSpec(
-            num_scalar_prefetch=1,
-            grid=(1,),
-            in_specs=[whole(x) for x in parts] + [pl.BlockSpec(memory_space=pltpu.VMEM)],
-            out_specs=[whole(x) for x in out_shape],
-            scratch_shapes=[pltpu.VMEM((TOK, depth), jnp.bfloat16)],
-        ),
+        grid=(1,),
+        in_specs=[whole(x) for x in parts]
+            + [
+                pl.BlockSpec(
+                    weight.shape, lambda i: (0, 0), pipeline_mode=pl.Buffered(1)
+                )
+            ],
+        out_specs=[whole(x) for x in out_shape],
+        scratch_shapes=[pltpu.VMEM((TOK, depth), jnp.bfloat16)],
         out_shape=out_shape,
         compiler_params=pltpu.CompilerParams(vmem_limit_bytes=VMEM),
         cost_estimate=pl.CostEstimate(
             flops=2 * TOK * depth * width, transcendentals=4096, bytes_accessed=6 << 20
         ),
         name="merge_project",
-    )(place, *parts, weight)
+    )(*parts, weight)
 
 
 def body(queries, key_vectors, value_vectors, out_weight):
@@ -221,8 +229,7 @@
     parts = list(parts)
     for r in FIRST_OUT:
         parts[r] = to_slot(parts[r], SLOTS[r])
-    place = jnp.stack([lax.axis_index("c"), lax.axis_index("xh")]).astype(jnp.int32)
-    send_other, send_own, keep_other, keep_own = project(place, parts, out_weight)
+    send_other, send_own, keep_other, keep_own = project(parts, out_weight)
     other = keep_other + flip(send_other, "c").astype(jnp.float32)
     arrived = flip(other.astype(jnp.bfloat16), "xh").astype(jnp.float32)
     return keep_own + flip(send_own, "c").astype(jnp.float32) + arrived

time: 79.6 us -> 74.9 us (0.941)
  Pallas kernels: 11.6 us -> 7.68 us
  local copies, waits for them, and re-layouts: 4.77 us -> 2.76 us
  waiting for transfers between devices: 23.8 us -> 25.3 us
    pallas_call x2, Pallas kernels: 3.37 us -> 0.04 us  [pack(): pl.pallas_call(pack_kernel, grid=(1,), in_specs=[pl.BlockSpec(keys.shape,...]
    unnamed x8, local copies, waits for them, and re-layouts: 4.73 us -> 2.72 us
    ppermute x12, waiting for transfers between devices: 5.02 us -> 6.21 us  [shift(): return lax.ppermute(x, axis, [(i, (i + by) % n) for i in range(n)])]
  transfers between devices with their start and end apart: 23 -> 23, of which waited for: 10 -> 10; matrix products, arithmetic and copies ran while one was open for 0% -> 0% of each run, Pallas kernels for 9% -> 7%
where the time goes in v3:
time: 74.9 us; the launch traced here: 74.7 us
  starting transfers between devices  37.9 us (51%)
  waiting for transfers between devices  25.3 us (34%)
  Pallas kernels  7.68 us (10%)
  local copies, waits for them, and re-layouts  2.76 us (4%)
  other arithmetic  0.93 us (1%)
    ppermute x12, starting transfers between devices, shift(): return lax.ppermute(x, axis, [(i, (i + by) % n) for i in range(n)])  20.5 us
    ppermute x4, waiting for transfers between devices, flip(): return lax.ppermute(x, axis, [(0, 1), (1, 0)])  10.8 us
    ppermute x4, starting transfers between devices, flip(): return lax.ppermute(x, axis, [(0, 1), (1, 0)])  9.35 us
    ppermute x7, waiting for transfers between devices, to_slot(): return lax.ppermute(x, PLANE, pairs)  8.32 us
    ppermute x7, starting transfers between devices, to_slot(): return lax.ppermute(x, PLANE, pairs)  8.11 us
    pallas_call x2, Pallas kernels, attend(): pl.pallas_call(functools.partial(attend_kernel, len(blocks), last), grid=...  6.67 us
    ppermute x12, waiting for transfers between devices, shift(): return lax.ppermute(x, axis, [(i, (i + by) % n) for i in range(n)])  6.21 us
    unnamed x8, local copies, waits for them, and re-layouts  2.72 us
  transfers between devices with their start and end apart: 23, of which 10 were waited for; matrix products, arithmetic and copies ran while one was open for 0% of the time, Pallas kernels for 7%

profile of v3, /device:TPU:1, one launch (start us, length us, event | category | flops | bytes accessed | tf_op | source)
XLA Modules:
  0.0 74.7 jit_solution(9293194275776786396)
XLA Ops:
  1.8 2.5 %collective-permute-start = (bf16[256,512]{1,0:T(8,128)(2,1)S(1)}, bf16[256,512]{1,0:T(8,128)(2,1)S(1)}, u32[]{:S(2)}, u32[]{:S(2)}) collective-permute-start(bf16[256,512]{1,0:T(8,128)(2,1)S(1)} %pack.2.refs_5_), channel_id=1, source_target_pairs={{0,32},{32,64},{64,96},{96,128},{128,160},{160,192},{192,224},{224... | collective-permute-start | bytes 786440 | tf_op jit(solution)/shard_map/ppermute | solution.py:26
  4.4 4.0 %collective-permute-start.1 = (bf16[256,512]{1,0:T(8,128)(2,1)S(1)}, bf16[256,512]{1,0:T(8,128)(2,1)S(1)}, u32[]{:S(2)}, u32[]{:S(2)}) collective-permute-start(bf16[256,512]{1,0:T(8,128)(2,1)S(1)} %pack.2.refs_5_), channel_id=1, source_target_pairs={{0,224},{32,0},{64,32},{96,64},{128,96},{160,128},{192,160},{224,1... | collective-permute-start | bytes 786440 | tf_op jit(solution)/shard_map/ppermute | solution.py:26
  8.4 1.2 %collective-permute-start.2 = (bf16[128,512]{1,0:T(8,128)(2,1)}, bf16[128,512]{1,0:T(8,128)(2,1)S(1)}, u32[]{:S(2)}, u32[]{:S(2)}) collective-permute-start(bf16[128,512]{1,0:T(8,128)(2,1)} %k.3), channel_id=1, source_target_pairs={{0,4},{4,0},{1,5},{5,1},{2,6},{6,2},{3,7},{7,3},{8,12},{12,8},{9,1... | collective-permute-start | bytes 393224 | tf_op jit(solution)/shard_map/ppermute | solution.py:36
  9.6 3.1 %collective-permute-done.2.v = bf16[128,512]{1,0:T(8,128)(2,1)S(1)} collective-permute-done((bf16[128,512]{1,0:T(8,128)(2,1)}, bf16[128,512]{1,0:T(8,128)(2,1)S(1)}, u32[]{:S(2)}, u32[]{:S(2)}) %collective-permute-start.2) | collective-permute-done | bytes 131104 | tf_op jit(solution)/shard_map/ppermute | solution.py:36
  14.3 1.3 %collective-permute-start.5 = (bf16[256,512]{1,0:T(8,128)(2,1)S(1)}, bf16[256,512]{1,0:T(8,128)(2,1)S(1)}, u32[]{:S(2)}, u32[]{:S(2)}) collective-permute-start(bf16[256,512]{1,0:T(8,128)(2,1)S(1)} %pack.3.refs_0_), channel_id=1, source_target_pairs={{0,8},{8,16},{16,24},{24,0},{1,9},{9,17},{17,25},{25,1},{2,10},{10... | collective-permute-start | bytes 786440 | tf_op jit(solution)/shard_map/ppermute | solution.py:26
  15.6 1.4 %collective-permute-start.6 = (bf16[256,512]{1,0:T(8,128)(2,1)S(1)}, bf16[256,512]{1,0:T(8,128)(2,1)S(1)}, u32[]{:S(2)}, u32[]{:S(2)}) collective-permute-start(bf16[256,512]{1,0:T(8,128)(2,1)S(1)} %pack.3.refs_0_), channel_id=1, source_target_pairs={{0,24},{8,0},{16,8},{24,16},{1,25},{9,1},{17,9},{25,17},{2,26},{10... | collective-permute-start | bytes 786440 | tf_op jit(solution)/shard_map/ppermute | solution.py:26
  17.1 2.7 %collective-permute-start.4 = (bf16[256,512]{1,0:T(8,128)(2,1)S(1)}, bf16[256,512]{1,0:T(8,128)(2,1)S(1)}, u32[]{:S(2)}, u32[]{:S(2)}) collective-permute-start(bf16[256,512]{1,0:T(8,128)(2,1)S(1)} %collective-permute-done.1.refs_7_), channel_id=1, source_target_pairs={{0,224},{32,0},{64,32},{96,64},{128,96},{160,128},{192,160},{224,1... | collective-permute-start | bytes 786440 | tf_op jit(solution)/shard_map/ppermute | solution.py:26
  19.8 2.5 %collective-permute-done.5.refs_3_ = bf16[256,512]{1,0:T(8,128)(2,1)S(1)} collective-permute-done((bf16[256,512]{1,0:T(8,128)(2,1)S(1)}, bf16[256,512]{1,0:T(8,128)(2,1)S(1)}, u32[]{:S(2)}, u32[]{:S(2)}) %collective-permute-start.5) | collective-permute-done | bytes 262176 | tf_op jit(solution)/shard_map/ppermute | solution.py:26
  22.3 2.1 %collective-permute-done.3.refs_8_ = bf16[256,512]{1,0:T(8,128)(2,1)S(1)} collective-permute-done((bf16[256,512]{1,0:T(8,128)(2,1)S(1)}, bf16[256,512]{1,0:T(8,128)(2,1)S(1)}, u32[]{:S(2)}, u32[]{:S(2)}) %collective-permute-start.3) | collective-permute-done | bytes 262176 | tf_op jit(solution)/shard_map/ppermute | solution.py:26
  25.4 1.7 %collective-permute-start.11 = (bf16[256,512]{1,0:T(8,128)(2,1)S(1)}, bf16[256,512]{1,0:T(8,128)(2,1)S(1)}, u32[]{:S(2)}, u32[]{:S(2)}) collective-permute-start(bf16[256,512]{1,0:T(8,128)(2,1)S(1)} %collective-permute-done.4.refs_9_), channel_id=1, source_target_pairs={{0,224},{32,0},{64,32},{96,64},{128,96},{160,128},{192,160},{224,1... | collective-permute-start | bytes 786440 | tf_op jit(solution)/shard_map/ppermute | solution.py:26
  27.2 2.7 %collective-permute-start.8 = (bf16[128,512]{1,0:T(8,128)(2,1)S(1)}, bf16[128,512]{1,0:T(8,128)(2,1)S(1)}, u32[]{:S(2)}, u32[]{:S(2)}) collective-permute-start(bf16[128,512]{1,0:T(8,128)(2,1)S(1)} %slice.13), channel_id=1, source_target_pairs={{0,24},{8,0},{16,8},{24,16},{1,25},{9,1},{17,9},{25,17},{2,26},{10... | collective-permute-start | bytes 393224 | tf_op jit(solution)/shard_map/ppermute | solution.py:26
  30.9 2.9 %collective-permute-start.12 = (bf16[128,512]{1,0:T(8,128)(2,1)S(1)}, bf16[128,512]{1,0:T(8,128)(2,1)S(1)}, u32[]{:S(2)}, u32[]{:S(2)}) collective-permute-start(bf16[128,512]{1,0:T(8,128)(2,1)S(1)} %slice.17), channel_id=1, source_target_pairs={{0,224},{32,0},{64,32},{96,64},{128,96},{160,128},{192,160},{224,1... | collective-permute-start | bytes 393224 | tf_op jit(solution)/shard_map/ppermute | solution.py:26
  33.9 5.3 %attend.2 = (f32[512,1024]{1,0:T(8,128)S(1)}, f32[4,2,1024]{2,1,0:T(2,128)S(1)}) custom-call(bf16[256,512]{1,0:T(8,128)(2,1)S(1)} %pack.3.refs_0_, bf16[128,512]{1,0:T(8,128)(2,1)S(1)} %collective-permute-done.7.refs_1_, bf16[128,512]{1,0:T(8,128)(2,1)S(1)} %collective-permute-done.8.refs_2_, bf16[256,512]{1,0:T(8,128)(2,1)S(1)} %collective-permute-done.5.refs_3_, ...), custom_call_target="tpu_custom_call" | custom-call | flops 5637144576 | bytes 4194304 | tf_op jit(solution)/shard_map/attend/pallas_call | solution.py:145
  39.2 1.4 %attend.3 = (bf16[528,128]{1,0:T(8,128)(2,1)S(1)}, bf16[528,128]{1,0:T(8,128)(2,1)S(1)}, bf16[528,128]{1,0:T(8,128)(2,1)S(1)}, bf16[528,128]{1,0:T(8,128)(2,1)S(...) custom-call(bf16[256,512]{1,0:T(8,128)(2,1)S(1)} %pack.3.refs_0_, ...), custom_call_target="tpu_custom_call" | custom-call | flops 805306368 | bytes 4194304 | tf_op jit(solution)/shard_map/attend/pallas_call | solution.py:145
  40.6 1.3 %collective-permute-start.13 = (bf16[528,128]{1,0:T(8,128)(2,1)S(1)}, bf16[528,128]{1,0:T(8,128)(2,1)S(1)}, u32[]{:S(2)}, u32[]{:S(2)}) collective-permute-start(bf16[528,128]{1,0:T(8,128)(2,1)S(1)} %get-tuple-element.36), channel_id=1, source_target_pairs={{0,4},{4,0},{8,12},{12,8},{16,20},{20,16},{24,28},{28,24},{1,5},{5... | collective-permute-start | bytes 405512 | tf_op jit(solution)/shard_map/ppermute | solution.py:32
  41.9 1.6 %collective-permute-start.14 = (bf16[528,128]{1,0:T(8,128)(2,1)S(1)}, bf16[528,128]{1,0:T(8,128)(2,1)S(1)}, u32[]{:S(2)}, u32[]{:S(2)}) collective-permute-start(bf16[528,128]{1,0:T(8,128)(2,1)S(1)} %get-tuple-element.37), channel_id=1, source_target_pairs={{0,16},{4,20},{8,24},{12,28},{16,0},{20,4},{24,8},{28,12},{1,17},{... | collective-permute-start | bytes 405512 | tf_op jit(solution)/shard_map/ppermute | solution.py:32
  43.5 1.3 %collective-permute-start.15 = (bf16[528,128]{1,0:T(8,128)(2,1)S(1)}, bf16[528,128]{1,0:T(8,128)(2,1)S(1)}, u32[]{:S(2)}, u32[]{:S(2)}) collective-permute-start(bf16[528,128]{1,0:T(8,128)(2,1)S(1)} %get-tuple-element.38), channel_id=1, source_target_pairs={{0,20},{4,16},{8,28},{12,24},{16,4},{20,0},{24,12},{28,8},{1,21},{... | collective-permute-start | bytes 405512 | tf_op jit(solution)/shard_map/ppermute | solution.py:32
  44.8 1.4 %collective-permute-start.16 = (bf16[528,128]{1,0:T(8,128)(2,1)S(1)}, bf16[528,128]{1,0:T(8,128)(2,1)S(1)}, u32[]{:S(2)}, u32[]{:S(2)}) collective-permute-start(bf16[528,128]{1,0:T(8,128)(2,1)S(1)} %get-tuple-element.39), channel_id=1, source_target_pairs={{0,24},{4,28},{8,0},{12,4},{16,8},{20,12},{24,16},{28,20},{1,25},{... | collective-permute-start | bytes 405512 | tf_op jit(solution)/shard_map/ppermute | solution.py:32
  46.2 1.4 %collective-permute-start.17 = (bf16[528,128]{1,0:T(8,128)(2,1)S(1)}, bf16[528,128]{1,0:T(8,128)(2,1)S(1)}, u32[]{:S(2)}, u32[]{:S(2)}) collective-permute-start(bf16[528,128]{1,0:T(8,128)(2,1)S(1)} %get-tuple-element.40), channel_id=1, source_target_pairs={{0,28},{4,24},{8,4},{12,0},{16,12},{20,8},{24,20},{28,16},{1,29},{... | collective-permute-start | bytes 405512 | tf_op jit(solution)/shard_map/ppermute | solution.py:32
  48.7 1.5 %collective-permute-done.15.refs_3_ = bf16[528,128]{1,0:T(8,128)(2,1)S(1)} collective-permute-done((bf16[528,128]{1,0:T(8,128)(2,1)S(1)}, bf16[528,128]{1,0:T(8,128)(2,1)S(1)}, u32[]{:S(2)}, u32[]{:S(2)}) %collective-permute-start.15) | collective-permute-done | bytes 135200 | tf_op jit(solution)/shard_map/ppermute | solution.py:32
  51.3 5.7 %collective-permute-done.18.refs_6_ = bf16[528,128]{1,0:T(8,128)(2,1)S(1)} collective-permute-done((bf16[528,128]{1,0:T(8,128)(2,1)S(1)}, bf16[528,128]{1,0:T(8,128)(2,1)S(1)}, u32[]{:S(2)}, u32[]{:S(2)}) %collective-permute-start.18) | collective-permute-done | bytes 135200 | tf_op jit(solution)/shard_map/ppermute | solution.py:32
  58.0 5.5 %collective-permute-start.21 = (bf16[32,4096]{1,0:T(8,128)(2,1)S(1)}, bf16[32,4096]{1,0:T(8,128)(2,1)S(1)}, u32[]{:S(2)}, u32[]{:S(2)}) collective-permute-start(bf16[32,4096]{1,0:T(8,128)(2,1)S(1)} %get-tuple-element.46), channel_id=1, source_target_pairs={{0,1},{1,0},{2,3},{3,2},{4,5},{5,4},{6,7},{7,6},{8,9},{9,8},{10,11... | collective-permute-start | bytes 786440 | tf_op jit(solution)/shard_map/ppermute | solution.py:36
  64.8 2.5 %collective-permute-start.22 = (bf16[32,4096]{1,0:T(8,128)(2,1)S(1)}, bf16[32,4096]{1,0:T(8,128)(2,1)S(1)}, u32[]{:S(2)}, u32[]{:S(2)}) collective-permute-start(bf16[32,4096]{1,0:T(8,128)(2,1)S(1)} %add_convert_fusion), channel_id=1, source_target_pairs={{0,2},{2,0},{1,3},{3,1},{4,6},{6,4},{5,7},{7,5},{8,10},{10,8},{9,1... | collective-permute-start | bytes 786440 | tf_op jit(solution)/shard_map/ppermute | solution.py:36
  67.3 6.6 %collective-permute-done.22 = bf16[32,4096]{1,0:T(8,128)(2,1)S(1)} collective-permute-done((bf16[32,4096]{1,0:T(8,128)(2,1)S(1)}, bf16[32,4096]{1,0:T(8,128)(2,1)S(1)}, u32[]{:S(2)}, u32[]{:S(2)}) %collective-permute-start.22) | collective-permute-done | bytes 262176 | tf_op jit(solution)/shard_map/ppermute | solution.py:36
  (41 shorter events, 10.8 us)
Async XLA Ops:
  1.8 12.5 %collective-permute-start = (bf16[256,512]{1,0:T(8,128)(2,1)S(1)}, bf16[256,512]{1,0:T(8,128)(2,1)S(1)}, u32[]{:S(2)}, u32[]{:S(2)}) collective-permute-start(bf16[256,512]{1,0:T(8,128)(2,1)S(1)} %pack.2.refs_5_), channel_id=1, source_target_pairs={{0,32},{32,64},{64,96},{96,128},{128,160},{160,192},{192,224},{224... | collective-permute-start | bytes 786440 | tf_op jit(solution)/shard_map/ppermute | solution.py:26
  4.4 10.0 %collective-permute-start.1 = (bf16[256,512]{1,0:T(8,128)(2,1)S(1)}, bf16[256,512]{1,0:T(8,128)(2,1)S(1)}, u32[]{:S(2)}, u32[]{:S(2)}) collective-permute-start(bf16[256,512]{1,0:T(8,128)(2,1)S(1)} %pack.2.refs_5_), channel_id=1, source_target_pairs={{0,224},{32,0},{64,32},{96,64},{128,96},{160,128},{192,160},{224,1... | collective-permute-start | bytes 786440 | tf_op jit(solution)/shard_map/ppermute | solution.py:26
  8.4 4.3 %collective-permute-start.2 = (bf16[128,512]{1,0:T(8,128)(2,1)}, bf16[128,512]{1,0:T(8,128)(2,1)S(1)}, u32[]{:S(2)}, u32[]{:S(2)}) collective-permute-start(bf16[128,512]{1,0:T(8,128)(2,1)} %k.3), channel_id=1, source_target_pairs={{0,4},{4,0},{1,5},{5,1},{2,6},{6,2},{3,7},{7,3},{8,12},{12,8},{9,1... | collective-permute-start | bytes 393224 | tf_op jit(solution)/shard_map/ppermute | solution.py:36
  14.3 7.9 %collective-permute-start.5 = (bf16[256,512]{1,0:T(8,128)(2,1)S(1)}, bf16[256,512]{1,0:T(8,128)(2,1)S(1)}, u32[]{:S(2)}, u32[]{:S(2)}) collective-permute-start(bf16[256,512]{1,0:T(8,128)(2,1)S(1)} %pack.3.refs_0_), channel_id=1, source_target_pairs={{0,8},{8,16},{16,24},{24,0},{1,9},{9,17},{17,25},{25,1},{2,10},{10... | collective-permute-start | bytes 786440 | tf_op jit(solution)/shard_map/ppermute | solution.py:26
  15.6 6.6 %collective-permute-start.6 = (bf16[256,512]{1,0:T(8,128)(2,1)S(1)}, bf16[256,512]{1,0:T(8,128)(2,1)S(1)}, u32[]{:S(2)}, u32[]{:S(2)}) collective-permute-start(bf16[256,512]{1,0:T(8,128)(2,1)S(1)} %pack.3.refs_0_), channel_id=1, source_target_pairs={{0,24},{8,0},{16,8},{24,16},{1,25},{9,1},{17,9},{25,17},{2,26},{10... | collective-permute-start | bytes 786440 | tf_op jit(solution)/shard_map/ppermute | solution.py:26
  17.1 7.3 %collective-permute-start.3 = (bf16[256,512]{1,0:T(8,128)(2,1)S(1)}, bf16[256,512]{1,0:T(8,128)(2,1)S(1)}, u32[]{:S(2)}, u32[]{:S(2)}) collective-permute-start(bf16[256,512]{1,0:T(8,128)(2,1)S(1)} %collective-permute-done.refs_6_), channel_id=1, source_target_pairs={{0,32},{32,64},{64,96},{96,128},{128,160},{160,192},{192,224},{224... | collective-permute-start | bytes 786440 | tf_op jit(solution)/shard_map/ppermute | solution.py:26
  17.1 7.3 %collective-permute-start.4 = (bf16[256,512]{1,0:T(8,128)(2,1)S(1)}, bf16[256,512]{1,0:T(8,128)(2,1)S(1)}, u32[]{:S(2)}, u32[]{:S(2)}) collective-permute-start(bf16[256,512]{1,0:T(8,128)(2,1)S(1)} %collective-permute-done.1.refs_7_), channel_id=1, source_target_pairs={{0,224},{32,0},{64,32},{96,64},{128,96},{160,128},{192,160},{224,1... | collective-permute-start | bytes 786440 | tf_op jit(solution)/shard_map/ppermute | solution.py:26
  24.4 6.4 %collective-permute-start.9 = (bf16[256,512]{1,0:T(8,128)(2,1)S(1)}, bf16[256,512]{1,0:T(8,128)(2,1)S(1)}, u32[]{:S(2)}, u32[]{:S(2)}) collective-permute-start(bf16[256,512]{1,0:T(8,128)(2,1)S(1)} %collective-permute-done.3.refs_8_), channel_id=1, source_target_pairs={{0,32},{32,64},{64,96},{96,128},{128,160},{160,192},{192,224},{224... | collective-permute-start | bytes 786440 | tf_op jit(solution)/shard_map/ppermute | solution.py:26
  25.4 5.6 %collective-permute-start.11 = (bf16[256,512]{1,0:T(8,128)(2,1)S(1)}, bf16[256,512]{1,0:T(8,128)(2,1)S(1)}, u32[]{:S(2)}, u32[]{:S(2)}) collective-permute-start(bf16[256,512]{1,0:T(8,128)(2,1)S(1)} %collective-permute-done.4.refs_9_), channel_id=1, source_target_pairs={{0,224},{32,0},{64,32},{96,64},{128,96},{160,128},{192,160},{224,1... | collective-permute-start | bytes 786440 | tf_op jit(solution)/shard_map/ppermute | solution.py:26
  27.1 6.8 %collective-permute-start.7 = (bf16[128,512]{1,0:T(8,128)(2,1)S(1)}, bf16[128,512]{1,0:T(8,128)(2,1)S(1)}, u32[]{:S(2)}, u32[]{:S(2)}) collective-permute-start(bf16[128,512]{1,0:T(8,128)(2,1)S(1)} %slice.12), channel_id=1, source_target_pairs={{0,8},{8,16},{16,24},{24,0},{1,9},{9,17},{17,25},{25,1},{2,10},{10... | collective-permute-start | bytes 393224 | tf_op jit(solution)/shard_map/ppermute | solution.py:26
  27.2 6.7 %collective-permute-start.8 = (bf16[128,512]{1,0:T(8,128)(2,1)S(1)}, bf16[128,512]{1,0:T(8,128)(2,1)S(1)}, u32[]{:S(2)}, u32[]{:S(2)}) collective-permute-start(bf16[128,512]{1,0:T(8,128)(2,1)S(1)} %slice.13), channel_id=1, source_target_pairs={{0,24},{8,0},{16,8},{24,16},{1,25},{9,1},{17,9},{25,17},{2,26},{10... | collective-permute-start | bytes 393224 | tf_op jit(solution)/shard_map/ppermute | solution.py:26
  30.8 8.3 %collective-permute-start.10 = (bf16[128,512]{1,0:T(8,128)(2,1)S(1)}, bf16[128,512]{1,0:T(8,128)(2,1)S(1)}, u32[]{:S(2)}, u32[]{:S(2)}) collective-permute-start(bf16[128,512]{1,0:T(8,128)(2,1)S(1)} %slice.16), channel_id=1, source_target_pairs={{0,32},{32,64},{64,96},{96,128},{128,160},{160,192},{192,224},{224... | collective-permute-start | bytes 393224 | tf_op jit(solution)/shard_map/ppermute | solution.py:26
  30.9 8.2 %collective-permute-start.12 = (bf16[128,512]{1,0:T(8,128)(2,1)S(1)}, bf16[128,512]{1,0:T(8,128)(2,1)S(1)}, u32[]{:S(2)}, u32[]{:S(2)}) collective-permute-start(bf16[128,512]{1,0:T(8,128)(2,1)S(1)} %slice.17), channel_id=1, source_target_pairs={{0,224},{32,0},{64,32},{96,64},{128,96},{160,128},{192,160},{224,1... | collective-permute-start | bytes 393224 | tf_op jit(solution)/shard_map/ppermute | solution.py:26
  33.9 23.2 %copy-start = (bf16[512,4096]{1,0:T(8,128)(2,1)S(1)}, bf16[512,4096]{1,0:T(8,128)(2,1)}, u32[]{:S(2)}) copy-start(bf16[512,4096]{1,0:T(8,128)(2,1)} %refs_8_.1) | copy-start | bytes 12582916
  40.6 7.1 %collective-permute-start.13 = (bf16[528,128]{1,0:T(8,128)(2,1)S(1)}, bf16[528,128]{1,0:T(8,128)(2,1)S(1)}, u32[]{:S(2)}, u32[]{:S(2)}) collective-permute-start(bf16[528,128]{1,0:T(8,128)(2,1)S(1)} %get-tuple-element.36), channel_id=1, source_target_pairs={{0,4},{4,0},{8,12},{12,8},{16,20},{20,16},{24,28},{28,24},{1,5},{5... | collective-permute-start | bytes 405512 | tf_op jit(solution)/shard_map/ppermute | solution.py:32
  41.9 6.8 %collective-permute-start.14 = (bf16[528,128]{1,0:T(8,128)(2,1)S(1)}, bf16[528,128]{1,0:T(8,128)(2,1)S(1)}, u32[]{:S(2)}, u32[]{:S(2)}) collective-permute-start(bf16[528,128]{1,0:T(8,128)(2,1)S(1)} %get-tuple-element.37), channel_id=1, source_target_pairs={{0,16},{4,20},{8,24},{12,28},{16,0},{20,4},{24,8},{28,12},{1,17},{... | collective-permute-start | bytes 405512 | tf_op jit(solution)/shard_map/ppermute | solution.py:32
  43.5 6.8 %collective-permute-start.15 = (bf16[528,128]{1,0:T(8,128)(2,1)S(1)}, bf16[528,128]{1,0:T(8,128)(2,1)S(1)}, u32[]{:S(2)}, u32[]{:S(2)}) collective-permute-start(bf16[528,128]{1,0:T(8,128)(2,1)S(1)} %get-tuple-element.38), channel_id=1, source_target_pairs={{0,20},{4,16},{8,28},{12,24},{16,4},{20,0},{24,12},{28,8},{1,21},{... | collective-permute-start | bytes 405512 | tf_op jit(solution)/shard_map/ppermute | solution.py:32
  44.8 5.4 %collective-permute-start.16 = (bf16[528,128]{1,0:T(8,128)(2,1)S(1)}, bf16[528,128]{1,0:T(8,128)(2,1)S(1)}, u32[]{:S(2)}, u32[]{:S(2)}) collective-permute-start(bf16[528,128]{1,0:T(8,128)(2,1)S(1)} %get-tuple-element.39), channel_id=1, source_target_pairs={{0,24},{4,28},{8,0},{12,4},{16,8},{20,12},{24,16},{28,20},{1,25},{... | collective-permute-start | bytes 405512 | tf_op jit(solution)/shard_map/ppermute | solution.py:32
  46.2 5.1 %collective-permute-start.17 = (bf16[528,128]{1,0:T(8,128)(2,1)S(1)}, bf16[528,128]{1,0:T(8,128)(2,1)S(1)}, u32[]{:S(2)}, u32[]{:S(2)}) collective-permute-start(bf16[528,128]{1,0:T(8,128)(2,1)S(1)} %get-tuple-element.40), channel_id=1, source_target_pairs={{0,28},{4,24},{8,4},{12,0},{16,12},{20,8},{24,20},{28,16},{1,29},{... | collective-permute-start | bytes 405512 | tf_op jit(solution)/shard_map/ppermute | solution.py:32
  47.6 9.4 %collective-permute-start.18 = (bf16[528,128]{1,0:T(8,128)(2,1)S(1)}, bf16[528,128]{1,0:T(8,128)(2,1)S(1)}, u32[]{:S(2)}, u32[]{:S(2)}) collective-permute-start(bf16[528,128]{1,0:T(8,128)(2,1)S(1)} %get-tuple-element.41), channel_id=1, source_target_pairs={{0,8},{4,12},{8,16},{12,20},{16,24},{20,28},{24,0},{28,4},{1,9},{5... | collective-permute-start | bytes 405512 | tf_op jit(solution)/shard_map/ppermute | solution.py:32
  48.6 8.4 %collective-permute-start.19 = (bf16[528,128]{1,0:T(8,128)(2,1)S(1)}, bf16[528,128]{1,0:T(8,128)(2,1)S(1)}, u32[]{:S(2)}, u32[]{:S(2)}) collective-permute-start(bf16[528,128]{1,0:T(8,128)(2,1)S(1)} %get-tuple-element.42), channel_id=1, source_target_pairs={{0,12},{4,8},{8,20},{12,16},{16,28},{20,24},{24,4},{28,0},{1,13},{... | collective-permute-start | bytes 405512 | tf_op jit(solution)/shard_map/ppermute | solution.py:32
  58.0 6.7 %collective-permute-start.21 = (bf16[32,4096]{1,0:T(8,128)(2,1)S(1)}, bf16[32,4096]{1,0:T(8,128)(2,1)S(1)}, u32[]{:S(2)}, u32[]{:S(2)}) collective-permute-start(bf16[32,4096]{1,0:T(8,128)(2,1)S(1)} %get-tuple-element.46), channel_id=1, source_target_pairs={{0,1},{1,0},{2,3},{3,2},{4,5},{5,4},{6,7},{7,6},{8,9},{9,8},{10,11... | collective-permute-start | bytes 786440 | tf_op jit(solution)/shard_map/ppermute | solution.py:36
  63.5 3.7 %collective-permute-start.20 = (bf16[32,4096]{1,0:T(8,128)(2,1)S(1)}, bf16[32,4096]{1,0:T(8,128)(2,1)S(1)}, u32[]{:S(2)}, u32[]{:S(2)}) collective-permute-start(bf16[32,4096]{1,0:T(8,128)(2,1)S(1)} %get-tuple-element.44), channel_id=1, source_target_pairs={{0,1},{1,0},{2,3},{3,2},{4,5},{5,4},{6,7},{7,6},{8,9},{9,8},{10,11... | collective-permute-start | bytes 786440 | tf_op jit(solution)/shard_map/ppermute | solution.py:36
  64.8 9.1 %collective-permute-start.22 = (bf16[32,4096]{1,0:T(8,128)(2,1)S(1)}, bf16[32,4096]{1,0:T(8,128)(2,1)S(1)}, u32[]{:S(2)}, u32[]{:S(2)}) collective-permute-start(bf16[32,4096]{1,0:T(8,128)(2,1)S(1)} %add_convert_fusion), channel_id=1, source_target_pairs={{0,2},{2,0},{1,3},{3,1},{4,6},{6,4},{5,7},{7,5},{8,10},{10,8},{9,1... | collective-permute-start | bytes 786440 | tf_op jit(solution)/shard_map/ppermute | solution.py:36
  (3 other events, 2.7 us)

commit v4 on v3

--- a/solution.py
+++ b/solution.py
@@ -219,7 +219,6 @@
     above, below = shift(pair, "y", 1), shift(pair, "y", -1)
     up, down = shift(up, "z", 1), shift(down, "z", -1)
     blocks += [up, down]
-    up, down, above, below = lax.optimization_barrier((up, down, above, below))
     up, down = shift(up, "z", 1), shift(down, "z", -1)
     blocks += [up, down]
     far = (shift(up[:TOK], "z", 1), shift(down[TOK:], "z", -1))
@@ -229,7 +228,7 @@
     parts = list(parts)
     for r in FIRST_OUT:
         parts[r] = to_slot(parts[r], SLOTS[r])
-    send_other, send_own, keep_other, keep_own = project(parts, out_weight)
+    send_other, send_own, keep_other, keep_own = project([parts[r] for r in FIRST_OUT] + parts[:1], out_weight)
     other = keep_other + flip(send_other, "c").astype(jnp.float32)
     arrived = flip(other.astype(jnp.bfloat16), "xh").astype(jnp.float32)
     return keep_own + flip(send_own, "c").astype(jnp.float32) + arrived

time: 74.9 us -> 72.9 us (0.973)
  waiting for transfers between devices: 25.3 us -> 18.9 us
  starting transfers between devices: 37.9 us -> 42.3 us
    ppermute x12, waiting for transfers between devices: 6.21 us -> 2.46 us  [shift(): return lax.ppermute(x, axis, [(i, (i + by) % n) for i in range(n)])]
    ppermute x7, waiting for transfers between devices: 8.32 us -> 5.7 us  [to_slot(): return lax.ppermute(x, PLANE, pairs)]
    ppermute x7, starting transfers between devices: 8.11 us -> 10.7 us  [to_slot(): return lax.ppermute(x, PLANE, pairs)]
    ppermute x12, starting transfers between devices: 20.5 us -> 21.5 us  [shift(): return lax.ppermute(x, axis, [(i, (i + by) % n) for i in range(n)])]
    ppermute x4, starting transfers between devices: 9.35 us -> 10.2 us  [flip(): return lax.ppermute(x, axis, [(0, 1), (1, 0)])]
  transfers between devices with their start and end apart: 23 -> 23, of which waited for: 10 -> 9; matrix products, arithmetic and copies ran while one was open for 0% -> 0% of each run, Pallas kernels for 7% -> 7%
where the time goes in v4:
time: 72.9 us; the launch traced here: 72.8 us
  starting transfers between devices  42.3 us (58%)
  waiting for transfers between devices  18.9 us (26%)
  Pallas kernels  7.7 us (11%)
  local copies, waits for them, and re-layouts  2.76 us (4%)
  other arithmetic  0.93 us (1%)
    ppermute x12, starting transfers between devices, shift(): return lax.ppermute(x, axis, [(i, (i + by) % n) for i in range(n)])  21.5 us
    ppermute x4, waiting for transfers between devices, flip(): return lax.ppermute(x, axis, [(0, 1), (1, 0)])  10.7 us
    ppermute x7, starting transfers between devices, to_slot(): return lax.ppermute(x, PLANE, pairs)  10.7 us
    ppermute x4, starting transfers between devices, flip(): return lax.ppermute(x, axis, [(0, 1), (1, 0)])  10.2 us
    pallas_call x2, Pallas kernels, attend(): pl.pallas_call(functools.partial(attend_kernel, len(blocks), last), grid=...  6.69 us
    ppermute x7, waiting for transfers between devices, to_slot(): return lax.ppermute(x, PLANE, pairs)  5.7 us
    unnamed x8, local copies, waits for them, and re-layouts  2.72 us
    ppermute x12, waiting for transfers between devices, shift(): return lax.ppermute(x, axis, [(i, (i + by) % n) for i in range(n)])  2.46 us
  transfers between devices with their start and end apart: 23, of which 9 were waited for; matrix products, arithmetic and copies ran while one was open for 0% of the time, Pallas kernels for 7%

profile of v4, /device:TPU:1, one launch (start us, length us, event | category | flops | bytes accessed | tf_op | source)
XLA Modules:
  0.0 72.8 jit_solution(7568060400336204092)
XLA Ops:
  1.8 2.5 %collective-permute-start = (bf16[256,512]{1,0:T(8,128)(2,1)S(1)}, bf16[256,512]{1,0:T(8,128)(2,1)S(1)}, u32[]{:S(2)}, u32[]{:S(2)}) collective-permute-start(bf16[256,512]{1,0:T(8,128)(2,1)S(1)} %pack.2.refs_5_), channel_id=1, source_target_pairs={{0,32},{32,64},{64,96},{96,128},{128,160},{160,192},{192,224},{224... | collective-permute-start | bytes 786440 | tf_op jit(solution)/shard_map/ppermute | solution.py:26
  4.4 4.0 %collective-permute-start.1 = (bf16[256,512]{1,0:T(8,128)(2,1)S(1)}, bf16[256,512]{1,0:T(8,128)(2,1)S(1)}, u32[]{:S(2)}, u32[]{:S(2)}) collective-permute-start(bf16[256,512]{1,0:T(8,128)(2,1)S(1)} %pack.2.refs_5_), channel_id=1, source_target_pairs={{0,224},{32,0},{64,32},{96,64},{128,96},{160,128},{192,160},{224,1... | collective-permute-start | bytes 786440 | tf_op jit(solution)/shard_map/ppermute | solution.py:26
  8.4 1.2 %collective-permute-start.2 = (bf16[128,512]{1,0:T(8,128)(2,1)}, bf16[128,512]{1,0:T(8,128)(2,1)S(1)}, u32[]{:S(2)}, u32[]{:S(2)}) collective-permute-start(bf16[128,512]{1,0:T(8,128)(2,1)} %k.3), channel_id=1, source_target_pairs={{0,4},{4,0},{1,5},{5,1},{2,6},{6,2},{3,7},{7,3},{8,12},{12,8},{9,1... | collective-permute-start | bytes 393224 | tf_op jit(solution)/shard_map/ppermute | solution.py:36
  9.6 3.1 %collective-permute-done.2.v = bf16[128,512]{1,0:T(8,128)(2,1)S(1)} collective-permute-done((bf16[128,512]{1,0:T(8,128)(2,1)}, bf16[128,512]{1,0:T(8,128)(2,1)S(1)}, u32[]{:S(2)}, u32[]{:S(2)}) %collective-permute-start.2) | collective-permute-done | bytes 131104 | tf_op jit(solution)/shard_map/ppermute | solution.py:36
  14.3 2.4 %collective-permute-start.10 = (bf16[256,512]{1,0:T(8,128)(2,1)S(1)}, bf16[256,512]{1,0:T(8,128)(2,1)S(1)}, u32[]{:S(2)}, u32[]{:S(2)}) collective-permute-start(bf16[256,512]{1,0:T(8,128)(2,1)S(1)} %collective-permute-done.1.refs_7_), channel_id=1, source_target_pairs={{0,224},{32,0},{64,32},{96,64},{128,96},{160,128},{192,160},{224,1... | collective-permute-start | bytes 786440 | tf_op jit(solution)/shard_map/ppermute | solution.py:26
  16.8 1.3 %collective-permute-start.3 = (bf16[256,512]{1,0:T(8,128)(2,1)S(1)}, bf16[256,512]{1,0:T(8,128)(2,1)S(1)}, u32[]{:S(2)}, u32[]{:S(2)}) collective-permute-start(bf16[256,512]{1,0:T(8,128)(2,1)S(1)} %pack.3.refs_0_), channel_id=1, source_target_pairs={{0,8},{8,16},{16,24},{24,0},{1,9},{9,17},{17,25},{25,1},{2,10},{10... | collective-permute-start | bytes 786440 | tf_op jit(solution)/shard_map/ppermute | solution.py:26
  18.1 1.4 %collective-permute-start.5 = (bf16[256,512]{1,0:T(8,128)(2,1)S(1)}, bf16[256,512]{1,0:T(8,128)(2,1)S(1)}, u32[]{:S(2)}, u32[]{:S(2)}) collective-permute-start(bf16[256,512]{1,0:T(8,128)(2,1)S(1)} %pack.3.refs_0_), channel_id=1, source_target_pairs={{0,24},{8,0},{16,8},{24,16},{1,25},{9,1},{17,9},{25,17},{2,26},{10... | collective-permute-start | bytes 786440 | tf_op jit(solution)/shard_map/ppermute | solution.py:26
  19.5 1.4 %collective-permute-done.10.refs_9_ = bf16[256,512]{1,0:T(8,128)(2,1)S(1)} collective-permute-done((bf16[256,512]{1,0:T(8,128)(2,1)S(1)}, bf16[256,512]{1,0:T(8,128)(2,1)S(1)}, u32[]{:S(2)}, u32[]{:S(2)}) %collective-permute-start.10) | collective-permute-done | bytes 262176 | tf_op jit(solution)/shard_map/ppermute | solution.py:26
  20.9 3.3 %collective-permute-start.11 = (bf16[256,512]{1,0:T(8,128)(2,1)S(1)}, bf16[256,512]{1,0:T(8,128)(2,1)S(1)}, u32[]{:S(2)}, u32[]{:S(2)}) collective-permute-start(bf16[256,512]{1,0:T(8,128)(2,1)S(1)} %collective-permute-done.10.refs_9_), channel_id=1, source_target_pairs={{0,224},{32,0},{64,32},{96,64},{128,96},{160,128},{192,160},{224,1... | collective-permute-start | bytes 786440 | tf_op jit(solution)/shard_map/ppermute | solution.py:26
  24.3 1.4 %collective-permute-start.4 = (bf16[128,512]{1,0:T(8,128)(2,1)S(1)}, bf16[128,512]{1,0:T(8,128)(2,1)S(1)}, u32[]{:S(2)}, u32[]{:S(2)}) collective-permute-start(bf16[128,512]{1,0:T(8,128)(2,1)S(1)} %slice.16), channel_id=1, source_target_pairs={{0,8},{8,16},{16,24},{24,0},{1,9},{9,17},{17,25},{25,1},{2,10},{10... | collective-permute-start | bytes 393224 | tf_op jit(solution)/shard_map/ppermute | solution.py:26
  25.7 1.5 %collective-permute-start.6 = (bf16[128,512]{1,0:T(8,128)(2,1)S(1)}, bf16[128,512]{1,0:T(8,128)(2,1)S(1)}, u32[]{:S(2)}, u32[]{:S(2)}) collective-permute-start(bf16[128,512]{1,0:T(8,128)(2,1)S(1)} %slice.17), channel_id=1, source_target_pairs={{0,24},{8,0},{16,8},{24,16},{1,25},{9,1},{17,9},{25,17},{2,26},{10... | collective-permute-start | bytes 393224 | tf_op jit(solution)/shard_map/ppermute | solution.py:26
  27.6 3.2 %collective-permute-start.12 = (bf16[128,512]{1,0:T(8,128)(2,1)S(1)}, bf16[128,512]{1,0:T(8,128)(2,1)S(1)}, u32[]{:S(2)}, u32[]{:S(2)}) collective-permute-start(bf16[128,512]{1,0:T(8,128)(2,1)S(1)} %slice.19), channel_id=1, source_target_pairs={{0,224},{32,0},{64,32},{96,64},{128,96},{160,128},{192,160},{224,1... | collective-permute-start | bytes 393224 | tf_op jit(solution)/shard_map/ppermute | solution.py:26
  31.1 5.3 %attend.2 = (f32[512,1024]{1,0:T(8,128)S(1)}, f32[4,2,1024]{2,1,0:T(2,128)S(1)}) custom-call(bf16[256,512]{1,0:T(8,128)(2,1)S(1)} %pack.3.refs_0_, bf16[128,512]{1,0:T(8,128)(2,1)S(1)} %collective-permute-done.4.refs_1_, bf16[128,512]{1,0:T(8,128)(2,1)S(1)} %collective-permute-done.6.refs_2_, bf16[256,512]{1,0:T(8,128)(2,1)S(1)} %collective-permute-done.3.refs_3_, ...), custom_call_target="tpu_custom_call" | custom-call | flops 5637144576 | bytes 4194304 | tf_op jit(solution)/shard_map/attend/pallas_call | solution.py:145
  36.4 1.4 %attend.3 = (bf16[528,128]{1,0:T(8,128)(2,1)S(1)}, bf16[528,128]{1,0:T(8,128)(2,1)S(1)}, bf16[528,128]{1,0:T(8,128)(2,1)S(1)}, bf16[528,128]{1,0:T(8,128)(2,1)S(...) custom-call(bf16[256,512]{1,0:T(8,128)(2,1)S(1)} %pack.3.refs_0_, ...), custom_call_target="tpu_custom_call" | custom-call | flops 805306368 | bytes 4194304 | tf_op jit(solution)/shard_map/attend/pallas_call | solution.py:145
  37.8 3.0 %collective-permute-start.13 = (bf16[528,128]{1,0:T(8,128)(2,1)S(1)}, bf16[528,128]{1,0:T(8,128)(2,1)S(1)}, u32[]{:S(2)}, u32[]{:S(2)}) collective-permute-start(bf16[528,128]{1,0:T(8,128)(2,1)S(1)} %get-tuple-element.27), channel_id=1, source_target_pairs={{0,16},{4,20},{8,24},{12,28},{16,0},{20,4},{24,8},{28,12},{1,17},{... | collective-permute-start | bytes 405512 | tf_op jit(solution)/shard_map/ppermute | solution.py:32
  41.9 2.7 %collective-permute-start.15 = (bf16[528,128]{1,0:T(8,128)(2,1)S(1)}, bf16[528,128]{1,0:T(8,128)(2,1)S(1)}, u32[]{:S(2)}, u32[]{:S(2)}) collective-permute-start(bf16[528,128]{1,0:T(8,128)(2,1)S(1)} %get-tuple-element.29), channel_id=1, source_target_pairs={{0,28},{4,24},{8,4},{12,0},{16,12},{20,8},{24,20},{28,16},{1,29},{... | collective-permute-start | bytes 405512 | tf_op jit(solution)/shard_map/ppermute | solution.py:32
  44.5 3.6 %collective-permute-start.17 = (bf16[528,128]{1,0:T(8,128)(2,1)S(1)}, bf16[528,128]{1,0:T(8,128)(2,1)S(1)}, u32[]{:S(2)}, u32[]{:S(2)}) collective-permute-start(bf16[528,128]{1,0:T(8,128)(2,1)S(1)} %get-tuple-element.31), channel_id=1, source_target_pairs={{0,24},{4,28},{8,0},{12,4},{16,8},{20,12},{24,16},{28,20},{1,25},{... | collective-permute-start | bytes 405512 | tf_op jit(solution)/shard_map/ppermute | solution.py:32
  48.5 2.0 %collective-permute-done.16.refs_3_ = bf16[528,128]{1,0:T(8,128)(2,1)S(1)} collective-permute-done((bf16[528,128]{1,0:T(8,128)(2,1)S(1)}, bf16[528,128]{1,0:T(8,128)(2,1)S(1)}, u32[]{:S(2)}, u32[]{:S(2)}) %collective-permute-start.16) | collective-permute-done | bytes 135200 | tf_op jit(solution)/shard_map/ppermute | solution.py:32
  50.5 1.4 %collective-permute-done.17.refs_4_ = bf16[528,128]{1,0:T(8,128)(2,1)S(1)} collective-permute-done((bf16[528,128]{1,0:T(8,128)(2,1)S(1)}, bf16[528,128]{1,0:T(8,128)(2,1)S(1)}, u32[]{:S(2)}, u32[]{:S(2)}) %collective-permute-start.17) | collective-permute-done | bytes 135200 | tf_op jit(solution)/shard_map/ppermute | solution.py:32
  51.9 2.3 %collective-permute-done.18.refs_5_ = bf16[528,128]{1,0:T(8,128)(2,1)S(1)} collective-permute-done((bf16[528,128]{1,0:T(8,128)(2,1)S(1)}, bf16[528,128]{1,0:T(8,128)(2,1)S(1)}, u32[]{:S(2)}, u32[]{:S(2)}) %collective-permute-start.18) | collective-permute-done | bytes 135200 | tf_op jit(solution)/shard_map/ppermute | solution.py:32
  55.2 6.4 %collective-permute-start.21 = (bf16[32,4096]{1,0:T(8,128)(2,1)S(1)}, bf16[32,4096]{1,0:T(8,128)(2,1)S(1)}, u32[]{:S(2)}, u32[]{:S(2)}) collective-permute-start(bf16[32,4096]{1,0:T(8,128)(2,1)S(1)} %get-tuple-element.38), channel_id=1, source_target_pairs={{0,1},{1,0},{2,3},{3,2},{4,5},{5,4},{6,7},{7,6},{8,9},{9,8},{10,11... | collective-permute-start | bytes 786440 | tf_op jit(solution)/shard_map/ppermute | solution.py:36
  61.7 1.1 %collective-permute-done.21 = bf16[32,4096]{1,0:T(8,128)(2,1)S(1)} collective-permute-done((bf16[32,4096]{1,0:T(8,128)(2,1)S(1)}, bf16[32,4096]{1,0:T(8,128)(2,1)S(1)}, u32[]{:S(2)}, u32[]{:S(2)}) %collective-permute-start.21) | collective-permute-done | bytes 262176 | tf_op jit(solution)/shard_map/ppermute | solution.py:36
  62.8 2.5 %collective-permute-start.22 = (bf16[32,4096]{1,0:T(8,128)(2,1)S(1)}, bf16[32,4096]{1,0:T(8,128)(2,1)S(1)}, u32[]{:S(2)}, u32[]{:S(2)}) collective-permute-start(bf16[32,4096]{1,0:T(8,128)(2,1)S(1)} %add_convert_fusion), channel_id=1, source_target_pairs={{0,2},{2,0},{1,3},{3,1},{4,6},{6,4},{5,7},{7,5},{8,10},{10,8},{9,1... | collective-permute-start | bytes 786440 | tf_op jit(solution)/shard_map/ppermute | solution.py:36
  65.3 6.6 %collective-permute-done.22 = bf16[32,4096]{1,0:T(8,128)(2,1)S(1)} collective-permute-done((bf16[32,4096]{1,0:T(8,128)(2,1)S(1)}, bf16[32,4096]{1,0:T(8,128)(2,1)S(1)}, u32[]{:S(2)}, u32[]{:S(2)}) %collective-permute-start.22) | collective-permute-done | bytes 262176 | tf_op jit(solution)/shard_map/ppermute | solution.py:36
  (41 shorter events, 7.5 us)
Async XLA Ops:
  1.8 12.5 %collective-permute-start = (bf16[256,512]{1,0:T(8,128)(2,1)S(1)}, bf16[256,512]{1,0:T(8,128)(2,1)S(1)}, u32[]{:S(2)}, u32[]{:S(2)}) collective-permute-start(bf16[256,512]{1,0:T(8,128)(2,1)S(1)} %pack.2.refs_5_), channel_id=1, source_target_pairs={{0,32},{32,64},{64,96},{96,128},{128,160},{160,192},{192,224},{224... | collective-permute-start | bytes 786440 | tf_op jit(solution)/shard_map/ppermute | solution.py:26
  4.4 10.0 %collective-permute-start.1 = (bf16[256,512]{1,0:T(8,128)(2,1)S(1)}, bf16[256,512]{1,0:T(8,128)(2,1)S(1)}, u32[]{:S(2)}, u32[]{:S(2)}) collective-permute-start(bf16[256,512]{1,0:T(8,128)(2,1)S(1)} %pack.2.refs_5_), channel_id=1, source_target_pairs={{0,224},{32,0},{64,32},{96,64},{128,96},{160,128},{192,160},{224,1... | collective-permute-start | bytes 786440 | tf_op jit(solution)/shard_map/ppermute | solution.py:26
  8.4 4.3 %collective-permute-start.2 = (bf16[128,512]{1,0:T(8,128)(2,1)}, bf16[128,512]{1,0:T(8,128)(2,1)S(1)}, u32[]{:S(2)}, u32[]{:S(2)}) collective-permute-start(bf16[128,512]{1,0:T(8,128)(2,1)} %k.3), channel_id=1, source_target_pairs={{0,4},{4,0},{1,5},{5,1},{2,6},{6,2},{3,7},{7,3},{8,12},{12,8},{9,1... | collective-permute-start | bytes 393224 | tf_op jit(solution)/shard_map/ppermute | solution.py:36
  14.3 6.6 %collective-permute-start.10 = (bf16[256,512]{1,0:T(8,128)(2,1)S(1)}, bf16[256,512]{1,0:T(8,128)(2,1)S(1)}, u32[]{:S(2)}, u32[]{:S(2)}) collective-permute-start(bf16[256,512]{1,0:T(8,128)(2,1)S(1)} %collective-permute-done.1.refs_7_), channel_id=1, source_target_pairs={{0,224},{32,0},{64,32},{96,64},{128,96},{160,128},{192,160},{224,1... | collective-permute-start | bytes 786440 | tf_op jit(solution)/shard_map/ppermute | solution.py:26
  16.8 7.5 %collective-permute-start.7 = (bf16[256,512]{1,0:T(8,128)(2,1)S(1)}, bf16[256,512]{1,0:T(8,128)(2,1)S(1)}, u32[]{:S(2)}, u32[]{:S(2)}) collective-permute-start(bf16[256,512]{1,0:T(8,128)(2,1)S(1)} %collective-permute-done.refs_6_), channel_id=1, source_target_pairs={{0,32},{32,64},{64,96},{96,128},{128,160},{160,192},{192,224},{224... | collective-permute-start | bytes 786440 | tf_op jit(solution)/shard_map/ppermute | solution.py:26
  16.8 7.5 %collective-permute-start.3 = (bf16[256,512]{1,0:T(8,128)(2,1)S(1)}, bf16[256,512]{1,0:T(8,128)(2,1)S(1)}, u32[]{:S(2)}, u32[]{:S(2)}) collective-permute-start(bf16[256,512]{1,0:T(8,128)(2,1)S(1)} %pack.3.refs_0_), channel_id=1, source_target_pairs={{0,8},{8,16},{16,24},{24,0},{1,9},{9,17},{17,25},{25,1},{2,10},{10... | collective-permute-start | bytes 786440 | tf_op jit(solution)/shard_map/ppermute | solution.py:26
  18.1 7.6 %collective-permute-start.5 = (bf16[256,512]{1,0:T(8,128)(2,1)S(1)}, bf16[256,512]{1,0:T(8,128)(2,1)S(1)}, u32[]{:S(2)}, u32[]{:S(2)}) collective-permute-start(bf16[256,512]{1,0:T(8,128)(2,1)S(1)} %pack.3.refs_0_), channel_id=1, source_target_pairs={{0,24},{8,0},{16,8},{24,16},{1,25},{9,1},{17,9},{25,17},{2,26},{10... | collective-permute-start | bytes 786440 | tf_op jit(solution)/shard_map/ppermute | solution.py:26
  20.9 6.6 %collective-permute-start.11 = (bf16[256,512]{1,0:T(8,128)(2,1)S(1)}, bf16[256,512]{1,0:T(8,128)(2,1)S(1)}, u32[]{:S(2)}, u32[]{:S(2)}) collective-permute-start(bf16[256,512]{1,0:T(8,128)(2,1)S(1)} %collective-permute-done.10.refs_9_), channel_id=1, source_target_pairs={{0,224},{32,0},{64,32},{96,64},{128,96},{160,128},{192,160},{224,1... | collective-permute-start | bytes 786440 | tf_op jit(solution)/shard_map/ppermute | solution.py:26
  24.3 6.5 %collective-permute-start.8 = (bf16[256,512]{1,0:T(8,128)(2,1)S(1)}, bf16[256,512]{1,0:T(8,128)(2,1)S(1)}, u32[]{:S(2)}, u32[]{:S(2)}) collective-permute-start(bf16[256,512]{1,0:T(8,128)(2,1)S(1)} %collective-permute-done.7.refs_8_), channel_id=1, source_target_pairs={{0,32},{32,64},{64,96},{96,128},{128,160},{160,192},{192,224},{224... | collective-permute-start | bytes 786440 | tf_op jit(solution)/shard_map/ppermute | solution.py:26
  24.3 6.8 %collective-permute-start.4 = (bf16[128,512]{1,0:T(8,128)(2,1)S(1)}, bf16[128,512]{1,0:T(8,128)(2,1)S(1)}, u32[]{:S(2)}, u32[]{:S(2)}) collective-permute-start(bf16[128,512]{1,0:T(8,128)(2,1)S(1)} %slice.16), channel_id=1, source_target_pairs={{0,8},{8,16},{16,24},{24,0},{1,9},{9,17},{17,25},{25,1},{2,10},{10... | collective-permute-start | bytes 393224 | tf_op jit(solution)/shard_map/ppermute | solution.py:26
  25.7 5.4 %collective-permute-start.6 = (bf16[128,512]{1,0:T(8,128)(2,1)S(1)}, bf16[128,512]{1,0:T(8,128)(2,1)S(1)}, u32[]{:S(2)}, u32[]{:S(2)}) collective-permute-start(bf16[128,512]{1,0:T(8,128)(2,1)S(1)} %slice.17), channel_id=1, source_target_pairs={{0,24},{8,0},{16,8},{24,16},{1,25},{9,1},{17,9},{25,17},{2,26},{10... | collective-permute-start | bytes 393224 | tf_op jit(solution)/shard_map/ppermute | solution.py:26
  27.6 8.8 %collective-permute-start.12 = (bf16[128,512]{1,0:T(8,128)(2,1)S(1)}, bf16[128,512]{1,0:T(8,128)(2,1)S(1)}, u32[]{:S(2)}, u32[]{:S(2)}) collective-permute-start(bf16[128,512]{1,0:T(8,128)(2,1)S(1)} %slice.19), channel_id=1, source_target_pairs={{0,224},{32,0},{64,32},{96,64},{128,96},{160,128},{192,160},{224,1... | collective-permute-start | bytes 393224 | tf_op jit(solution)/shard_map/ppermute | solution.py:26
  30.8 5.6 %collective-permute-start.9 = (bf16[128,512]{1,0:T(8,128)(2,1)S(1)}, bf16[128,512]{1,0:T(8,128)(2,1)S(1)}, u32[]{:S(2)}, u32[]{:S(2)}) collective-permute-start(bf16[128,512]{1,0:T(8,128)(2,1)S(1)} %slice.18), channel_id=1, source_target_pairs={{0,32},{32,64},{64,96},{96,128},{128,160},{160,192},{192,224},{224... | collective-permute-start | bytes 393224 | tf_op jit(solution)/shard_map/ppermute | solution.py:26
  31.1 23.1 %copy-start = (bf16[512,4096]{1,0:T(8,128)(2,1)S(1)}, bf16[512,4096]{1,0:T(8,128)(2,1)}, u32[]{:S(2)}) copy-start(bf16[512,4096]{1,0:T(8,128)(2,1)} %refs_8_.1) | copy-start | bytes 12582916
  37.8 10.3 %collective-permute-start.13 = (bf16[528,128]{1,0:T(8,128)(2,1)S(1)}, bf16[528,128]{1,0:T(8,128)(2,1)S(1)}, u32[]{:S(2)}, u32[]{:S(2)}) collective-permute-start(bf16[528,128]{1,0:T(8,128)(2,1)S(1)} %get-tuple-element.27), channel_id=1, source_target_pairs={{0,16},{4,20},{8,24},{12,28},{16,0},{20,4},{24,8},{28,12},{1,17},{... | collective-permute-start | bytes 405512 | tf_op jit(solution)/shard_map/ppermute | solution.py:32
  40.8 7.3 %collective-permute-start.14 = (bf16[528,128]{1,0:T(8,128)(2,1)S(1)}, bf16[528,128]{1,0:T(8,128)(2,1)S(1)}, u32[]{:S(2)}, u32[]{:S(2)}) collective-permute-start(bf16[528,128]{1,0:T(8,128)(2,1)S(1)} %get-tuple-element.28), channel_id=1, source_target_pairs={{0,20},{4,16},{8,28},{12,24},{16,4},{20,0},{24,12},{28,8},{1,21},{... | collective-permute-start | bytes 405512 | tf_op jit(solution)/shard_map/ppermute | solution.py:32
  41.9 6.6 %collective-permute-start.15 = (bf16[528,128]{1,0:T(8,128)(2,1)S(1)}, bf16[528,128]{1,0:T(8,128)(2,1)S(1)}, u32[]{:S(2)}, u32[]{:S(2)}) collective-permute-start(bf16[528,128]{1,0:T(8,128)(2,1)S(1)} %get-tuple-element.29), channel_id=1, source_target_pairs={{0,28},{4,24},{8,4},{12,0},{16,12},{20,8},{24,20},{28,16},{1,29},{... | collective-permute-start | bytes 405512 | tf_op jit(solution)/shard_map/ppermute | solution.py:32
  44.5 6.0 %collective-permute-start.16 = (bf16[528,128]{1,0:T(8,128)(2,1)S(1)}, bf16[528,128]{1,0:T(8,128)(2,1)S(1)}, u32[]{:S(2)}, u32[]{:S(2)}) collective-permute-start(bf16[528,128]{1,0:T(8,128)(2,1)S(1)} %get-tuple-element.30), channel_id=1, source_target_pairs={{0,12},{4,8},{8,20},{12,16},{16,28},{20,24},{24,4},{28,0},{1,13},{... | collective-permute-start | bytes 405512 | tf_op jit(solution)/shard_map/ppermute | solution.py:32
  44.5 7.4 %collective-permute-start.17 = (bf16[528,128]{1,0:T(8,128)(2,1)S(1)}, bf16[528,128]{1,0:T(8,128)(2,1)S(1)}, u32[]{:S(2)}, u32[]{:S(2)}) collective-permute-start(bf16[528,128]{1,0:T(8,128)(2,1)S(1)} %get-tuple-element.31), channel_id=1, source_target_pairs={{0,24},{4,28},{8,0},{12,4},{16,8},{20,12},{24,16},{28,20},{1,25},{... | collective-permute-start | bytes 405512 | tf_op jit(solution)/shard_map/ppermute | solution.py:32
  48.1 6.1 %collective-permute-start.18 = (bf16[528,128]{1,0:T(8,128)(2,1)S(1)}, bf16[528,128]{1,0:T(8,128)(2,1)S(1)}, u32[]{:S(2)}, u32[]{:S(2)}) collective-permute-start(bf16[528,128]{1,0:T(8,128)(2,1)S(1)} %get-tuple-element.32), channel_id=1, source_target_pairs={{0,8},{4,12},{8,16},{12,20},{16,24},{20,28},{24,0},{28,4},{1,9},{5... | collective-permute-start | bytes 405512 | tf_op jit(solution)/shard_map/ppermute | solution.py:32
  48.1 6.1 %collective-permute-start.19 = (bf16[528,128]{1,0:T(8,128)(2,1)S(1)}, bf16[528,128]{1,0:T(8,128)(2,1)S(1)}, u32[]{:S(2)}, u32[]{:S(2)}) collective-permute-start(bf16[528,128]{1,0:T(8,128)(2,1)S(1)} %get-tuple-element.33), channel_id=1, source_target_pairs={{0,4},{4,0},{8,12},{12,8},{16,20},{20,16},{24,28},{28,24},{1,5},{5... | collective-permute-start | bytes 405512 | tf_op jit(solution)/shard_map/ppermute | solution.py:32
  55.2 7.5 %collective-permute-start.21 = (bf16[32,4096]{1,0:T(8,128)(2,1)S(1)}, bf16[32,4096]{1,0:T(8,128)(2,1)S(1)}, u32[]{:S(2)}, u32[]{:S(2)}) collective-permute-start(bf16[32,4096]{1,0:T(8,128)(2,1)S(1)} %get-tuple-element.38), channel_id=1, source_target_pairs={{0,1},{1,0},{2,3},{3,2},{4,5},{5,4},{6,7},{7,6},{8,9},{9,8},{10,11... | collective-permute-start | bytes 786440 | tf_op jit(solution)/shard_map/ppermute | solution.py:36
  61.6 3.8 %collective-permute-start.20 = (bf16[32,4096]{1,0:T(8,128)(2,1)S(1)}, bf16[32,4096]{1,0:T(8,128)(2,1)S(1)}, u32[]{:S(2)}, u32[]{:S(2)}) collective-permute-start(bf16[32,4096]{1,0:T(8,128)(2,1)S(1)} %get-tuple-element.36), channel_id=1, source_target_pairs={{0,1},{1,0},{2,3},{3,2},{4,5},{5,4},{6,7},{7,6},{8,9},{9,8},{10,11... | collective-permute-start | bytes 786440 | tf_op jit(solution)/shard_map/ppermute | solution.py:36
  62.8 9.1 %collective-permute-start.22 = (bf16[32,4096]{1,0:T(8,128)(2,1)S(1)}, bf16[32,4096]{1,0:T(8,128)(2,1)S(1)}, u32[]{:S(2)}, u32[]{:S(2)}) collective-permute-start(bf16[32,4096]{1,0:T(8,128)(2,1)S(1)} %add_convert_fusion), channel_id=1, source_target_pairs={{0,2},{2,0},{1,3},{3,1},{4,6},{6,4},{5,7},{7,5},{8,10},{10,8},{9,1... | collective-permute-start | bytes 786440 | tf_op jit(solution)/shard_map/ppermute | solution.py:36
  (3 other events, 2.7 us)

commit v5 on v4

--- a/solution.py
+++ b/solution.py
@@ -11,7 +11,7 @@
 AXES = {"z": 8, "y": 4, "xl": 2, "xh": 2, "c": 2}
 PLANE = ("y", "xl")
 SLOTS = ((0, 0), (0, 1), (2, 0), (2, 1), (-1, 0), (-1, 1), (1, 0), (1, 1))
-FIRST_OUT = (2, 3, 5, 7, 4, 6, 1)
+FIRST_OUT = (5, 7, 3, 2, 4, 6, 1)
 SPAN = 4
 LOG2E = 1.4426950408889634
 TOK = 128

time: 72.9 us -> 72.9 us (level)
  waiting for transfers between devices: 18.9 us -> 22.3 us
  starting transfers between devices: 42.3 us -> 38.9 us
    ppermute x7, waiting for transfers between devices: 5.7 us -> 9.1 us  [to_slot(): return lax.ppermute(x, PLANE, pairs)]
    ppermute x4, starting transfers between devices: 10.2 us -> 7.08 us  [flip(): return lax.ppermute(x, axis, [(0, 1), (1, 0)])]
  transfers between devices with their start and end apart: 23 -> 23, of which waited for: 9 -> 11; matrix products, arithmetic and copies ran while one was open for 0% -> 0% of each run, Pallas kernels for 7% -> 7%
where the time goes in v5:
time: 72.9 us; the launch traced here: 72.8 us
  starting transfers between devices  38.9 us (53%)
  waiting for transfers between devices  22.3 us (31%)
  Pallas kernels  7.7 us (11%)
  local copies, waits for them, and re-layouts  2.76 us (4%)
  other arithmetic  0.93 us (1%)
    ppermute x12, starting transfers between devices, shift(): return lax.ppermute(x, axis, [(i, (i + by) % n) for i in range(n)])  21.5 us
    ppermute x4, waiting for transfers between devices, flip(): return lax.ppermute(x, axis, [(0, 1), (1, 0)])  10.7 us
    ppermute x7, starting transfers between devices, to_slot(): return lax.ppermute(x, PLANE, pairs)  10.4 us
    ppermute x7, waiting for transfers between devices, to_slot(): return lax.ppermute(x, PLANE, pairs)  9.1 us
    ppermute x4, starting transfers between devices, flip(): return lax.ppermute(x, axis, [(0, 1), (1, 0)])  7.08 us
    pallas_call x2, Pallas kernels, attend(): pl.pallas_call(functools.partial(attend_kernel, len(blocks), last), grid=...  6.69 us
    unnamed x8, local copies, waits for them, and re-layouts  2.72 us
    ppermute x12, waiting for transfers between devices, shift(): return lax.ppermute(x, axis, [(i, (i + by) % n) for i in range(n)])  2.46 us
  transfers between devices with their start and end apart: 23, of which 11 were waited for; matrix products, arithmetic and copies ran while one was open for 0% of the time, Pallas kernels for 7%

profile of v5, /device:TPU:1, one launch (start us, length us, event | category | flops | bytes accessed | tf_op | source)
XLA Modules:
  0.0 72.8 jit_solution(3563889441606937715)
XLA Ops:
  1.8 2.5 %collective-permute-start = (bf16[256,512]{1,0:T(8,128)(2,1)S(1)}, bf16[256,512]{1,0:T(8,128)(2,1)S(1)}, u32[]{:S(2)}, u32[]{:S(2)}) collective-permute-start(bf16[256,512]{1,0:T(8,128)(2,1)S(1)} %pack.2.refs_5_), channel_id=1, source_target_pairs={{0,32},{32,64},{64,96},{96,128},{128,160},{160,192},{192,224},{224... | collective-permute-start | bytes 786440 | tf_op jit(solution)/shard_map/ppermute | solution.py:26
  4.4 4.0 %collective-permute-start.1 = (bf16[256,512]{1,0:T(8,128)(2,1)S(1)}, bf16[256,512]{1,0:T(8,128)(2,1)S(1)}, u32[]{:S(2)}, u32[]{:S(2)}) collective-permute-start(bf16[256,512]{1,0:T(8,128)(2,1)S(1)} %pack.2.refs_5_), channel_id=1, source_target_pairs={{0,224},{32,0},{64,32},{96,64},{128,96},{160,128},{192,160},{224,1... | collective-permute-start | bytes 786440 | tf_op jit(solution)/shard_map/ppermute | solution.py:26
  8.4 1.2 %collective-permute-start.2 = (bf16[128,512]{1,0:T(8,128)(2,1)}, bf16[128,512]{1,0:T(8,128)(2,1)S(1)}, u32[]{:S(2)}, u32[]{:S(2)}) collective-permute-start(bf16[128,512]{1,0:T(8,128)(2,1)} %k.3), channel_id=1, source_target_pairs={{0,4},{4,0},{1,5},{5,1},{2,6},{6,2},{3,7},{7,3},{8,12},{12,8},{9,1... | collective-permute-start | bytes 393224 | tf_op jit(solution)/shard_map/ppermute | solution.py:36
  9.6 3.1 %collective-permute-done.2.v = bf16[128,512]{1,0:T(8,128)(2,1)S(1)} collective-permute-done((bf16[128,512]{1,0:T(8,128)(2,1)}, bf16[128,512]{1,0:T(8,128)(2,1)S(1)}, u32[]{:S(2)}, u32[]{:S(2)}) %collective-permute-start.2) | collective-permute-done | bytes 131104 | tf_op jit(solution)/shard_map/ppermute | solution.py:36
  14.3 2.4 %collective-permute-start.10 = (bf16[256,512]{1,0:T(8,128)(2,1)S(1)}, bf16[256,512]{1,0:T(8,128)(2,1)S(1)}, u32[]{:S(2)}, u32[]{:S(2)}) collective-permute-start(bf16[256,512]{1,0:T(8,128)(2,1)S(1)} %collective-permute-done.1.refs_7_), channel_id=1, source_target_pairs={{0,224},{32,0},{64,32},{96,64},{128,96},{160,128},{192,160},{224,1... | collective-permute-start | bytes 786440 | tf_op jit(solution)/shard_map/ppermute | solution.py:26
  16.8 1.3 %collective-permute-start.3 = (bf16[256,512]{1,0:T(8,128)(2,1)S(1)}, bf16[256,512]{1,0:T(8,128)(2,1)S(1)}, u32[]{:S(2)}, u32[]{:S(2)}) collective-permute-start(bf16[256,512]{1,0:T(8,128)(2,1)S(1)} %pack.3.refs_0_), channel_id=1, source_target_pairs={{0,8},{8,16},{16,24},{24,0},{1,9},{9,17},{17,25},{25,1},{2,10},{10... | collective-permute-start | bytes 786440 | tf_op jit(solution)/shard_map/ppermute | solution.py:26
  18.1 1.4 %collective-permute-start.5 = (bf16[256,512]{1,0:T(8,128)(2,1)S(1)}, bf16[256,512]{1,0:T(8,128)(2,1)S(1)}, u32[]{:S(2)}, u32[]{:S(2)}) collective-permute-start(bf16[256,512]{1,0:T(8,128)(2,1)S(1)} %pack.3.refs_0_), channel_id=1, source_target_pairs={{0,24},{8,0},{16,8},{24,16},{1,25},{9,1},{17,9},{25,17},{2,26},{10... | collective-permute-start | bytes 786440 | tf_op jit(solution)/shard_map/ppermute | solution.py:26
  19.5 1.4 %collective-permute-done.10.refs_9_ = bf16[256,512]{1,0:T(8,128)(2,1)S(1)} collective-permute-done((bf16[256,512]{1,0:T(8,128)(2,1)S(1)}, bf16[256,512]{1,0:T(8,128)(2,1)S(1)}, u32[]{:S(2)}, u32[]{:S(2)}) %collective-permute-start.10) | collective-permute-done | bytes 262176 | tf_op jit(solution)/shard_map/ppermute | solution.py:26
  20.9 3.3 %collective-permute-start.11 = (bf16[256,512]{1,0:T(8,128)(2,1)S(1)}, bf16[256,512]{1,0:T(8,128)(2,1)S(1)}, u32[]{:S(2)}, u32[]{:S(2)}) collective-permute-start(bf16[256,512]{1,0:T(8,128)(2,1)S(1)} %collective-permute-done.10.refs_9_), channel_id=1, source_target_pairs={{0,224},{32,0},{64,32},{96,64},{128,96},{160,128},{192,160},{224,1... | collective-permute-start | bytes 786440 | tf_op jit(solution)/shard_map/ppermute | solution.py:26
  24.3 1.4 %collective-permute-start.4 = (bf16[128,512]{1,0:T(8,128)(2,1)S(1)}, bf16[128,512]{1,0:T(8,128)(2,1)S(1)}, u32[]{:S(2)}, u32[]{:S(2)}) collective-permute-start(bf16[128,512]{1,0:T(8,128)(2,1)S(1)} %slice.16), channel_id=1, source_target_pairs={{0,8},{8,16},{16,24},{24,0},{1,9},{9,17},{17,25},{25,1},{2,10},{10... | collective-permute-start | bytes 393224 | tf_op jit(solution)/shard_map/ppermute | solution.py:26
  25.7 1.5 %collective-permute-start.6 = (bf16[128,512]{1,0:T(8,128)(2,1)S(1)}, bf16[128,512]{1,0:T(8,128)(2,1)S(1)}, u32[]{:S(2)}, u32[]{:S(2)}) collective-permute-start(bf16[128,512]{1,0:T(8,128)(2,1)S(1)} %slice.17), channel_id=1, source_target_pairs={{0,24},{8,0},{16,8},{24,16},{1,25},{9,1},{17,9},{25,17},{2,26},{10... | collective-permute-start | bytes 393224 | tf_op jit(solution)/shard_map/ppermute | solution.py:26
  27.6 3.2 %collective-permute-start.12 = (bf16[128,512]{1,0:T(8,128)(2,1)S(1)}, bf16[128,512]{1,0:T(8,128)(2,1)S(1)}, u32[]{:S(2)}, u32[]{:S(2)}) collective-permute-start(bf16[128,512]{1,0:T(8,128)(2,1)S(1)} %slice.19), channel_id=1, source_target_pairs={{0,224},{32,0},{64,32},{96,64},{128,96},{160,128},{192,160},{224,1... | collective-permute-start | bytes 393224 | tf_op jit(solution)/shard_map/ppermute | solution.py:26
  31.1 5.3 %attend.2 = (f32[512,1024]{1,0:T(8,128)S(1)}, f32[4,2,1024]{2,1,0:T(2,128)S(1)}) custom-call(bf16[256,512]{1,0:T(8,128)(2,1)S(1)} %pack.3.refs_0_, bf16[128,512]{1,0:T(8,128)(2,1)S(1)} %collective-permute-done.4.refs_1_, bf16[128,512]{1,0:T(8,128)(2,1)S(1)} %collective-permute-done.6.refs_2_, bf16[256,512]{1,0:T(8,128)(2,1)S(1)} %collective-permute-done.3.refs_3_, ...), custom_call_target="tpu_custom_call" | custom-call | flops 5637144576 | bytes 4194304 | tf_op jit(solution)/shard_map/attend/pallas_call | solution.py:145
  36.4 1.4 %attend.3 = (bf16[528,128]{1,0:T(8,128)(2,1)S(1)}, bf16[528,128]{1,0:T(8,128)(2,1)S(1)}, bf16[528,128]{1,0:T(8,128)(2,1)S(1)}, bf16[528,128]{1,0:T(8,128)(2,1)S(...) custom-call(bf16[256,512]{1,0:T(8,128)(2,1)S(1)} %pack.3.refs_0_, ...), custom_call_target="tpu_custom_call" | custom-call | flops 805306368 | bytes 4194304 | tf_op jit(solution)/shard_map/attend/pallas_call | solution.py:145
  37.8 3.7 %collective-permute-start.13 = (bf16[528,128]{1,0:T(8,128)(2,1)S(1)}, bf16[528,128]{1,0:T(8,128)(2,1)S(1)}, u32[]{:S(2)}, u32[]{:S(2)}) collective-permute-start(bf16[528,128]{1,0:T(8,128)(2,1)S(1)} %get-tuple-element.27), channel_id=1, source_target_pairs={{0,28},{4,24},{8,4},{12,0},{16,12},{20,8},{24,20},{28,16},{1,29},{... | collective-permute-start | bytes 405512 | tf_op jit(solution)/shard_map/ppermute | solution.py:32
  41.6 2.5 %collective-permute-start.15 = (bf16[528,128]{1,0:T(8,128)(2,1)S(1)}, bf16[528,128]{1,0:T(8,128)(2,1)S(1)}, u32[]{:S(2)}, u32[]{:S(2)}) collective-permute-start(bf16[528,128]{1,0:T(8,128)(2,1)S(1)} %get-tuple-element.29), channel_id=1, source_target_pairs={{0,20},{4,16},{8,28},{12,24},{16,4},{20,0},{24,12},{28,8},{1,21},{... | collective-permute-start | bytes 405512 | tf_op jit(solution)/shard_map/ppermute | solution.py:32
  44.5 3.6 %collective-permute-start.17 = (bf16[528,128]{1,0:T(8,128)(2,1)S(1)}, bf16[528,128]{1,0:T(8,128)(2,1)S(1)}, u32[]{:S(2)}, u32[]{:S(2)}) collective-permute-start(bf16[528,128]{1,0:T(8,128)(2,1)S(1)} %get-tuple-element.31), channel_id=1, source_target_pairs={{0,24},{4,28},{8,0},{12,4},{16,8},{20,12},{24,16},{28,20},{1,25},{... | collective-permute-start | bytes 405512 | tf_op jit(solution)/shard_map/ppermute | solution.py:32
  49.0 1.4 %collective-permute-done.16.refs_3_ = bf16[528,128]{1,0:T(8,128)(2,1)S(1)} collective-permute-done((bf16[528,128]{1,0:T(8,128)(2,1)S(1)}, bf16[528,128]{1,0:T(8,128)(2,1)S(1)}, u32[]{:S(2)}, u32[]{:S(2)}) %collective-permute-start.16) | collective-permute-done | bytes 135200 | tf_op jit(solution)/shard_map/ppermute | solution.py:32
  50.4 5.0 %collective-permute-done.17.refs_4_ = bf16[528,128]{1,0:T(8,128)(2,1)S(1)} collective-permute-done((bf16[528,128]{1,0:T(8,128)(2,1)S(1)}, bf16[528,128]{1,0:T(8,128)(2,1)S(1)}, u32[]{:S(2)}, u32[]{:S(2)}) %collective-permute-start.17) | collective-permute-done | bytes 135200 | tf_op jit(solution)/shard_map/ppermute | solution.py:32
  55.4 1.9 %collective-permute-done.18.refs_5_ = bf16[528,128]{1,0:T(8,128)(2,1)S(1)} collective-permute-done((bf16[528,128]{1,0:T(8,128)(2,1)S(1)}, bf16[528,128]{1,0:T(8,128)(2,1)S(1)}, u32[]{:S(2)}, u32[]{:S(2)}) %collective-permute-start.18) | collective-permute-done | bytes 135200 | tf_op jit(solution)/shard_map/ppermute | solution.py:32
  58.3 3.2 %collective-permute-start.21 = (bf16[32,4096]{1,0:T(8,128)(2,1)S(1)}, bf16[32,4096]{1,0:T(8,128)(2,1)S(1)}, u32[]{:S(2)}, u32[]{:S(2)}) collective-permute-start(bf16[32,4096]{1,0:T(8,128)(2,1)S(1)} %get-tuple-element.38), channel_id=1, source_target_pairs={{0,1},{1,0},{2,3},{3,2},{4,5},{5,4},{6,7},{7,6},{8,9},{9,8},{10,11... | collective-permute-start | bytes 786440 | tf_op jit(solution)/shard_map/ppermute | solution.py:36
  61.6 1.1 %collective-permute-done.21 = bf16[32,4096]{1,0:T(8,128)(2,1)S(1)} collective-permute-done((bf16[32,4096]{1,0:T(8,128)(2,1)S(1)}, bf16[32,4096]{1,0:T(8,128)(2,1)S(1)}, u32[]{:S(2)}, u32[]{:S(2)}) %collective-permute-start.21) | collective-permute-done | bytes 262176 | tf_op jit(solution)/shard_map/ppermute | solution.py:36
  62.8 2.5 %collective-permute-start.22 = (bf16[32,4096]{1,0:T(8,128)(2,1)S(1)}, bf16[32,4096]{1,0:T(8,128)(2,1)S(1)}, u32[]{:S(2)}, u32[]{:S(2)}) collective-permute-start(bf16[32,4096]{1,0:T(8,128)(2,1)S(1)} %add_convert_fusion), channel_id=1, source_target_pairs={{0,2},{2,0},{1,3},{3,1},{4,6},{6,4},{5,7},{7,5},{8,10},{10,8},{9,1... | collective-permute-start | bytes 786440 | tf_op jit(solution)/shard_map/ppermute | solution.py:36
  65.3 6.6 %collective-permute-done.22 = bf16[32,4096]{1,0:T(8,128)(2,1)S(1)} collective-permute-done((bf16[32,4096]{1,0:T(8,128)(2,1)S(1)}, bf16[32,4096]{1,0:T(8,128)(2,1)S(1)}, u32[]{:S(2)}, u32[]{:S(2)}) %collective-permute-start.22) | collective-permute-done | bytes 262176 | tf_op jit(solution)/shard_map/ppermute | solution.py:36
  (41 shorter events, 7.5 us)
Async XLA Ops:
  1.8 12.5 %collective-permute-start = (bf16[256,512]{1,0:T(8,128)(2,1)S(1)}, bf16[256,512]{1,0:T(8,128)(2,1)S(1)}, u32[]{:S(2)}, u32[]{:S(2)}) collective-permute-start(bf16[256,512]{1,0:T(8,128)(2,1)S(1)} %pack.2.refs_5_), channel_id=1, source_target_pairs={{0,32},{32,64},{64,96},{96,128},{128,160},{160,192},{192,224},{224... | collective-permute-start | bytes 786440 | tf_op jit(solution)/shard_map/ppermute | solution.py:26
  4.4 10.0 %collective-permute-start.1 = (bf16[256,512]{1,0:T(8,128)(2,1)S(1)}, bf16[256,512]{1,0:T(8,128)(2,1)S(1)}, u32[]{:S(2)}, u32[]{:S(2)}) collective-permute-start(bf16[256,512]{1,0:T(8,128)(2,1)S(1)} %pack.2.refs_5_), channel_id=1, source_target_pairs={{0,224},{32,0},{64,32},{96,64},{128,96},{160,128},{192,160},{224,1... | collective-permute-start | bytes 786440 | tf_op jit(solution)/shard_map/ppermute | solution.py:26
  8.4 4.3 %collective-permute-start.2 = (bf16[128,512]{1,0:T(8,128)(2,1)}, bf16[128,512]{1,0:T(8,128)(2,1)S(1)}, u32[]{:S(2)}, u32[]{:S(2)}) collective-permute-start(bf16[128,512]{1,0:T(8,128)(2,1)} %k.3), channel_id=1, source_target_pairs={{0,4},{4,0},{1,5},{5,1},{2,6},{6,2},{3,7},{7,3},{8,12},{12,8},{9,1... | collective-permute-start | bytes 393224 | tf_op jit(solution)/shard_map/ppermute | solution.py:36
  14.3 6.6 %collective-permute-start.10 = (bf16[256,512]{1,0:T(8,128)(2,1)S(1)}, bf16[256,512]{1,0:T(8,128)(2,1)S(1)}, u32[]{:S(2)}, u32[]{:S(2)}) collective-permute-start(bf16[256,512]{1,0:T(8,128)(2,1)S(1)} %collective-permute-done.1.refs_7_), channel_id=1, source_target_pairs={{0,224},{32,0},{64,32},{96,64},{128,96},{160,128},{192,160},{224,1... | collective-permute-start | bytes 786440 | tf_op jit(solution)/shard_map/ppermute | solution.py:26
  16.8 7.5 %collective-permute-start.7 = (bf16[256,512]{1,0:T(8,128)(2,1)S(1)}, bf16[256,512]{1,0:T(8,128)(2,1)S(1)}, u32[]{:S(2)}, u32[]{:S(2)}) collective-permute-start(bf16[256,512]{1,0:T(8,128)(2,1)S(1)} %collective-permute-done.refs_6_), channel_id=1, source_target_pairs={{0,32},{32,64},{64,96},{96,128},{128,160},{160,192},{192,224},{224... | collective-permute-start | bytes 786440 | tf_op jit(solution)/shard_map/ppermute | solution.py:26
  16.8 7.5 %collective-permute-start.3 = (bf16[256,512]{1,0:T(8,128)(2,1)S(1)}, bf16[256,512]{1,0:T(8,128)(2,1)S(1)}, u32[]{:S(2)}, u32[]{:S(2)}) collective-permute-start(bf16[256,512]{1,0:T(8,128)(2,1)S(1)} %pack.3.refs_0_), channel_id=1, source_target_pairs={{0,8},{8,16},{16,24},{24,0},{1,9},{9,17},{17,25},{25,1},{2,10},{10... | collective-permute-start | bytes 786440 | tf_op jit(solution)/shard_map/ppermute | solution.py:26
  18.1 7.6 %collective-permute-start.5 = (bf16[256,512]{1,0:T(8,128)(2,1)S(1)}, bf16[256,512]{1,0:T(8,128)(2,1)S(1)}, u32[]{:S(2)}, u32[]{:S(2)}) collective-permute-start(bf16[256,512]{1,0:T(8,128)(2,1)S(1)} %pack.3.refs_0_), channel_id=1, source_target_pairs={{0,24},{8,0},{16,8},{24,16},{1,25},{9,1},{17,9},{25,17},{2,26},{10... | collective-permute-start | bytes 786440 | tf_op jit(solution)/shard_map/ppermute | solution.py:26
  20.9 6.6 %collective-permute-start.11 = (bf16[256,512]{1,0:T(8,128)(2,1)S(1)}, bf16[256,512]{1,0:T(8,128)(2,1)S(1)}, u32[]{:S(2)}, u32[]{:S(2)}) collective-permute-start(bf16[256,512]{1,0:T(8,128)(2,1)S(1)} %collective-permute-done.10.refs_9_), channel_id=1, source_target_pairs={{0,224},{32,0},{64,32},{96,64},{128,96},{160,128},{192,160},{224,1... | collective-permute-start | bytes 786440 | tf_op jit(solution)/shard_map/ppermute | solution.py:26
  24.3 6.5 %collective-permute-start.8 = (bf16[256,512]{1,0:T(8,128)(2,1)S(1)}, bf16[256,512]{1,0:T(8,128)(2,1)S(1)}, u32[]{:S(2)}, u32[]{:S(2)}) collective-permute-start(bf16[256,512]{1,0:T(8,128)(2,1)S(1)} %collective-permute-done.7.refs_8_), channel_id=1, source_target_pairs={{0,32},{32,64},{64,96},{96,128},{128,160},{160,192},{192,224},{224... | collective-permute-start | bytes 786440 | tf_op jit(solution)/shard_map/ppermute | solution.py:26
  24.3 6.8 %collective-permute-start.4 = (bf16[128,512]{1,0:T(8,128)(2,1)S(1)}, bf16[128,512]{1,0:T(8,128)(2,1)S(1)}, u32[]{:S(2)}, u32[]{:S(2)}) collective-permute-start(bf16[128,512]{1,0:T(8,128)(2,1)S(1)} %slice.16), channel_id=1, source_target_pairs={{0,8},{8,16},{16,24},{24,0},{1,9},{9,17},{17,25},{25,1},{2,10},{10... | collective-permute-start | bytes 393224 | tf_op jit(solution)/shard_map/ppermute | solution.py:26
  25.7 5.4 %collective-permute-start.6 = (bf16[128,512]{1,0:T(8,128)(2,1)S(1)}, bf16[128,512]{1,0:T(8,128)(2,1)S(1)}, u32[]{:S(2)}, u32[]{:S(2)}) collective-permute-start(bf16[128,512]{1,0:T(8,128)(2,1)S(1)} %slice.17), channel_id=1, source_target_pairs={{0,24},{8,0},{16,8},{24,16},{1,25},{9,1},{17,9},{25,17},{2,26},{10... | collective-permute-start | bytes 393224 | tf_op jit(solution)/shard_map/ppermute | solution.py:26
  27.6 8.8 %collective-permute-start.12 = (bf16[128,512]{1,0:T(8,128)(2,1)S(1)}, bf16[128,512]{1,0:T(8,128)(2,1)S(1)}, u32[]{:S(2)}, u32[]{:S(2)}) collective-permute-start(bf16[128,512]{1,0:T(8,128)(2,1)S(1)} %slice.19), channel_id=1, source_target_pairs={{0,224},{32,0},{64,32},{96,64},{128,96},{160,128},{192,160},{224,1... | collective-permute-start | bytes 393224 | tf_op jit(solution)/shard_map/ppermute | solution.py:26
  30.8 5.6 %collective-permute-start.9 = (bf16[128,512]{1,0:T(8,128)(2,1)S(1)}, bf16[128,512]{1,0:T(8,128)(2,1)S(1)}, u32[]{:S(2)}, u32[]{:S(2)}) collective-permute-start(bf16[128,512]{1,0:T(8,128)(2,1)S(1)} %slice.18), channel_id=1, source_target_pairs={{0,32},{32,64},{64,96},{96,128},{128,160},{160,192},{192,224},{224... | collective-permute-start | bytes 393224 | tf_op jit(solution)/shard_map/ppermute | solution.py:26
  31.1 26.3 %copy-start = (bf16[512,4096]{1,0:T(8,128)(2,1)S(1)}, bf16[512,4096]{1,0:T(8,128)(2,1)}, u32[]{:S(2)}) copy-start(bf16[512,4096]{1,0:T(8,128)(2,1)} %refs_8_.1) | copy-start | bytes 12582916
  37.8 10.3 %collective-permute-start.13 = (bf16[528,128]{1,0:T(8,128)(2,1)S(1)}, bf16[528,128]{1,0:T(8,128)(2,1)S(1)}, u32[]{:S(2)}, u32[]{:S(2)}) collective-permute-start(bf16[528,128]{1,0:T(8,128)(2,1)S(1)} %get-tuple-element.27), channel_id=1, source_target_pairs={{0,28},{4,24},{8,4},{12,0},{16,12},{20,8},{24,20},{28,16},{1,29},{... | collective-permute-start | bytes 405512 | tf_op jit(solution)/shard_map/ppermute | solution.py:32
  41.6 7.0 %collective-permute-start.14 = (bf16[528,128]{1,0:T(8,128)(2,1)S(1)}, bf16[528,128]{1,0:T(8,128)(2,1)S(1)}, u32[]{:S(2)}, u32[]{:S(2)}) collective-permute-start(bf16[528,128]{1,0:T(8,128)(2,1)S(1)} %get-tuple-element.28), channel_id=1, source_target_pairs={{0,12},{4,8},{8,20},{12,16},{16,28},{20,24},{24,4},{28,0},{1,13},{... | collective-permute-start | bytes 405512 | tf_op jit(solution)/shard_map/ppermute | solution.py:32
  41.6 7.4 %collective-permute-start.15 = (bf16[528,128]{1,0:T(8,128)(2,1)S(1)}, bf16[528,128]{1,0:T(8,128)(2,1)S(1)}, u32[]{:S(2)}, u32[]{:S(2)}) collective-permute-start(bf16[528,128]{1,0:T(8,128)(2,1)S(1)} %get-tuple-element.29), channel_id=1, source_target_pairs={{0,20},{4,16},{8,28},{12,24},{16,4},{20,0},{24,12},{28,8},{1,21},{... | collective-permute-start | bytes 405512 | tf_op jit(solution)/shard_map/ppermute | solution.py:32
  44.1 6.3 %collective-permute-start.16 = (bf16[528,128]{1,0:T(8,128)(2,1)S(1)}, bf16[528,128]{1,0:T(8,128)(2,1)S(1)}, u32[]{:S(2)}, u32[]{:S(2)}) collective-permute-start(bf16[528,128]{1,0:T(8,128)(2,1)S(1)} %get-tuple-element.30), channel_id=1, source_target_pairs={{0,16},{4,20},{8,24},{12,28},{16,0},{20,4},{24,8},{28,12},{1,17},{... | collective-permute-start | bytes 405512 | tf_op jit(solution)/shard_map/ppermute | solution.py:32
  44.5 10.9 %collective-permute-start.17 = (bf16[528,128]{1,0:T(8,128)(2,1)S(1)}, bf16[528,128]{1,0:T(8,128)(2,1)S(1)}, u32[]{:S(2)}, u32[]{:S(2)}) collective-permute-start(bf16[528,128]{1,0:T(8,128)(2,1)S(1)} %get-tuple-element.31), channel_id=1, source_target_pairs={{0,24},{4,28},{8,0},{12,4},{16,8},{20,12},{24,16},{28,20},{1,25},{... | collective-permute-start | bytes 405512 | tf_op jit(solution)/shard_map/ppermute | solution.py:32
  48.1 9.2 %collective-permute-start.18 = (bf16[528,128]{1,0:T(8,128)(2,1)S(1)}, bf16[528,128]{1,0:T(8,128)(2,1)S(1)}, u32[]{:S(2)}, u32[]{:S(2)}) collective-permute-start(bf16[528,128]{1,0:T(8,128)(2,1)S(1)} %get-tuple-element.32), channel_id=1, source_target_pairs={{0,8},{4,12},{8,16},{12,20},{16,24},{20,28},{24,0},{28,4},{1,9},{5... | collective-permute-start | bytes 405512 | tf_op jit(solution)/shard_map/ppermute | solution.py:32
  48.6 8.8 %collective-permute-start.19 = (bf16[528,128]{1,0:T(8,128)(2,1)S(1)}, bf16[528,128]{1,0:T(8,128)(2,1)S(1)}, u32[]{:S(2)}, u32[]{:S(2)}) collective-permute-start(bf16[528,128]{1,0:T(8,128)(2,1)S(1)} %get-tuple-element.33), channel_id=1, source_target_pairs={{0,4},{4,0},{8,12},{12,8},{16,20},{20,16},{24,28},{28,24},{1,5},{5... | collective-permute-start | bytes 405512 | tf_op jit(solution)/shard_map/ppermute | solution.py:32
  58.3 4.4 %collective-permute-start.21 = (bf16[32,4096]{1,0:T(8,128)(2,1)S(1)}, bf16[32,4096]{1,0:T(8,128)(2,1)S(1)}, u32[]{:S(2)}, u32[]{:S(2)}) collective-permute-start(bf16[32,4096]{1,0:T(8,128)(2,1)S(1)} %get-tuple-element.38), channel_id=1, source_target_pairs={{0,1},{1,0},{2,3},{3,2},{4,5},{5,4},{6,7},{7,6},{8,9},{9,8},{10,11... | collective-permute-start | bytes 786440 | tf_op jit(solution)/shard_map/ppermute | solution.py:36
  61.5 3.8 %collective-permute-start.20 = (bf16[32,4096]{1,0:T(8,128)(2,1)S(1)}, bf16[32,4096]{1,0:T(8,128)(2,1)S(1)}, u32[]{:S(2)}, u32[]{:S(2)}) collective-permute-start(bf16[32,4096]{1,0:T(8,128)(2,1)S(1)} %get-tuple-element.36), channel_id=1, source_target_pairs={{0,1},{1,0},{2,3},{3,2},{4,5},{5,4},{6,7},{7,6},{8,9},{9,8},{10,11... | collective-permute-start | bytes 786440 | tf_op jit(solution)/shard_map/ppermute | solution.py:36
  62.8 9.1 %collective-permute-start.22 = (bf16[32,4096]{1,0:T(8,128)(2,1)S(1)}, bf16[32,4096]{1,0:T(8,128)(2,1)S(1)}, u32[]{:S(2)}, u32[]{:S(2)}) collective-permute-start(bf16[32,4096]{1,0:T(8,128)(2,1)S(1)} %add_convert_fusion), channel_id=1, source_target_pairs={{0,2},{2,0},{1,3},{3,1},{4,6},{6,4},{5,7},{7,5},{8,10},{10,8},{9,1... | collective-permute-start | bytes 786440 | tf_op jit(solution)/shard_map/ppermute | solution.py:36
  (3 other events, 2.7 us)
